TPU v7x, 256 devices: a whole 4x4x8 slice. The times are simulated.
256 devices in a mesh: seq: 32 (over z_lo, x, core), samp: 8 (over y, z_hi).
Axes of the slice: x: 4, y: 4, z: 8 (z_hi: 2, z_lo: 4; z = z_hi * 4 + z_lo), core: 2. Of those that a mesh axis runs over, the one named last changes fastest.
Arguments:
- atoms_in: bfloat16 [8, 8192, 128], P('samp', 'seq'), may hold values from -6 to 6
- pair_feats: bfloat16 [256, 16, 32, 128], P('seq'), may hold values from -3 to 3
- window_shift: int32 [256], P('seq'), may hold values from -64 to -32
- atom_token: int32 [8192], P('seq'), may hold values from 0 to 1023, as said below
- token_counts: int32 [1024], P('seq'), may hold values from 1 to 15, as said below
- token_grad: bfloat16 [8, 1024, 384], P('samp', 'seq'), may hold values from -6 to 6
- norm_gain: float32 [2, 128], replicated, may hold values from 0.1 to 1.9
- weight_in: bfloat16 [2, 128, 512], replicated, may hold values from -0.5 to 0.5
- weight_out: bfloat16 [2, 128, 128], replicated, may hold values from -0.5 to 0.5
- weight_bias: float32 [2, 16, 4], replicated, may hold values from -1.5 to 1.5
- weight_token: bfloat16 [128, 384], replicated, may hold values from -0.5 to 0.5
Outputs:
- grad_atoms: bfloat16 [8, 8192, 128], P('samp', 'seq')
- grad_pair: bfloat16 [256, 16, 32, 128], P(('seq', 'samp'))
- grad_gain: float32 [2, 128], replicated
- grad_weight_in: float32 [2, 128, 512], replicated
- grad_weight_out: float32 [2, 128, 128], replicated
- grad_weight_bias: float32 [2, 16, 4], replicated
- grad_weight_token: float32 [128, 384], replicated
Inputs may be any that keep to these rules, and one draw needn't show every extreme that they name: atom_token never falls and names for each atom the token whose atoms include it; token t has token_counts[t] atoms, all of them together. Atoms k*256 to (k+1)*256 - 1 belong to tokens k*32 - 1 to (k+1)*32 - 1, and for k > 0 the first of them to token k*32 - 1. `token_counts`: the counts add up to 8192.
All inputs are finite; a program needn't handle non-finite values.
Results may differ from a plain program's by a relative error of at most 0.02.
Values may be sent and summed in bfloat16 or wider, within the bound.
No kernel may reach another device: no remote copies, remote signals or barrier semaphores. Data moves between devices by JAX's collectives and lax.ppermute only.
A program may use at most 64 MiB of HBM per device.

v0:
```python
from functools import partial

import jax
import jax.numpy as jnp
from jax import lax
from jax.sharding import PartitionSpec as P

HALO = 64


EPSILON = 1e-05
highest = lax.Precision.HIGHEST


def padded(cells, sides, width):
    for axis, dim in sides:
        count = lax.axis_size(axis)
        ends = count - 1
        head = lax.slice_in_dim(cells, 0, width, axis=dim)
        tail = lax.slice_in_dim(cells, cells.shape[dim] - width, cells.shape[dim], axis=dim)
        cells = jnp.concatenate(
            [
                lax.ppermute(tail, axis, [(i, (i + 1) % count) for i in range(ends)]),
                cells,
                lax.ppermute(head, axis, [((i + 1) % count, i) for i in range(ends)]),
            ],
            axis=dim,
        )
    return cells


def shifted(array, axis, by):
    length = lax.axis_size(axis)
    pairs = [(i, i + by) for i in range(length) if 0 <= i + by < length]
    return lax.ppermute(array, axis, pairs)


def narrow(value):
    return lax.optimization_barrier(value.astype(jnp.bfloat16)).astype(jnp.float32)


def normalize(state, gain):
    centred = state - jnp.mean(state, -1, keepdims=True)
    variance = jnp.mean(centred * centred, -1, keepdims=True)
    return narrow(centred * lax.rsqrt(variance + EPSILON) * gain)


def project(normed, weight):
    return jnp.dot(normed, weight, precision=highest)


def pair_bias(pair_float, bias_weight):
    return jnp.einsum("jcik,ch->jhik", pair_float, bias_weight, precision=highest)


def reach_blocks(rows, block_count, query_rows, pieces):
    channels = rows.shape[-1]
    parts = [
        rows[m * query_rows : m * query_rows + block_count * query_rows].reshape(
            block_count, query_rows, channels
        )
        for m in range(pieces)
    ]
    return jnp.concatenate(parts, 1)


def attend(queries, keys_ext, values_ext, bias, window_shift, first_query, first_key, atom_total):
    block_count, head_count, query_rows, key_count = bias.shape
    channels = queries.shape[1]
    head_size = channels // head_count
    margin = first_query - first_key
    span = keys_ext.shape[0] - block_count * query_rows + query_rows
    pieces = span // query_rows
    offsets = jnp.arange(span, dtype=jnp.int32)
    relative = offsets[None, :] - margin - window_shift[:, None]
    position = (
        first_key
        + jnp.arange(block_count, dtype=jnp.int32)[:, None] * query_rows
        + offsets[None, :]
    )
    inside = (relative >= 0) & (relative < key_count) & (position >= 0) & (position < atom_total)
    window_keys = jnp.arange(key_count, dtype=jnp.int32)
    placement = (relative[:, None, :] == window_keys[None, :, None]).astype(jnp.float32)
    bias_wide = jnp.einsum("jhik,jkl->jhil", bias, placement, precision=highest)
    key_rows = narrow(reach_blocks(keys_ext, block_count, query_rows, pieces)).reshape(
        block_count, span, head_count, head_size
    )
    value_rows = narrow(reach_blocks(values_ext, block_count, query_rows, pieces)).reshape(
        block_count, span, head_count, head_size
    )
    query_block = narrow(queries).reshape(block_count, query_rows, head_count, head_size)
    scores = (
        jnp.einsum("jihd,jkhd->jhik", query_block, key_rows, precision=highest)
        / jnp.sqrt(jnp.float32(head_size))
        + bias_wide
    )
    masked = jnp.where(inside[:, None, None, :], scores, -jnp.inf)
    weights = jnp.exp(masked)
    attention = narrow(weights / jnp.sum(weights, -1, keepdims=True))
    attended = jnp.einsum("jhik,jkhd->jihd", attention, value_rows, precision=highest)
    return attended.reshape(block_count * query_rows, channels)


def finish(
    projected,
    lower,
    upper,
    state,
    bias,
    out_weight,
    kv_weight,
    window_shift,
    first_atom,
    atom_total,
    from_inputs,
):
    channels = state.shape[-1]
    rim_rows = lower.shape[0]
    rows = jnp.concatenate([lower, projected[:, channels : 3 * channels], upper], 0)
    attended = attend(
        projected[:, :channels],
        rows[:, :channels],
        rows[:, channels:],
        bias,
        window_shift,
        first_atom,
        first_atom - rim_rows,
        atom_total,
    )
    update = jnp.dot(narrow(attended), out_weight, precision=highest)
    return state + jax.nn.sigmoid(projected[:, 3 * channels :]) * update


def token_head(state, weight):
    return jax.nn.silu(jnp.dot(narrow(state), weight, precision=highest))


def body(
    atoms_in,
    pair_feats,
    window_shift,
    atom_token,
    token_counts,
    token_grad,
    norm_gain,
    weight_in,
    weight_out,
    weight_bias,
    weight_token,
):
    shard = lax.axis_index("seq")
    atom_rows = atoms_in.shape[1]
    token_rows = token_grad.shape[1]
    channels = atoms_in.shape[2]
    layers = weight_in.shape[0]
    atom_total = atom_rows * lax.axis_size("seq")
    first_atom = shard * atom_rows
    pair_float = pair_feats.astype(jnp.float32)
    in_float = weight_in.astype(jnp.float32)
    out_float = weight_out.astype(jnp.float32)
    token_float = weight_token.astype(jnp.float32)
    layer_apply = jax.vmap(
        partial(
            finish,
            window_shift=window_shift,
            first_atom=first_atom,
            atom_total=atom_total,
            from_inputs=False,
        ),
        in_axes=(0, 0, 0, 0, None, None, None),
    )
    state = atoms_in.astype(jnp.float32)
    saved = []
    for layer in range(layers):
        bias = pair_bias(pair_float, weight_bias[layer])
        normed = normalize(state, norm_gain[layer])
        projected = jnp.dot(
            normed.astype(jnp.bfloat16), weight_in[layer], preferred_element_type=jnp.float32
        )
        outgoing = projected[:, :, channels : 3 * channels].astype(jnp.bfloat16)
        extended = padded(outgoing, (("seq", 1),), HALO)
        lower = extended[:, :HALO].astype(jnp.float32)
        upper = extended[:, HALO + atom_rows :].astype(jnp.float32)
        kv_weight = in_float[layer][:, channels : 3 * channels]
        saved.append((state, normed, projected, bias, lower, upper, kv_weight))
        state = layer_apply(projected, lower, upper, state, bias, out_float[layer], kv_weight)
    scaled = token_grad.astype(jnp.float32) / token_counts.astype(jnp.float32)[None, :, None]
    below = shifted(scaled[:, token_rows - 1 :], "seq", 1)
    token_table = jnp.concatenate([below, scaled], 1)
    local_index = atom_token - (shard * token_rows - 1)
    cotangent = jnp.take(token_table, local_index, axis=1)
    _, token_back = jax.vjp(token_head, state, token_float)
    grad_state, grad_token = token_back(cotangent)
    grad_gains = [None] * layers
    grad_inputs = [None] * layers
    grad_outputs = [None] * layers
    grad_biases = [None] * layers
    pair_local = jnp.zeros(pair_float.shape, jnp.float32)
    for layer in reversed(range(layers)):
        state_in, normed, projected, bias, lower, upper, kv_weight = saved[layer]
        _, layer_back = jax.vjp(
            layer_apply, projected, lower, upper, state_in, bias, out_float[layer], kv_weight
        )
        grad_proj, grad_lower, grad_upper, grad_residual, grad_bias, grad_out, grad_kv = layer_back(
            grad_state
        )
        _, project_back = jax.vjp(project, normed, in_float[layer])
        from_below = shifted(grad_upper.astype(jnp.bfloat16), "seq", 1).astype(grad_upper.dtype)
        from_above = shifted(grad_lower.astype(jnp.bfloat16), "seq", -1).astype(grad_lower.dtype)
        grad_proj = grad_proj.at[:, :HALO, channels : 3 * channels].add(from_below)
        grad_proj = grad_proj.at[:, atom_rows - HALO :, channels : 3 * channels].add(from_above)
        grad_normed, grad_in = project_back(grad_proj)
        _, norm_back = jax.vjp(normalize, state_in, norm_gain[layer])
        grad_norm, grad_gain = norm_back(grad_normed)
        grad_state = grad_residual + grad_norm
        grad_gains[layer] = grad_gain
        grad_inputs[layer] = grad_in
        grad_outputs[layer] = grad_out
        grad_biases[layer] = jnp.einsum("jcik,jhik->ch", pair_float, grad_bias, precision=highest)
        pair_local = pair_local + jnp.einsum(
            "jhik,ch->jcik", grad_bias, weight_bias[layer], precision=highest
        )
    pair_sum = lax.psum_scatter(
        pair_local.astype(jnp.bfloat16), "samp", scatter_dimension=0, tiled=True
    )
    totals = lax.psum(
        (
            jnp.stack(grad_gains),
            jnp.stack(grad_inputs),
            jnp.stack(grad_outputs),
            jnp.stack(grad_biases),
            grad_token,
        ),
        ("seq", "samp"),
    )
    return (
        grad_state.astype(jnp.bfloat16),
        pair_sum,
        totals[0],
        totals[1],
        totals[2],
        totals[3],
        totals[4],
    )


def solution(mesh):
    return jax.shard_map(
        body,
        mesh=mesh,
        in_specs=(
            P("samp", "seq", None),
            P("seq", None, None, None),
            P("seq"),
            P("seq"),
            P("seq"),
            P("samp", "seq", None),
            P(),
            P(),
            P(),
            P(),
            P(),
        ),
        out_specs=(
            P("samp", "seq", None),
            P(("seq", "samp"), None, None, None),
            P(),
            P(),
            P(),
            P(),
            P(),
        ),
        check_vma=False,
    )
```

profile of v0, /device:TPU:1, one launch (start us, length us, event | category | flops | bytes accessed | tf_op | source)
XLA Modules:
  0.0 504.1 jit_solution(13690139700951834181)
XLA Ops:
  9.6 4.5 collective-permute-start
  21.0 1.9 collective-permute-start.2
  23.0 3.6 collective-permute-start.1
  26.6 2.2 fusion.38
  36.8 2.1 fusion.192
  44.4 1.9 collective-permute-start.4
  46.4 3.8 collective-permute-start.3
  55.5 2.1 fusion.194
  69.3 2.2 convolution_convert_fusion.4
  76.7 1.9 fusion.28
  82.4 2.9 convolution_bitcast_fusion.8
  85.3 3.3 fusion.60
  93.8 4.0 collective-permute-start.5
  98.8 2.0 add_select_fusion.1
  100.8 2.7 scatter-add.14
  107.7 1.9 fusion.98
  120.6 1.9 fusion.26
  129.4 4.6 collective-permute-start.7
  134.0 4.1 fusion.4
  142.3 2.4 convolution_bitcast_fusion.9
  144.8 2.7 add_select_fusion
  147.5 2.7 scatter-add.16
  151.9 88.4 %all-reduce.30 = (f32[2,128]{1,0:T(2,128)}, f32[2,16,4]{1,2,0:T(4,128)}) all-reduce(f32[2,128]{1,0:T(2,128)S(1)} %pad_maximum_fusion.3, f32[2,16,4]{1,2,0:T(4,128)S(1)} %pad_maximum_fusion.2), channel_id=1, replica_groups=mesh['seq'=32,'samp'=8] {'seq','samp'}, use_global_device_ids=true, to_apply=%region_16.17 | all-reduce | flops 384 | bytes 3072 | tf_op jit(solution)/shard_map/psum | solution.py:226
  244.0 247.7 %all-reduce.34.cloned.1.call-done = (f32[2,128,512]{2,1,0:T(8,128)}, f32[2,128,128]{2,1,0:T(8,128)}, f32[128,384]{1,0:T(8,128)}) async-done(((f32[2,128,512]{2,1,0:T(8,128)}, f32[2,128,128]{2,1,0:T(8,128)}, f32[128,384]{1,0:T(8,128)}), (f32[2,128,512]{2,1,0:T(8,128)}, f32[2,128,128]{2,1,0:T(8,128)}, f32[128,384]{1,0:T(8,128)})) %all-reduce.34.cloned.1.call-update) | async-done | bytes 851984 | tf_op jit(solution)/shard_map/psum | solution.py:226
  (317 shorter events, 89.6 us)
Async XLA Ops:
  8.0 18.6 %copy-start = (bf16[8,16,32,128]{3,2,1,0:T(8,128)(2,1)S(1)}, bf16[8,16,32,128]{3,2,1,0:T(8,128)(2,1)}, u32[]{:S(2)}) copy-start(bf16[8,16,32,128]{3,2,1,0:T(8,128)(2,1)} %param.20) | copy-start | bytes 3145732
  8.0 20.8 %copy-start.58 = (f32[2,16,4]{1,2,0:T(4,128)S(1)}, f32[2,16,4]{1,2,0:T(4,128)}, u32[]{:S(2)}) copy-start(f32[2,16,4]{1,2,0:T(4,128)} %param.28) | copy-start | bytes 1540
  8.0 234.4 %reduce-scatter.2.cloned.1.call-start = ((), (), s32[]{:S(2)}) async-start(), calls=%async_computation.1 | async-start | bytes 1179648 | tf_op jit(solution)/shard_map/reduce_scatter | solution.py:223
  9.6 23.5 %collective-permute-start = (f32[1,1,384]{2,1,0:T(1,128)S(1)}, f32[1,1,384]{2,1,0:T(1,128)S(1)}, u32[]{:S(2)}, u32[]{:S(2)}) collective-permute-start(f32[1,1,384]{2,1,0:T(1,128)S(1)} %slice.386), channel_id=1, source_target_pairs={{0,8},{8,16},{16,24},{24,32},{32,40},{40,48},{48,56},{56,64},{64,7... | collective-permute-start | bytes 4616 | tf_op jit(solution)/shard_map/ppermute | solution.py:35
  18.0 11.5 %copy-start.61 = (f32[128]{0:T(128)}, f32[128]{0:T(128)S(1)}, u32[]{:S(2)}) copy-start(f32[128]{0:T(128)S(1)} %get-tuple-element.143) | copy-start | bytes 1540
  19.0 11.1 %copy-start.69 = (s32[8]{0:T(128)S(1)}, s32[8]{0:T(128)}, u32[]{:S(2)}) copy-start(s32[8]{0:T(128)} %param.21) | copy-start | bytes 100
  20.2 11.3 %copy-start.71 = (s32[3]{0:T(128)S(1)}, s32[3]{0:T(128)}, u32[]{:S(2)}) copy-start(s32[3]{0:T(128)} %constant.170.clone.1) | copy-start | bytes 40
  20.2 12.1 %copy-start.70 = (s32[256]{0:T(256)S(1)}, s32[256]{0:T(256)}, u32[]{:S(2)}) copy-start(s32[256]{0:T(256)} %param.22) | copy-start | bytes 3076
  21.0 13.9 %collective-permute-start.2 = (bf16[1,64,256]{2,1,0:T(8,128)(2,1)S(1)}, bf16[1,64,256]{2,1,0:T(8,128)(2,1)S(1)}, u32[]{:S(2)}, u32[]{:S(2)}) collective-permute-start(bf16[1,64,256]{2,1,0:T(8,128)(2,1)S(1)} %get-tuple-element.140), channel_id=1, source_target_pairs={{8,0},{16,8},{24,16},{32,24},{40,32},{48,40},{56,48},{64,56},{72,6... | collective-permute-start | bytes 98312 | tf_op jit(solution)/shard_map/ppermute | solution.py:25
  23.0 12.0 %collective-permute-start.1 = (bf16[1,64,256]{2,1,0:T(8,128)(2,1)S(1)}, bf16[1,64,256]{2,1,0:T(8,128)(2,1)S(1)}, u32[]{:S(2)}, u32[]{:S(2)}) collective-permute-start(bf16[1,64,256]{2,1,0:T(8,128)(2,1)S(1)} %get-tuple-element.141), channel_id=1, source_target_pairs={{0,8},{8,16},{16,24},{24,32},{32,40},{40,48},{48,56},{56,64},{64,7... | collective-permute-start | bytes 98312 | tf_op jit(solution)/shard_map/ppermute | solution.py:23
  44.4 6.7 %collective-permute-start.4 = (bf16[1,64,256]{2,1,0:T(8,128)(2,1)S(1)}, bf16[1,64,256]{2,1,0:T(8,128)(2,1)S(1)}, u32[]{:S(2)}, u32[]{:S(2)}) collective-permute-start(bf16[1,64,256]{2,1,0:T(8,128)(2,1)S(1)} %get-tuple-element.136), channel_id=1, source_target_pairs={{8,0},{16,8},{24,16},{32,24},{40,32},{48,40},{56,48},{64,56},{72,6... | collective-permute-start | bytes 98312 | tf_op jit(solution)/shard_map/ppermute | solution.py:25
  46.4 4.8 collective-permute-start.3
  88.6 15.7 %copy-start.26 = (bf16[2,128,512]{2,1,0:T(8,128)(2,1)S(1)}, bf16[2,128,512]{2,1,0:T(8,128)(2,1)}, u32[]{:S(2)}) copy-start(bf16[2,128,512]{2,1,0:T(8,128)(2,1)} %param.26) | copy-start | bytes 786436
  91.8 11.7 %collective-permute-start.6 = (bf16[1,64,256]{2,1,0:T(8,128)(2,1)}, bf16[1,64,256]{2,1,0:T(8,128)(2,1)}, u32[]{:S(2)}, u32[]{:S(2)}) collective-permute-start(bf16[1,64,256]{2,1,0:T(8,128)(2,1)} %get-tuple-element.116), channel_id=1, source_target_pairs={{8,0},{16,8},{24,16},{32,24},{40,32},{48,40},{56,48},{64,56},{72,6... | collective-permute-start | bytes 98312 | tf_op jit(solution)/shard_map/ppermute | solution.py:35
  93.8 5.0 %collective-permute-start.5 = (bf16[1,64,256]{2,1,0:T(8,128)(2,1)S(1)}, bf16[1,64,256]{2,1,0:T(8,128)(2,1)S(1)}, u32[]{:S(2)}, u32[]{:S(2)}) collective-permute-start(bf16[1,64,256]{2,1,0:T(8,128)(2,1)S(1)} %get-tuple-element.117), channel_id=1, source_target_pairs={{0,8},{8,16},{16,24},{24,32},{32,40},{40,48},{48,56},{56,64},{64,7... | collective-permute-start | bytes 98312 | tf_op jit(solution)/shard_map/ppermute | solution.py:35
  103.5 11.1 %copy-start.3 = (bf16[1,8,4,32,160]{4,3,2,1,0:T(8,128)(2,1)S(1)}, bf16[1,8,4,32,160]{4,3,2,1,0:T(8,128)(2,1)}, u32[]{:S(2)}) copy-start(bf16[1,8,4,32,160]{4,3,2,1,0:T(8,128)(2,1)} %copy-done.2) | copy-start | bytes 983044
  127.5 22.7 %collective-permute-start.8 = (bf16[1,64,256]{2,1,0:T(8,128)(2,1)}, bf16[1,64,256]{2,1,0:T(8,128)(2,1)}, u32[]{:S(2)}, u32[]{:S(2)}) collective-permute-start(bf16[1,64,256]{2,1,0:T(8,128)(2,1)} %get-tuple-element.114), channel_id=1, source_target_pairs={{8,0},{16,8},{24,16},{32,24},{40,32},{48,40},{56,48},{64,56},{72,6... | collective-permute-start | bytes 98312 | tf_op jit(solution)/shard_map/ppermute | solution.py:35
  129.4 10.5 %copy-start.28 = (f32[1,256,256]{2,1,0:T(8,128)S(1)}, f32[1,256,256]{2,1,0:T(8,128)}, u32[]{:S(2)}) copy-start(f32[1,256,256]{2,1,0:T(8,128)} %fusion.77) | copy-start | bytes 786436
  129.4 11.4 %copy-start.32 = (bf16[1,256,128]{2,1,0:T(8,128)(2,1)S(1)}, bf16[1,256,128]{2,1,0:T(8,128)(2,1)}, u32[]{:S(2)}) copy-start(bf16[1,256,128]{2,1,0:T(8,128)(2,1)} %copy-done.31) | copy-start | bytes 196612
  129.4 15.3 %collective-permute-start.7 = (bf16[1,64,256]{2,1,0:T(8,128)(2,1)}, bf16[1,64,256]{2,1,0:T(8,128)(2,1)}, u32[]{:S(2)}, u32[]{:S(2)}) collective-permute-start(bf16[1,64,256]{2,1,0:T(8,128)(2,1)} %get-tuple-element.115), channel_id=1, source_target_pairs={{0,8},{8,16},{16,24},{24,32},{32,40},{40,48},{48,56},{56,64},{64,7... | collective-permute-start | bytes 98312 | tf_op jit(solution)/shard_map/ppermute | solution.py:35
  138.2 353.4 %all-reduce.34.cloned.1.call-start = ((), (), s32[]{:S(2)}) async-start(), calls=%async_computation.2 | async-start | bytes 1703936 | tf_op jit(solution)/shard_map/psum | solution.py:226
  140.8 10.2 %copy-start.27 = (bf16[2,128,512]{2,1,0:T(8,128)(2,1)S(1)}, bf16[2,128,512]{2,1,0:T(8,128)(2,1)}, u32[]{:S(2)}) copy-start(bf16[2,128,512]{2,1,0:T(8,128)(2,1)} %param.26) | copy-start | bytes 786436
  142.3 98.0 %copy-start.34 = (bf16[1,256,128]{2,1,0:T(8,128)(2,1)S(1)}, bf16[1,256,128]{2,1,0:T(8,128)(2,1)}, u32[]{:S(2)}) copy-start(bf16[1,256,128]{2,1,0:T(8,128)(2,1)} %copy-done.33) | copy-start | bytes 196612
  150.2 91.3 %copy-start.36 = (f32[1,256,128]{2,1,0:T(8,128)S(1)}, f32[1,256,128]{2,1,0:T(8,128)}, u32[]{:S(2)}) copy-start(f32[1,256,128]{2,1,0:T(8,128)} %copy-done.35) | copy-start | bytes 393220
  (61 other events, 227.3 us)
Sparse Core Ops, SparseCore 0:
  138.3 94.8 reduce-scatter.1
Sparse Core Ops, SparseCore 1:
  241.6 250.0 all-reduce.33
where the time goes:
time: 506 us; the launch traced here: 504 us
  waiting for transfers between devices  248 us (49%)
  blocking collectives  88.4 us (17%)
  matrix products  50.7 us (10%)
  local copies, waits for them, and re-layouts  40 us (8%)
  other arithmetic  31.9 us (6%)
  starting transfers between devices  28.4 us (6%)
  between operations  17 us (3%)
    psum x1, waiting for transfers between devices, body(): lax.psum((jnp.stack(grad_gains), jnp.stack(grad_inputs), jnp.stack(grad_o...  248 us
    psum x1, blocking collectives, body(): lax.psum((jnp.stack(grad_gains), jnp.stack(grad_inputs), jnp.stack(grad_o...  88.4 us
    ppermute x5, starting transfers between devices, shifted(): return lax.ppermute(array, axis, pairs)  17 us
    unnamed x170, local copies, waits for them, and re-layouts  14.8 us
  transfers between devices with their start and end apart: 11, of which 1 were waited for; matrix products, arithmetic and copies ran while one was open for 8% of the time, Pallas kernels for 0%

commit v1 on v0

v1 whole, which is shorter than its diff:
```python
from functools import partial

import jax
import jax.numpy as jnp
from jax import lax
from jax.experimental import pallas as pl
from jax.experimental.pallas import tpu as pltpu
from jax.sharding import PartitionSpec as P

HALO = 64
KWIN = 128
QBLK = 32
HEADS = 4
EPSILON = 1e-05
F32 = jnp.float32
BF16 = jnp.bfloat16
DIMS = (4, 4, 2, 4, 2)
WORLD = ("seq", "samp")


def moves(part, step):
    pairs = []
    for source in range(256):
        place, rest = [], source
        for size in reversed(DIMS):
            place.append(rest % size)
            rest //= size
        place.reverse()
        place[part] = (place[part] + step) % DIMS[part]
        target = 0
        for size, value in zip(DIMS, place):
            target = target * size + value
        pairs.append((source, target))
    return pairs


def hop(value, part, step):
    return lax.ppermute(value, WORLD, moves(part, step))


def shifted(array, by):
    length = lax.axis_size("seq")
    pairs = [(i, i + by) for i in range(length) if 0 <= i + by < length]
    return lax.ppermute(array, "seq", pairs)


def pair_up(own, got):
    if len(got) == 1:
        return own + got[0]
    return (own + got[1]) + (got[0] + got[2])


def everyone(value, part):
    return pair_up(value, [hop(value, part, k) for k in range(1, DIMS[part])])


def run(body, outs, args, smem=(), scratch=(), flops=10**8, nbytes=10**6):
    specs = [
        pl.BlockSpec(memory_space=pltpu.SMEM if i in smem else pltpu.VMEM) for i in range(len(args))
    ]
    return pl.pallas_call(
        body,
        out_shape=[jax.ShapeDtypeStruct(s, d) for s, d in outs],
        in_specs=specs,
        out_specs=[pl.BlockSpec(memory_space=pltpu.VMEM) for _ in outs],
        scratch_shapes=list(scratch),
        compiler_params=pltpu.CompilerParams(vmem_limit_bytes=24 * 2**20),
        cost_estimate=pl.CostEstimate(flops=flops, bytes_accessed=nbytes, transcendentals=0),
    )(*args)


def nn(a, b):
    return jnp.dot(a, b, preferred_element_type=F32)


def nt(a, b):
    return lax.dot_general(a, b, (((1,), (1,)), ((), ())), preferred_element_type=F32)


def tn(a, b):
    return lax.dot_general(a, b, (((0,), (0,)), ((), ())), preferred_element_type=F32)


def stats(state):
    centred = state - jnp.mean(state, -1, keepdims=True)
    scale = lax.rsqrt(jnp.mean(centred * centred, -1, keepdims=True) + EPSILON)
    return centred * scale, scale


def sigmoid(value):
    return 1.0 / (1.0 + jnp.exp(-value))


def head_mask(rows):
    row = lax.broadcasted_iota(jnp.int32, (rows, 128), 0) // QBLK
    lane = lax.broadcasted_iota(jnp.int32, (rows, 128), 1) // 32
    return row == lane


def stacked(block, mask):
    return jnp.where(mask, jnp.concatenate([block.astype(F32)] * HEADS, 0), 0.0).astype(BF16)


def picked(wide, mask):
    wide = jnp.where(mask, wide, 0.0)
    return (wide[0:32] + wide[32:64]) + (wide[64:96] + wide[96:128])


def project_into(state, gain, weight, normed_ref, q_ref, kv_ref, gate_ref, head_ref, tail_ref):
    unit, _ = stats(state)
    normed = (unit * gain).astype(BF16)
    normed_ref[...] = normed
    projected = nn(normed, weight)
    q_ref[...] = projected[:, 0:128].astype(BF16)
    kv = projected[:, 128:384].astype(BF16)
    kv_ref[...] = kv
    gate_ref[...] = sigmoid(projected[:, 384:512])
    rows = kv.shape[0]
    head_ref[...] = kv[0:HALO]
    tail_ref[0:HALO, :] = kv[rows - HALO : rows]


def count_rows(counts):
    size = counts.shape[1]
    row = lax.broadcasted_iota(jnp.int32, (size, size), 0)
    lane = lax.broadcasted_iota(jnp.int32, (size, size), 1)
    column = jnp.sum(jnp.where(row == lane, counts.astype(F32), 0.0), -1, keepdims=True)
    return jnp.broadcast_to(column, (size, 128))


def first_kernel(atoms, gain, weight, grad, counts, normed, q, kv, gate, head, tail):
    project_into(
        atoms[...].astype(F32), gain[0:1, :], weight[0], normed, q, kv, gate, head, tail
    )
    last = lax.broadcasted_iota(jnp.int32, (16, 384), 0) == 15
    row = jnp.where(last, grad[16:32, :].astype(F32), 0.0).astype(BF16)
    many = jnp.where(last[:, :128], count_rows(counts[...])[16:32], 0.0).astype(BF16)
    tail[HALO : HALO + 16, :] = row[:, 0:256]
    tail[HALO + 16 : HALO + 32, 0:128] = row[:, 256:384]
    tail[HALO + 16 : HALO + 32, 128:256] = many


def bias_kernel(weight, pair, bias):
    def block(j, carry):
        totals = [None] * 8
        for c in range(16):
            part = pair[j, c * 32 : (c + 1) * 32, :].astype(F32)
            for m in range(8):
                term = part * weight[m // 4, c, m % 4]
                totals[m] = term if c == 0 else totals[m] + term
        for m in range(8):
            bias[m // 4, j, (m % 4) * 32 : (m % 4 + 1) * 32, :] = totals[m]
        return carry

    lax.fori_loop(0, pair.shape[0], block, 0)


def load_window(kv, lower, upper, keys, values):
    rows = kv.shape[0]
    for ref, at in ((keys, 0), (values, 128)):
        ref[0:HALO, :] = lower[0:HALO, at : at + 128].astype(F32)
        ref[HALO : HALO + rows, :] = kv[:, at : at + 128].astype(F32)
        ref[HALO + rows : HALO + rows + HALO, :] = upper[:, at : at + 128].astype(F32)


def attention_forward(shift, q, bias, layer, keys, values, chances, att, atom_total):
    blocks = q.shape[0] // QBLK
    mask = head_mask(128)
    first = lax.axis_index("seq") * q.shape[0]
    lane = lax.broadcasted_iota(jnp.int32, (1, KWIN), 1)
    for j in range(blocks):
        begin = j * QBLK + shift[j]
        window = pl.ds(begin + HALO, KWIN)
        key = keys[window, :].astype(BF16)
        value = values[window, :].astype(BF16)
        wide = stacked(q[j * QBLK : (j + 1) * QBLK, :], mask)
        scores = nt(wide, key) * (32.0**-0.5) + bias[layer, j]
        place = first + begin + lane
        inside = jnp.logical_and(place >= 0, place < atom_total)
        weights = jnp.where(inside, jnp.exp(scores), 0.0)
        chance = weights * (1.0 / jnp.sum(weights, -1, keepdims=True))
        chances[j] = chance
        out = nn(chance.astype(BF16), value)
        att[j * QBLK : (j + 1) * QBLK, :] = picked(out, mask).astype(BF16)


def attention_backward(
    shift, q, keys, values, chances, grad_att, grad_q, grad_keys, grad_values, score_grad
):
    blocks = q.shape[0] // QBLK
    mask = head_mask(128)
    grad_keys[...] = jnp.zeros_like(grad_keys)
    grad_values[...] = jnp.zeros_like(grad_values)
    for j in range(blocks):
        window = pl.ds(j * QBLK + shift[j] + HALO, KWIN)
        rows = slice(j * QBLK, (j + 1) * QBLK)
        key = keys[window, :].astype(BF16)
        value = values[window, :].astype(BF16)
        wide = stacked(q[rows, :], mask)
        out = stacked(grad_att[rows, :], mask)
        chance = chances[j]
        grad_chance = nt(out, value).astype(BF16).astype(F32)
        term = chance * grad_chance
        grad_score = term - chance * jnp.sum(term, -1, keepdims=True)
        score_grad[j] = grad_score.astype(BF16)
        scaled = (grad_score * (32.0**-0.5)).astype(BF16)
        grad_q[rows, :] = picked(nn(scaled, key), mask).astype(BF16)
        grad_keys[window, :] += tn(scaled, wide).astype(BF16).astype(F32)
        grad_values[window, :] += tn(chance.astype(BF16), out).astype(BF16).astype(F32)


def share_scores(score_grad, own, one, two, three):
    y = lax.axis_index("samp") // 2
    for k, ref in enumerate((own, one, two, three)):
        ref[...] = score_grad[pl.ds(lax.rem(y + k, 4) * 2, 2)]


def forward_kernel(
    atom_total,
    shift,
    q,
    kv,
    lower,
    upper,
    bias,
    gate,
    atoms,
    weight_out,
    gain,
    weight_in,
    state,
    chances,
    att,
    normed,
    q_next,
    kv_next,
    gate_next,
    head,
    tail,
    keys,
    values,
):
    load_window(kv, lower, upper, keys, values)
    attention_forward(shift, q, bias, 0, keys, values, chances, att, atom_total)
    after = atoms[...].astype(F32) + gate[...] * nn(att[...], weight_out[0])
    state[...] = after
    project_into(
        after, gain[1:2, :], weight_in[1], normed, q_next, kv_next, gate_next, head, tail
    )


def layer_back(
    grad_state, gate, att, weight_out, layer, grad_gate, grad_update, grad_att, update=None
):
    if update is None:
        update = nn(att[...], weight_out[layer])
    gates = gate[...]
    grad_gate[...] = (grad_state * update * gates * (1.0 - gates)).astype(BF16)
    change = (grad_state * gates).astype(BF16)
    grad_update[...] = change
    grad_att[...] = nt(change, weight_out[layer]).astype(BF16)


def send_halo(grad_keys, grad_values, center, lower, upper):
    rows = center.shape[0]
    for ref, at in ((grad_keys, 0), (grad_values, 128)):
        lower[:, at : at + 128] = ref[0:HALO, :].astype(BF16)
        center[:, at : at + 128] = ref[HALO : HALO + rows, :]
        upper[:, at : at + 128] = ref[HALO + rows : HALO + rows + HALO, :].astype(BF16)


def middle_kernel(
    atom_total,
    shift,
    q,
    kv,
    lower,
    upper,
    bias,
    gate,
    state,
    weight_out,
    weight_token,
    grad,
    counts,
    atom_token,
    below,
    att,
    grad_update,
    narrow_state,
    grad_hidden,
    grad_state,
    grad_gate,
    grad_q,
    center,
    grad_lower,
    grad_upper,
    score_own,
    score_one,
    score_two,
    score_three,
    keys,
    values,
    chances,
    grad_att,
    grad_keys,
    grad_values,
    score_grad,
):
    load_window(kv, lower, upper, keys, values)
    attention_forward(shift, q, bias, 1, keys, values, chances, att, atom_total)
    update = nn(att[...], weight_out[1])
    after = (state[...] + gate[...] * update).astype(BF16)
    narrow_state[...] = after
    tokens = grad.shape[0]
    atoms = q.shape[0]
    place = atom_token[...] - lax.axis_index("seq") * tokens
    place = jnp.where(place < 0, tokens + 15, place)
    chosen = lax.broadcasted_iota(jnp.int32, (tokens + 16, atoms), 0) == place
    chosen = jnp.where(chosen, 1.0, 0.0).astype(BF16)
    own = jnp.concatenate([grad[...], count_rows(counts[...]).astype(BF16)], 1)
    before = jnp.concatenate([below[HALO : HALO + 16, :], below[HALO + 16 : HALO + 32, :]], 1)
    found = tn(chosen, jnp.concatenate([own, before], 0))
    many = found[:, 384:512]
    cotangent = found[:, 0:384] / jnp.concatenate([many] * 3, 1)
    hidden = nn(after, weight_token[...])
    open_ = sigmoid(hidden)
    back = (cotangent * (open_ * (1.0 + hidden * (1.0 - open_)))).astype(BF16)
    grad_hidden[...] = back
    rising = nt(back, weight_token[...]).astype(BF16).astype(F32)
    grad_state[...] = rising
    layer_back(rising, gate, att, weight_out, 1, grad_gate, grad_update, grad_att, update)
    attention_backward(
        shift, q, keys, values, chances, grad_att, grad_q, grad_keys, grad_values, score_grad
    )
    send_halo(grad_keys, grad_values, center, grad_lower, grad_upper)
    share_scores(score_grad, score_own, score_one, score_two, score_three)


def pair_weight_grad(pair, scores, out):
    y = lax.axis_index("samp") // 2
    left, right = [], []
    for k, ref in enumerate(scores):
        base = lax.rem(y + k, 4) * 2
        for m in range(2):
            left.append(pair[base + m])
            right.append(ref[m])
    product = nt(jnp.concatenate(left, 1), jnp.concatenate(right, 1))
    row = lax.rem(lax.broadcasted_iota(jnp.int32, product.shape, 0), QBLK)
    lane = lax.rem(lax.broadcasted_iota(jnp.int32, product.shape, 1), QBLK)
    product = jnp.where(row == lane, product, 0.0)
    for c in range(16):
        out[c : c + 1, :] = jnp.sum(product[c * 32 : (c + 1) * 32], 0, keepdims=True)


def middle_weights_kernel(
    pair, own, one, two, three, narrow_state, grad_hidden, att, grad_update, token, out, bias
):
    pair_weight_grad(pair, (own, one, two, three), bias)
    product = tn(narrow_state[...], grad_hidden[...])
    for m in range(3):
        token[m * 128 : (m + 1) * 128, :] = product[:, m * 128 : (m + 1) * 128]
    out[...] = tn(att[...], grad_update[...])


def join_projected(grad_q, center, from_below, from_above, grad_gate, joined):
    rows = center.shape[0]
    joined[:, 0:128] = grad_q[...]
    joined[:, 384:512] = grad_gate[...]
    joined[0:HALO, 128:384] = (center[0:HALO, :] + from_below[...].astype(F32)).astype(BF16)
    joined[HALO : rows - HALO, 128:384] = center[HALO : rows - HALO, :].astype(BF16)
    joined[rows - HALO : rows, 128:384] = (
        center[rows - HALO : rows, :] + from_above[...].astype(F32)
    ).astype(BF16)


def norm_back(grad_normed, state, gain):
    unit, scale = stats(state)
    grad_gain = jnp.sum(grad_normed * unit, 0, keepdims=True)
    back = grad_normed * gain
    back = scale * (
        back - jnp.mean(back, -1, keepdims=True) - unit * jnp.mean(back * unit, -1, keepdims=True)
    )
    return back, grad_gain


def backward_kernel(
    shift,
    grad_q_later,
    center_later,
    from_below,
    from_above,
    grad_gate_later,
    state,
    gain,
    weight_in,
    grad_state_later,
    q,
    kv,
    lower,
    upper,
    gate,
    att,
    weight_out,
    chances,
    joined,
    grad_gain,
    grad_update,
    grad_state,
    grad_gate,
    grad_q,
    center,
    grad_lower,
    grad_upper,
    score_own,
    score_one,
    score_two,
    score_three,
    keys,
    values,
    grad_att,
    grad_keys,
    grad_values,
    score_grad,
):
    load_window(kv, lower, upper, keys, values)
    join_projected(grad_q_later, center_later, from_below, from_above, grad_gate_later, joined)
    grad_normed = nt(joined[...], weight_in[1]).astype(BF16).astype(F32)
    back, gained = norm_back(grad_normed, state[...], gain[1:2, :])
    grad_gain[...] = gained
    rising = grad_state_later[...] + back
    grad_state[...] = rising
    layer_back(rising, gate, att, weight_out, 0, grad_gate, grad_update, grad_att)
    attention_backward(
        shift, q, keys, values, chances, grad_att, grad_q, grad_keys, grad_values, score_grad
    )
    send_halo(grad_keys, grad_values, center, grad_lower, grad_upper)
    share_scores(score_grad, score_own, score_one, score_two, score_three)


def backward_weights_kernel(
    pair, own, one, two, three, normed, joined, att, grad_update, inner, out, bias
):
    pair_weight_grad(pair, (own, one, two, three), bias)
    product = tn(normed[...], joined[...])
    for m in range(4):
        inner[m * 128 : (m + 1) * 128, :] = product[:, m * 128 : (m + 1) * 128]
    out[...] = tn(att[...], grad_update[...])


BIG = 208
SPAN = 224


def last_kernel(
    grad_q,
    center,
    from_below,
    from_above,
    grad_gate,
    atoms,
    gain,
    weight_in,
    grad_state,
    normed,
    token,
    out_later,
    inner_later,
    out_first,
    gain_later,
    bias_later,
    bias_first,
    grad_atoms,
    keep,
    send,
    joined,
    whole,
):
    join_projected(grad_q, center, from_below, from_above, grad_gate, joined)
    grad_normed = nt(joined[...], weight_in[0]).astype(BF16).astype(F32)
    back, gained = norm_back(grad_normed, atoms[...].astype(F32), gain[0:1, :])
    grad_atoms[...] = (grad_state[...] + back).astype(BF16)
    product = tn(normed[...], joined[...])
    sources = [(token, r) for r in range(0, 384, 16)]
    sources += [(out_later, r) for r in range(0, 128, 16)]
    sources += [(inner_later, r) for r in range(0, 512, 16)]
    sources += [(out_first, r) for r in range(0, 128, 16)]
    for index, (ref, r) in enumerate(sources):
        row = index * 16
        whole[row // BIG, row % BIG : row % BIG + 16, :] = ref[r : r + 16, :]
    for m in range(4):
        for r in range(0, 128, 16):
            row = 1152 + m * 128 + r
            whole[row // BIG, row % BIG : row % BIG + 16, :] = product[
                r : r + 16, m * 128 : (m + 1) * 128
            ]
    whole[0, BIG:SPAN, :] = bias_first[...]
    whole[1, BIG:SPAN, :] = bias_later[...]
    first = lax.broadcasted_iota(jnp.int32, (16, 128), 0) == 0
    whole[2, BIG:SPAN, :] = jnp.where(first, gained, gain_later[...])
    for m in range(3, 8):
        whole[m, BIG:SPAN, :] = jnp.zeros((16, 128), F32)
    core = lax.rem(lax.axis_index("seq"), 2)
    keep[...] = whole[pl.ds(core * 4, 4)]
    send[...] = whole[pl.ds((1 - core) * 4, 4)].astype(BF16)


def core_kernel(keep, got, own, one, two, three, whole):
    whole[...] = keep[...] + got[...].astype(F32)
    y = lax.axis_index("samp") // 2
    own[...] = whole[y]
    for k, ref in enumerate((one, two, three)):
        ref[...] = whole[lax.rem(y + k + 1, 4)].astype(BF16)


def quarter_kernel(own, one, two, three, half):
    y = lax.axis_index("samp") // 2
    half[y] = own[...]
    for k, ref in enumerate((one, two, three)):
        half[lax.rem(y + 3 - k, 4)] = ref[...]


def finish_kernel(half, got, grad_gain, inner, out, bias, token, whole):
    core = lax.rem(lax.axis_index("seq"), 2)
    whole[pl.ds(core * 4, 4)] = half[...]
    whole[pl.ds((1 - core) * 4, 4)] = got[...]

    def take(ref, base, blocks):
        for m in range(blocks):
            for r in range(0, 128, 16):
                row = base + m * 128 + r
                ref[r : r + 16, m * 128 : (m + 1) * 128] = whole[
                    row // BIG, row % BIG : row % BIG + 16, :
                ]

    take(token, 0, 3)
    take(out.at[1], 384, 1)
    take(inner.at[1], 512, 4)
    take(out.at[0], 1024, 1)
    take(inner.at[0], 1152, 4)
    grad_gain[...] = whole[2, BIG : BIG + 2, :]
    for layer in range(2):
        spread = whole[layer, BIG:SPAN, :]
        lane = lax.broadcasted_iota(jnp.int32, spread.shape, 1) // QBLK
        for h in range(HEADS):
            bias[layer, :, h : h + 1] = jnp.sum(
                jnp.where(lane == h, spread, 0.0), -1, keepdims=True
            )


def expand_kernel(weight, first, later, pair):
    refs = (first, later)
    for c in range(16):
        value = None
        for layer in range(2):
            for h in range(HEADS):
                term = refs[layer][h * 32 : (h + 1) * 32, :] * weight[layer, c, h]
                value = term if value is None else value + term
        pair[c * 32 : (c + 1) * 32, :] = value.astype(BF16)


def sum_scores(own, one, two, three):
    got = [hop(v, 3, k + 1).astype(F32) for k, v in enumerate((one, two, three))]
    both = pair_up(own.astype(F32), got)
    far = lax.rem(lax.axis_index("samp"), 2)
    away = lax.dynamic_index_in_dim(both, 1 - far, 0, False).astype(BF16)
    return lax.dynamic_index_in_dim(both, far, 0, False) + hop(away, 4, 1).astype(F32)


def body(
    atoms_in,
    pair_feats,
    window_shift,
    atom_token,
    token_counts,
    token_grad,
    norm_gain,
    weight_in,
    weight_out,
    weight_bias,
    weight_token,
):
    rows = atoms_in.shape[1]
    blocks = pair_feats.shape[0]
    atom_total = rows * lax.axis_size("seq")
    atoms = atoms_in[0]
    grad = token_grad[0]
    pair = pair_feats.reshape(blocks, 512, 128)
    counts = token_counts.reshape(1, -1)
    token_row = atom_token.reshape(1, -1)
    ext = rows + 2 * HALO
    window = [pltpu.VMEM((ext, 128), F32), pltpu.VMEM((ext, 128), F32)]
    square = ((blocks, 128, 128), F32)
    wide = ((rows, 128), BF16)
    full = ((rows, 128), F32)
    kv_shape = ((rows, 256), BF16)
    rim = ((HALO, 256), BF16)
    score_piece = ((2, 128, 128), BF16)

    normed0, q0, kv0, gate0, head0, tail0 = run(
        first_kernel,
        [wide, wide, kv_shape, full, rim, ((HALO + 32, 256), BF16)],
        (atoms, norm_gain, weight_in, grad, counts),
    )
    lower0 = shifted(tail0, 1)
    upper0 = shifted(head0, -1)
    (bias,) = run(
        bias_kernel,
        [((2, blocks, 128, 128), F32)],
        (weight_bias, pair),
        smem=(0,),
        nbytes=2 * 10**6,
    )
    state1, chances0, att0, normed1, q1, kv1, gate1, head1, tail1 = run(
        partial(forward_kernel, atom_total),
        [full, square, wide, wide, wide, kv_shape, full, rim, rim],
        (
            window_shift,
            q0,
            kv0,
            lower0,
            upper0,
            bias,
            gate0,
            atoms,
            weight_out,
            norm_gain,
            weight_in,
        ),
        smem=(0,),
        scratch=window,
    )
    lower1 = shifted(tail1, 1)
    upper1 = shifted(head1, -1)
    back_scratch = [
        pltpu.VMEM((rows, 128), BF16),
        pltpu.VMEM((ext, 128), F32),
        pltpu.VMEM((ext, 128), F32),
        pltpu.VMEM((blocks, 128, 128), BF16),
    ]
    (
        att1,
        grad_update1,
        narrow_state,
        grad_hidden,
        grad_state2,
        grad_gate1,
        grad_q1,
        center1,
        grad_lower1,
        grad_upper1,
        *scores1,
    ) = run(
        partial(middle_kernel, atom_total),
        [
            wide,
            wide,
            wide,
            ((rows, 384), BF16),
            full,
            wide,
            wide,
            ((rows, 256), F32),
            rim,
            rim,
            score_piece,
            score_piece,
            score_piece,
            score_piece,
        ],
        (
            window_shift,
            q1,
            kv1,
            lower1,
            upper1,
            bias,
            gate1,
            state1,
            weight_out,
            weight_token,
            grad,
            counts,
            token_row,
            lower0,
        ),
        smem=(0,),
        scratch=window + [pltpu.VMEM((blocks, 128, 128), F32)] + back_scratch,
    )
    from_below1 = shifted(grad_upper1, 1)
    from_above1 = shifted(grad_lower1, -1)
    grad_token, grad_out1, grad_bias1 = run(
        middle_weights_kernel,
        [((384, 128), F32), ((128, 128), F32), ((16, 128), F32)],
        (pair, *scores1, narrow_state, grad_hidden, att1, grad_update1),
    )
    (
        joined1,
        grad_gain1,
        grad_update0,
        grad_state1,
        grad_gate0,
        grad_q0,
        center0,
        grad_lower0,
        grad_upper0,
        *scores0,
    ) = run(
        backward_kernel,
        [
            ((rows, 512), BF16),
            ((1, 128), F32),
            wide,
            full,
            wide,
            wide,
            ((rows, 256), F32),
            rim,
            rim,
            score_piece,
            score_piece,
            score_piece,
            score_piece,
        ],
        (
            window_shift,
            grad_q1,
            center1,
            from_below1,
            from_above1,
            grad_gate1,
            state1,
            norm_gain,
            weight_in,
            grad_state2,
            q0,
            kv0,
            lower0,
            upper0,
            gate0,
            att0,
            weight_out,
            chances0,
        ),
        smem=(0,),
        scratch=window + back_scratch,
    )
    from_below0 = shifted(grad_upper0, 1)
    from_above0 = shifted(grad_lower0, -1)
    grad_in1, grad_out0, grad_bias0 = run(
        backward_weights_kernel,
        [((512, 128), F32), ((128, 128), F32), ((16, 128), F32)],
        (pair, *scores0, normed1, joined1, att0, grad_update0),
    )
    grad_atoms, keep, send = run(
        last_kernel,
        [wide, ((4, SPAN, 128), F32), ((4, SPAN, 128), BF16)],
        (
            grad_q0,
            center0,
            from_below0,
            from_above0,
            grad_gate0,
            atoms,
            norm_gain,
            weight_in,
            grad_state1,
            normed0,
            grad_token,
            grad_out1,
            grad_in1,
            grad_out0,
            grad_gain1,
            grad_bias1,
            grad_bias0,
        ),
        scratch=[pltpu.VMEM((rows, 512), BF16), pltpu.VMEM((8, SPAN, 128), F32)],
    )
    own, one, two, three = run(
        core_kernel,
        [((SPAN, 128), F32)] + [((SPAN, 128), BF16)] * 3,
        (keep, hop(send, 2, 1)),
        scratch=[pltpu.VMEM((4, SPAN, 128), F32)],
    )
    got = [hop(v, 3, k + 1).astype(F32) for k, v in enumerate((one, two, three))]
    total = pair_up(own, got)
    total = everyone(total, 1)
    total = everyone(total, 0)
    total = everyone(total, 4)
    (half,) = run(
        quarter_kernel,
        [((4, SPAN, 128), F32)],
        (total, *[hop(total, 3, k) for k in range(1, 4)]),
    )
    grad_gain, grad_in, grad_out, grad_bias, grad_token = run(
        finish_kernel,
        [
            ((2, 128), F32),
            ((2, 128, 512), F32),
            ((2, 128, 128), F32),
            ((2, 16, 4), F32),
            ((128, 384), F32),
        ],
        (half, hop(half, 2, 1)),
        scratch=[pltpu.VMEM((8, SPAN, 128), F32)],
    )
    (pair_sum,) = run(
        expand_kernel,
        [((512, 128), BF16)],
        (weight_bias, sum_scores(*scores0), sum_scores(*scores1)),
        smem=(0,),
    )
    return (
        grad_atoms[None],
        pair_sum.reshape(1, 16, 32, 128),
        grad_gain,
        grad_in,
        grad_out,
        grad_bias,
        grad_token,
    )


def solution(mesh):
    return jax.shard_map(
        body,
        mesh=mesh,
        in_specs=(
            P("samp", "seq", None),
            P("seq", None, None, None),
            P("seq"),
            P("seq"),
            P("seq"),
            P("samp", "seq", None),
            P(),
            P(),
            P(),
            P(),
            P(),
        ),
        out_specs=(
            P("samp", "seq", None),
            P(("seq", "samp"), None, None, None),
            P(),
            P(),
            P(),
            P(),
            P(),
        ),
        check_vma=False,
    )
```

time: 506 us -> 122 us (0.24)
  waiting for transfers between devices: 248 us -> 17.7 us
  blocking collectives: 88.4 us -> 0 us
  matrix products: 50.7 us -> 0 us
  starting transfers between devices: 28.4 us -> 75.4 us
  local copies, waits for them, and re-layouts: 40 us -> 6.53 us
  other arithmetic: 31.9 us -> 0.19 us
  Pallas kernels: 0 us -> 19.2 us
  between operations: 17 us -> 0.96 us
    psum x1 -> x0, waiting for transfers between devices: 248 us -> none  [body(): lax.psum((jnp.stack(grad_gains), jnp.stack(grad_inputs), jnp.stack(grad_o...]
    psum x1 -> x0, blocking collectives: 88.4 us -> none  [body(): lax.psum((jnp.stack(grad_gains), jnp.stack(grad_inputs), jnp.stack(grad_o...]
    dot_general x37 -> x0, matrix products: 50.7 us -> none  [the longest x4 7.99 us: attend(): bias_wide = jnp.einsum('jhik,jkl->jhil', bias, placement, precision=highest)]
    ppermute x9 -> x31, starting transfers between devices: 28.3 us -> 75.4 us  [the longest x23 54.6 us: hop(): return lax.ppermute(value, WORLD, moves(part, step))]
    pallas_call x0 -> x12, Pallas kernels: none -> 19.2 us  [run(): pl.pallas_call(body, out_shape=[jax.ShapeDtypeStruct(s, d) for s, d in ou...]
    ppermute x9 -> x31, waiting for transfers between devices: 0.07 us -> 17.7 us  [the longest x23 9.79 us: hop(): return lax.ppermute(value, WORLD, moves(part, step))]
    another operation x12 -> x0, other arithmetic: 8.64 us -> none
    unnamed x170 -> x32, local copies, waits for them, and re-layouts: 14.8 us -> 6.5 us
  transfers between devices with their start and end apart: 11 -> 31, of which waited for: 1 -> 8; matrix products, arithmetic and copies ran while one was open for 8% -> 0% of each run, Pallas kernels for 0% -> 4%
where the time goes in v1:
time: 122 us; the launch traced here: 120 us
  starting transfers between devices  75.4 us (62%)
  Pallas kernels  19.2 us (16%)
  waiting for transfers between devices  17.7 us (15%)
  local copies, waits for them, and re-layouts  6.53 us (5%)
    ppermute x23, starting transfers between devices, hop(): return lax.ppermute(value, WORLD, moves(part, step))  54.6 us
    ppermute x8, starting transfers between devices, shifted(): return lax.ppermute(array, 'seq', pairs)  20.8 us
    pallas_call x12, Pallas kernels, run(): pl.pallas_call(body, out_shape=[jax.ShapeDtypeStruct(s, d) for s, d in ou...  19.2 us
    ppermute x23, waiting for transfers between devices, hop(): return lax.ppermute(value, WORLD, moves(part, step))  9.79 us
    ppermute x8, waiting for transfers between devices, shifted(): return lax.ppermute(array, 'seq', pairs)  7.91 us
    unnamed x32, local copies, waits for them, and re-layouts  6.5 us
  transfers between devices with their start and end apart: 31, of which 8 were waited for; matrix products, arithmetic and copies ran while one was open for 0% of the time, Pallas kernels for 4%

profile of v1, /device:TPU:1, one launch (start us, length us, event | category | flops | bytes accessed | tf_op | source)
XLA Modules:
  0.0 120.0 jit_solution(14472821476968905911)
XLA Ops:
  4.3 4.5 %collective-permute-start = (bf16[96,256]{1,0:T(8,128)(2,1)S(1)}, bf16[96,256]{1,0:T(8,128)(2,1)S(1)}, u32[]{:S(2)}, u32[]{:S(2)}) collective-permute-start(bf16[96,256]{1,0:T(8,128)(2,1)S(1)} %get-tuple-element.69), channel_id=1, source_target_pairs={{0,8},{8,16},{16,24},{24,32},{32,40},{40,48},{48,56},{56,64},{64,7... | collective-permute-start | bytes 147464 | tf_op jit(solution)/shard_map/ppermute | solution.py:44
  12.1 2.1 %shard_map.163.bias = f32[2,8,128,128]{3,2,1,0:T(8,128)S(1)} custom-call(f32[2,16,4]{2,1,0:T(8,128)S(1)} %copy.18.weight, bf16[8,512,128]{2,1,0:T(8,128)(2,1)S(1)} %bitcast.15), custom_call_target="tpu_custom_call" | custom-call | flops 100000000 | bytes 2000000 | tf_op jit(solution)/shard_map/pallas_call | solution.py:61
  14.9 2.8 %shard_map.164 = (f32[256,128]{1,0:T(8,128)S(1)}, f32[8,128,128]{2,1,0:T(8,128)S(1)}, bf16[256,128]{1,0:T(8,128)(2,1)S(1)}, bf16[256,128]{1,0:T(8,128)(2,1)S(1)}...) custom-call(s32[8]{0:T(128)S(1)} %copy-done.11, ...), custom_call_target="tpu_custom_call" | custom-call | flops 100000000 | bytes 1000000 | tf_op jit(solution)/shard_map/pallas_call | solution.py:61
  17.7 3.6 %collective-permute-start.2 = (bf16[64,256]{1,0:T(8,128)(2,1)S(1)}, bf16[64,256]{1,0:T(8,128)(2,1)S(1)}, u32[]{:S(2)}, u32[]{:S(2)}) collective-permute-start(bf16[64,256]{1,0:T(8,128)(2,1)S(1)} %get-tuple-element.74), channel_id=1, source_target_pairs={{0,8},{8,16},{16,24},{24,32},{32,40},{40,48},{48,56},{56,64},{64,7... | collective-permute-start | bytes 98312 | tf_op jit(solution)/shard_map/ppermute | solution.py:44
  23.3 3.3 %collective-permute-done.3.upper = bf16[64,256]{1,0:T(8,128)(2,1)S(1)} collective-permute-done((bf16[64,256]{1,0:T(8,128)(2,1)S(1)}, bf16[64,256]{1,0:T(8,128)(2,1)S(1)}, u32[]{:S(2)}, u32[]{:S(2)}) %collective-permute-start.3) | collective-permute-done | bytes 32800 | tf_op jit(solution)/shard_map/ppermute | solution.py:44
  27.3 5.6 %shard_map.165 = (bf16[256,128]{1,0:T(8,128)(2,1)S(1)}, bf16[256,128]{1,0:T(8,128)(2,1)S(1)}, bf16[256,128]{1,0:T(8,128)(2,1)S(1)}, bf16[256,384]{1,0:T(8,128)(2...) custom-call(s32[8]{0:T(128)S(1)} %copy-done.11, ...), custom_call_target="tpu_custom_call" | custom-call | flops 100000000 | bytes 1000000 | tf_op jit(solution)/shard_map/pallas_call | solution.py:61
  32.9 2.1 %collective-permute-start.4 = (bf16[64,256]{1,0:T(8,128)(2,1)S(1)}, bf16[64,256]{1,0:T(8,128)(2,1)S(1)}, u32[]{:S(2)}, u32[]{:S(2)}) collective-permute-start(bf16[64,256]{1,0:T(8,128)(2,1)S(1)} %get-tuple-element.80), channel_id=1, source_target_pairs={{0,8},{8,16},{16,24},{24,32},{32,40},{40,48},{48,56},{56,64},{64,7... | collective-permute-start | bytes 98312 | tf_op jit(solution)/shard_map/ppermute | solution.py:44
  35.0 2.4 %collective-permute-start.5 = (bf16[64,256]{1,0:T(8,128)(2,1)S(1)}, bf16[64,256]{1,0:T(8,128)(2,1)S(1)}, u32[]{:S(2)}, u32[]{:S(2)}) collective-permute-start(bf16[64,256]{1,0:T(8,128)(2,1)S(1)} %get-tuple-element.81), channel_id=1, source_target_pairs={{8,0},{16,8},{24,16},{32,24},{40,32},{48,40},{56,48},{64,56},{72,6... | collective-permute-start | bytes 98312 | tf_op jit(solution)/shard_map/ppermute | solution.py:44
  37.4 2.8 %collective-permute-done.5.from_above = bf16[64,256]{1,0:T(8,128)(2,1)S(1)} collective-permute-done((bf16[64,256]{1,0:T(8,128)(2,1)S(1)}, bf16[64,256]{1,0:T(8,128)(2,1)S(1)}, u32[]{:S(2)}, u32[]{:S(2)}) %collective-permute-start.5) | collective-permute-done | bytes 32800 | tf_op jit(solution)/shard_map/ppermute | solution.py:44
  40.2 3.3 %shard_map.166 = (bf16[256,512]{1,0:T(8,128)(2,1)S(1)}, f32[1,128]{1,0:T(1,128)S(1)}, bf16[256,128]{1,0:T(8,128)(2,1)S(1)}, f32[256,128]{1,0:T(8,128)S(1)}, bf16...) custom-call(s32[8]{0:T(128)S(1)} %copy-done.11, ...), custom_call_target="tpu_custom_call" | custom-call | flops 100000000 | bytes 1000000 | tf_op jit(solution)/shard_map/pallas_call | solution.py:61
  45.5 2.4 %collective-permute-start.7 = (bf16[64,256]{1,0:T(8,128)(2,1)S(1)}, bf16[64,256]{1,0:T(8,128)(2,1)S(1)}, u32[]{:S(2)}, u32[]{:S(2)}) collective-permute-start(bf16[64,256]{1,0:T(8,128)(2,1)S(1)} %get-tuple-element.89), channel_id=1, source_target_pairs={{8,0},{16,8},{24,16},{32,24},{40,32},{48,40},{56,48},{64,56},{72,6... | collective-permute-start | bytes 98312 | tf_op jit(solution)/shard_map/ppermute | solution.py:44
  53.4 3.0 %collective-permute-start.17 = (bf16[224,128]{1,0:T(8,128)(2,1)S(1)}, bf16[224,128]{1,0:T(8,128)(2,1)S(1)}, u32[]{:S(2)}, u32[]{:S(2)}) collective-permute-start(bf16[224,128]{1,0:T(8,128)(2,1)S(1)} %get-tuple-element.119), channel_id=1, source_target_pairs={{0,4},{1,5},{2,6},{3,7},{4,0},{5,1},{6,2},{7,3},{8,12},{9,13},{10,... | collective-permute-start | bytes 172040 | tf_op jit(solution)/shard_map/ppermute | solution.py:38
  56.8 2.3 %collective-permute-start.19 = (bf16[224,128]{1,0:T(8,128)(2,1)S(1)}, bf16[224,128]{1,0:T(8,128)(2,1)S(1)}, u32[]{:S(2)}, u32[]{:S(2)}) collective-permute-start(bf16[224,128]{1,0:T(8,128)(2,1)S(1)} %get-tuple-element.121), channel_id=1, source_target_pairs={{0,6},{1,7},{2,0},{3,1},{4,2},{5,3},{6,4},{7,5},{8,14},{9,15},{10,... | collective-permute-start | bytes 172040 | tf_op jit(solution)/shard_map/ppermute | solution.py:38
  60.7 9.1 %collective-permute-start.20 = (f32[224,128]{1,0:T(8,128)S(1)}, f32[224,128]{1,0:T(8,128)S(1)}, u32[]{:S(2)}, u32[]{:S(2)}) collective-permute-start(f32[224,128]{1,0:T(8,128)S(1)} %add_add_fusion.4), channel_id=1, source_target_pairs={{0,32},{1,33},{2,34},{3,35},{4,36},{5,37},{6,38},{7,39},{8,40},{9,... | collective-permute-start | bytes 344072 | tf_op jit(solution)/shard_map/ppermute | solution.py:38
  69.7 2.9 %collective-permute-start.21 = (f32[224,128]{1,0:T(8,128)S(1)}, f32[224,128]{1,0:T(8,128)S(1)}, u32[]{:S(2)}, u32[]{:S(2)}) collective-permute-start(f32[224,128]{1,0:T(8,128)S(1)} %add_add_fusion.4), channel_id=1, source_target_pairs={{0,16},{1,17},{2,18},{3,19},{4,20},{5,21},{6,22},{7,23},{8,24},{9,... | collective-permute-start | bytes 344072 | tf_op jit(solution)/shard_map/ppermute | solution.py:38
  72.6 2.3 %collective-permute-done.21 = f32[224,128]{1,0:T(8,128)S(1)} collective-permute-done((f32[224,128]{1,0:T(8,128)S(1)}, f32[224,128]{1,0:T(8,128)S(1)}, u32[]{:S(2)}, u32[]{:S(2)}) %collective-permute-start.21) | collective-permute-done | bytes 114720 | tf_op jit(solution)/shard_map/ppermute | solution.py:38
  74.9 2.3 %collective-permute-done.22 = f32[224,128]{1,0:T(8,128)S(1)} collective-permute-done((f32[224,128]{1,0:T(8,128)S(1)}, f32[224,128]{1,0:T(8,128)S(1)}, u32[]{:S(2)}, u32[]{:S(2)}) %collective-permute-start.22) | collective-permute-done | bytes 114720 | tf_op jit(solution)/shard_map/ppermute | solution.py:38
  77.2 3.1 %collective-permute-start.23 = (f32[224,128]{1,0:T(8,128)S(1)}, f32[224,128]{1,0:T(8,128)S(1)}, u32[]{:S(2)}, u32[]{:S(2)}) collective-permute-start(f32[224,128]{1,0:T(8,128)S(1)} %add_add_fusion.3), channel_id=1, source_target_pairs={{0,128},{1,129},{2,130},{3,131},{4,132},{5,133},{6,134},{7,135},{8... | collective-permute-start | bytes 344072 | tf_op jit(solution)/shard_map/ppermute | solution.py:38
  80.4 3.3 %collective-permute-start.25 = (f32[224,128]{1,0:T(8,128)S(1)}, f32[224,128]{1,0:T(8,128)S(1)}, u32[]{:S(2)}, u32[]{:S(2)}) collective-permute-start(f32[224,128]{1,0:T(8,128)S(1)} %add_add_fusion.3), channel_id=1, source_target_pairs={{0,192},{1,193},{2,194},{3,195},{4,196},{5,197},{6,198},{7,199},{8... | collective-permute-start | bytes 344072 | tf_op jit(solution)/shard_map/ppermute | solution.py:38
  90.8 6.3 %collective-permute-start.26 = (f32[224,128]{1,0:T(8,128)S(1)}, f32[224,128]{1,0:T(8,128)S(1)}, u32[]{:S(2)}, u32[]{:S(2)}) collective-permute-start(f32[224,128]{1,0:T(8,128)S(1)} %add_add_fusion.2), channel_id=1, source_target_pairs={{0,1},{1,0},{2,3},{3,2},{4,5},{5,4},{6,7},{7,6},{8,9},{9,8},{10,11... | collective-permute-start | bytes 344072 | tf_op jit(solution)/shard_map/ppermute | solution.py:38
  97.2 2.1 %collective-permute-done.26 = f32[224,128]{1,0:T(8,128)S(1)} collective-permute-done((f32[224,128]{1,0:T(8,128)S(1)}, f32[224,128]{1,0:T(8,128)S(1)}, u32[]{:S(2)}, u32[]{:S(2)}) %collective-permute-start.26) | collective-permute-done | bytes 114720 | tf_op jit(solution)/shard_map/ppermute | solution.py:38
  99.5 3.0 %collective-permute-start.28 = (f32[224,128]{1,0:T(8,128)S(1)}, f32[224,128]{1,0:T(8,128)S(1)}, u32[]{:S(2)}, u32[]{:S(2)}) collective-permute-start(f32[224,128]{1,0:T(8,128)S(1)} %add.83.own), channel_id=1, source_target_pairs={{0,4},{1,5},{2,6},{3,7},{4,0},{5,1},{6,2},{7,3},{8,12},{9,13},{10,... | collective-permute-start | bytes 344072 | tf_op jit(solution)/shard_map/ppermute | solution.py:38
  103.1 6.4 %collective-permute-start.11 = (bf16[128,128]{1,0:T(8,128)(2,1)S(1)}, bf16[128,128]{1,0:T(8,128)(2,1)S(1)}, u32[]{:S(2)}, u32[]{:S(2)}) collective-permute-start(bf16[128,128]{1,0:T(8,128)(2,1)S(1)} %fusion), channel_id=1, source_target_pairs={{0,1},{1,0},{2,3},{3,2},{4,5},{5,4},{6,7},{7,6},{8,9},{9,8},{10,11... | collective-permute-start | bytes 98312 | tf_op jit(solution)/shard_map/ppermute | solution.py:38
  109.5 7.1 %collective-permute-start.30 = (f32[4,224,128]{2,1,0:T(8,128)S(1)}, f32[4,224,128]{2,1,0:T(8,128)S(1)}, u32[]{:S(2)}, u32[]{:S(2)}) collective-permute-start(f32[4,224,128]{2,1,0:T(8,128)S(1)} %shard_map.172.half), channel_id=1, source_target_pairs={{0,8},{1,9},{2,10},{3,11},{4,12},{5,13},{6,14},{7,15},{8,0},{9,1},... | collective-permute-start | bytes 1376264 | tf_op jit(solution)/shard_map/ppermute | solution.py:38
  (92 shorter events, 31.0 us)
Async XLA Ops:
  4.3 9.9 %collective-permute-start = (bf16[96,256]{1,0:T(8,128)(2,1)S(1)}, bf16[96,256]{1,0:T(8,128)(2,1)S(1)}, u32[]{:S(2)}, u32[]{:S(2)}) collective-permute-start(bf16[96,256]{1,0:T(8,128)(2,1)S(1)} %get-tuple-element.69), channel_id=1, source_target_pairs={{0,8},{8,16},{16,24},{24,32},{32,40},{40,48},{48,56},{56,64},{64,7... | collective-permute-start | bytes 147464 | tf_op jit(solution)/shard_map/ppermute | solution.py:44
  8.8 5.4 %collective-permute-start.1 = (bf16[64,256]{1,0:T(8,128)(2,1)S(1)}, bf16[64,256]{1,0:T(8,128)(2,1)S(1)}, u32[]{:S(2)}, u32[]{:S(2)}) collective-permute-start(bf16[64,256]{1,0:T(8,128)(2,1)S(1)} %get-tuple-element.70), channel_id=1, source_target_pairs={{8,0},{16,8},{24,16},{32,24},{40,32},{48,40},{56,48},{64,56},{72,6... | collective-permute-start | bytes 98312 | tf_op jit(solution)/shard_map/ppermute | solution.py:44
  17.7 5.6 %collective-permute-start.2 = (bf16[64,256]{1,0:T(8,128)(2,1)S(1)}, bf16[64,256]{1,0:T(8,128)(2,1)S(1)}, u32[]{:S(2)}, u32[]{:S(2)}) collective-permute-start(bf16[64,256]{1,0:T(8,128)(2,1)S(1)} %get-tuple-element.74), channel_id=1, source_target_pairs={{0,8},{8,16},{16,24},{24,32},{32,40},{40,48},{48,56},{56,64},{64,7... | collective-permute-start | bytes 98312 | tf_op jit(solution)/shard_map/ppermute | solution.py:44
  21.4 5.2 %collective-permute-start.3 = (bf16[64,256]{1,0:T(8,128)(2,1)S(1)}, bf16[64,256]{1,0:T(8,128)(2,1)S(1)}, u32[]{:S(2)}, u32[]{:S(2)}) collective-permute-start(bf16[64,256]{1,0:T(8,128)(2,1)S(1)} %get-tuple-element.75), channel_id=1, source_target_pairs={{8,0},{16,8},{24,16},{32,24},{40,32},{48,40},{56,48},{64,56},{72,6... | collective-permute-start | bytes 98312 | tf_op jit(solution)/shard_map/ppermute | solution.py:44
  35.0 5.2 %collective-permute-start.5 = (bf16[64,256]{1,0:T(8,128)(2,1)S(1)}, bf16[64,256]{1,0:T(8,128)(2,1)S(1)}, u32[]{:S(2)}, u32[]{:S(2)}) collective-permute-start(bf16[64,256]{1,0:T(8,128)(2,1)S(1)} %get-tuple-element.81), channel_id=1, source_target_pairs={{8,0},{16,8},{24,16},{32,24},{40,32},{48,40},{56,48},{64,56},{72,6... | collective-permute-start | bytes 98312 | tf_op jit(solution)/shard_map/ppermute | solution.py:44
  43.5 5.4 %collective-permute-start.6 = (bf16[64,256]{1,0:T(8,128)(2,1)S(1)}, bf16[64,256]{1,0:T(8,128)(2,1)S(1)}, u32[]{:S(2)}, u32[]{:S(2)}) collective-permute-start(bf16[64,256]{1,0:T(8,128)(2,1)S(1)} %get-tuple-element.88), channel_id=1, source_target_pairs={{0,8},{8,16},{16,24},{24,32},{32,40},{40,48},{48,56},{56,64},{64,7... | collective-permute-start | bytes 98312 | tf_op jit(solution)/shard_map/ppermute | solution.py:44
  53.4 5.7 %collective-permute-start.17 = (bf16[224,128]{1,0:T(8,128)(2,1)S(1)}, bf16[224,128]{1,0:T(8,128)(2,1)S(1)}, u32[]{:S(2)}, u32[]{:S(2)}) collective-permute-start(bf16[224,128]{1,0:T(8,128)(2,1)S(1)} %get-tuple-element.119), channel_id=1, source_target_pairs={{0,4},{1,5},{2,6},{3,7},{4,0},{5,1},{6,2},{7,3},{8,12},{9,13},{10,... | collective-permute-start | bytes 172040 | tf_op jit(solution)/shard_map/ppermute | solution.py:38
  60.7 11.9 %collective-permute-start.20 = (f32[224,128]{1,0:T(8,128)S(1)}, f32[224,128]{1,0:T(8,128)S(1)}, u32[]{:S(2)}, u32[]{:S(2)}) collective-permute-start(f32[224,128]{1,0:T(8,128)S(1)} %add_add_fusion.4), channel_id=1, source_target_pairs={{0,32},{1,33},{2,34},{3,35},{4,36},{5,37},{6,38},{7,39},{8,40},{9,... | collective-permute-start | bytes 344072 | tf_op jit(solution)/shard_map/ppermute | solution.py:38
  77.2 9.3 %collective-permute-start.23 = (f32[224,128]{1,0:T(8,128)S(1)}, f32[224,128]{1,0:T(8,128)S(1)}, u32[]{:S(2)}, u32[]{:S(2)}) collective-permute-start(f32[224,128]{1,0:T(8,128)S(1)} %add_add_fusion.3), channel_id=1, source_target_pairs={{0,128},{1,129},{2,130},{3,131},{4,132},{5,133},{6,134},{7,135},{8... | collective-permute-start | bytes 344072 | tf_op jit(solution)/shard_map/ppermute | solution.py:38
  80.4 7.5 %collective-permute-start.24 = (f32[224,128]{1,0:T(8,128)S(1)}, f32[224,128]{1,0:T(8,128)S(1)}, u32[]{:S(2)}, u32[]{:S(2)}) collective-permute-start(f32[224,128]{1,0:T(8,128)S(1)} %add_add_fusion.3), channel_id=1, source_target_pairs={{0,64},{1,65},{2,66},{3,67},{4,68},{5,69},{6,70},{7,71},{8,72},{9,... | collective-permute-start | bytes 344072 | tf_op jit(solution)/shard_map/ppermute | solution.py:38
  80.4 8.3 %collective-permute-start.25 = (f32[224,128]{1,0:T(8,128)S(1)}, f32[224,128]{1,0:T(8,128)S(1)}, u32[]{:S(2)}, u32[]{:S(2)}) collective-permute-start(f32[224,128]{1,0:T(8,128)S(1)} %add_add_fusion.3), channel_id=1, source_target_pairs={{0,192},{1,193},{2,194},{3,195},{4,196},{5,197},{6,198},{7,199},{8... | collective-permute-start | bytes 344072 | tf_op jit(solution)/shard_map/ppermute | solution.py:38
  83.6 6.3 %collective-permute-start.12 = (bf16[2,128,128]{2,1,0:T(8,128)(2,1)S(1)}, bf16[2,128,128]{2,1,0:T(8,128)(2,1)S(1)}, u32[]{:S(2)}, u32[]{:S(2)}) collective-permute-start(bf16[2,128,128]{2,1,0:T(8,128)(2,1)S(1)} %get-tuple-element.95.two), channel_id=1, source_target_pairs={{0,4},{1,5},{2,6},{3,7},{4,0},{5,1},{6,2},{7,3},{8,12},{9,13},{10,... | collective-permute-start | bytes 196616 | tf_op jit(solution)/shard_map/ppermute | solution.py:38
  85.2 5.6 %collective-permute-start.13 = (bf16[2,128,128]{2,1,0:T(8,128)(2,1)S(1)}, bf16[2,128,128]{2,1,0:T(8,128)(2,1)S(1)}, u32[]{:S(2)}, u32[]{:S(2)}) collective-permute-start(bf16[2,128,128]{2,1,0:T(8,128)(2,1)S(1)} %get-tuple-element.94.one), channel_id=1, source_target_pairs={{0,2},{1,3},{2,4},{3,5},{4,6},{5,7},{6,0},{7,1},{8,10},{9,11},{10,... | collective-permute-start | bytes 196616 | tf_op jit(solution)/shard_map/ppermute | solution.py:38
  86.6 10.5 %collective-permute-start.14 = (bf16[2,128,128]{2,1,0:T(8,128)(2,1)S(1)}, bf16[2,128,128]{2,1,0:T(8,128)(2,1)S(1)}, u32[]{:S(2)}, u32[]{:S(2)}) collective-permute-start(bf16[2,128,128]{2,1,0:T(8,128)(2,1)S(1)} %get-tuple-element.96.three), channel_id=1, source_target_pairs={{0,6},{1,7},{2,0},{3,1},{4,2},{5,3},{6,4},{7,5},{8,14},{9,15},{10,... | collective-permute-start | bytes 196616 | tf_op jit(solution)/shard_map/ppermute | solution.py:38
  87.9 11.7 %collective-permute-start.10 = (bf16[2,128,128]{2,1,0:T(8,128)(2,1)S(1)}, bf16[2,128,128]{2,1,0:T(8,128)(2,1)S(1)}, u32[]{:S(2)}, u32[]{:S(2)}) collective-permute-start(bf16[2,128,128]{2,1,0:T(8,128)(2,1)S(1)} %get-tuple-element.106.three), channel_id=1, source_target_pairs={{0,6},{1,7},{2,0},{3,1},{4,2},{5,3},{6,4},{7,5},{8,14},{9,15},{10,... | collective-permute-start | bytes 196616 | tf_op jit(solution)/shard_map/ppermute | solution.py:38
  88.7 13.8 %collective-permute-start.8 = (bf16[2,128,128]{2,1,0:T(8,128)(2,1)S(1)}, bf16[2,128,128]{2,1,0:T(8,128)(2,1)S(1)}, u32[]{:S(2)}, u32[]{:S(2)}) collective-permute-start(bf16[2,128,128]{2,1,0:T(8,128)(2,1)S(1)} %get-tuple-element.105.two), channel_id=1, source_target_pairs={{0,4},{1,5},{2,6},{3,7},{4,0},{5,1},{6,2},{7,3},{8,12},{9,13},{10,... | collective-permute-start | bytes 196616 | tf_op jit(solution)/shard_map/ppermute | solution.py:38
  89.9 13.1 %collective-permute-start.9 = (bf16[2,128,128]{2,1,0:T(8,128)(2,1)S(1)}, bf16[2,128,128]{2,1,0:T(8,128)(2,1)S(1)}, u32[]{:S(2)}, u32[]{:S(2)}) collective-permute-start(bf16[2,128,128]{2,1,0:T(8,128)(2,1)S(1)} %get-tuple-element.104.one), channel_id=1, source_target_pairs={{0,2},{1,3},{2,4},{3,5},{4,6},{5,7},{6,0},{7,1},{8,10},{9,11},{10,... | collective-permute-start | bytes 196616 | tf_op jit(solution)/shard_map/ppermute | solution.py:38
  90.8 8.5 %collective-permute-start.26 = (f32[224,128]{1,0:T(8,128)S(1)}, f32[224,128]{1,0:T(8,128)S(1)}, u32[]{:S(2)}, u32[]{:S(2)}) collective-permute-start(f32[224,128]{1,0:T(8,128)S(1)} %add_add_fusion.2), channel_id=1, source_target_pairs={{0,1},{1,0},{2,3},{3,2},{4,5},{5,4},{6,7},{7,6},{8,9},{9,8},{10,11... | collective-permute-start | bytes 344072 | tf_op jit(solution)/shard_map/ppermute | solution.py:38
  97.1 19.5 %collective-permute-start.15 = (bf16[128,128]{1,0:T(8,128)(2,1)S(1)}, bf16[128,128]{1,0:T(8,128)(2,1)S(1)}, u32[]{:S(2)}, u32[]{:S(2)}) collective-permute-start(bf16[128,128]{1,0:T(8,128)(2,1)S(1)} %fusion.1), channel_id=1, source_target_pairs={{0,1},{1,0},{2,3},{3,2},{4,5},{5,4},{6,7},{7,6},{8,9},{9,8},{10,11... | collective-permute-start | bytes 98312 | tf_op jit(solution)/shard_map/ppermute | solution.py:38
  99.3 10.1 %collective-permute-start.27 = (f32[224,128]{1,0:T(8,128)S(1)}, f32[224,128]{1,0:T(8,128)S(1)}, u32[]{:S(2)}, u32[]{:S(2)}) collective-permute-start(f32[224,128]{1,0:T(8,128)S(1)} %add.83.own), channel_id=1, source_target_pairs={{0,2},{1,3},{2,4},{3,5},{4,6},{5,7},{6,0},{7,1},{8,10},{9,11},{10,... | collective-permute-start | bytes 344072 | tf_op jit(solution)/shard_map/ppermute | solution.py:38
  99.5 9.9 %collective-permute-start.28 = (f32[224,128]{1,0:T(8,128)S(1)}, f32[224,128]{1,0:T(8,128)S(1)}, u32[]{:S(2)}, u32[]{:S(2)}) collective-permute-start(f32[224,128]{1,0:T(8,128)S(1)} %add.83.own), channel_id=1, source_target_pairs={{0,4},{1,5},{2,6},{3,7},{4,0},{5,1},{6,2},{7,3},{8,12},{9,13},{10,... | collective-permute-start | bytes 344072 | tf_op jit(solution)/shard_map/ppermute | solution.py:38
  102.5 7.0 %collective-permute-start.29 = (f32[224,128]{1,0:T(8,128)S(1)}, f32[224,128]{1,0:T(8,128)S(1)}, u32[]{:S(2)}, u32[]{:S(2)}) collective-permute-start(f32[224,128]{1,0:T(8,128)S(1)} %add.83.own), channel_id=1, source_target_pairs={{0,6},{1,7},{2,0},{3,1},{4,2},{5,3},{6,4},{7,5},{8,14},{9,15},{10,... | collective-permute-start | bytes 344072 | tf_op jit(solution)/shard_map/ppermute | solution.py:38
  103.1 13.6 %collective-permute-start.11 = (bf16[128,128]{1,0:T(8,128)(2,1)S(1)}, bf16[128,128]{1,0:T(8,128)(2,1)S(1)}, u32[]{:S(2)}, u32[]{:S(2)}) collective-permute-start(bf16[128,128]{1,0:T(8,128)(2,1)S(1)} %fusion), channel_id=1, source_target_pairs={{0,1},{1,0},{2,3},{3,2},{4,5},{5,4},{6,7},{7,6},{8,9},{9,8},{10,11... | collective-permute-start | bytes 98312 | tf_op jit(solution)/shard_map/ppermute | solution.py:38
  109.5 8.8 %collective-permute-start.30 = (f32[4,224,128]{2,1,0:T(8,128)S(1)}, f32[4,224,128]{2,1,0:T(8,128)S(1)}, u32[]{:S(2)}, u32[]{:S(2)}) collective-permute-start(f32[4,224,128]{2,1,0:T(8,128)S(1)} %shard_map.172.half), channel_id=1, source_target_pairs={{0,8},{1,9},{2,10},{3,11},{4,12},{5,13},{6,14},{7,15},{8,0},{9,1},... | collective-permute-start | bytes 1376264 | tf_op jit(solution)/shard_map/ppermute | solution.py:38
  (22 other events, 87.4 us)

commit v2 on v1

v2 whole, which is shorter than its diff:
```python
from functools import partial

import jax
import jax.numpy as jnp
from jax import lax
from jax.experimental import pallas as pl
from jax.experimental.pallas import tpu as pltpu
from jax.sharding import PartitionSpec as P

HALO = 64
KWIN = 128
QBLK = 32
HEADS = 4
EPSILON = 1e-05
F32 = jnp.float32
BF16 = jnp.bfloat16
DIMS = (4, 4, 2, 4, 2)
WORLD = ("seq", "samp")


def moves(part, step):
    pairs = []
    for source in range(256):
        place, rest = [], source
        for size in reversed(DIMS):
            place.append(rest % size)
            rest //= size
        place.reverse()
        place[part] = (place[part] + step) % DIMS[part]
        target = 0
        for size, value in zip(DIMS, place):
            target = target * size + value
        pairs.append((source, target))
    return pairs


def hop(value, part, step):
    return lax.ppermute(value, WORLD, moves(part, step))


def swapped(near, far):
    length = lax.axis_size("seq")
    chip = [(i, i ^ 1) for i in range(length)]
    across = [(i, i - 1 + 2 * (i % 2)) for i in range(length)]
    across = [(i, j) for i, j in across if 0 <= j < length]
    far = lax.ppermute(far, "seq", across)
    return lax.ppermute(near, "seq", chip), far


def pair_up(own, got):
    if len(got) == 1:
        return own + got[0]
    return (own + got[1]) + (got[0] + got[2])


def everyone(value, part):
    got = [hop(value, part, k).astype(F32) for k in range(1, DIMS[part])]
    return pair_up(value.astype(F32), got).astype(BF16)


def run(body, outs, args, smem=(), hbm=(), scratch=(), flops=10**8, nbytes=10**6):
    spaces = [pltpu.VMEM] * len(args)
    for i in smem:
        spaces[i] = pltpu.SMEM
    for i in hbm:
        spaces[i] = pltpu.HBM
    specs = [pl.BlockSpec(memory_space=space) for space in spaces]
    return pl.pallas_call(
        body,
        out_shape=[jax.ShapeDtypeStruct(s, d) for s, d in outs],
        in_specs=specs,
        out_specs=[pl.BlockSpec(memory_space=pltpu.VMEM) for _ in outs],
        scratch_shapes=list(scratch),
        compiler_params=pltpu.CompilerParams(vmem_limit_bytes=24 * 2**20),
        cost_estimate=pl.CostEstimate(flops=flops, bytes_accessed=nbytes, transcendentals=0),
    )(*args)


def nn(a, b):
    return jnp.dot(a, b, preferred_element_type=F32)


def nt(a, b):
    return lax.dot_general(a, b, (((1,), (1,)), ((), ())), preferred_element_type=F32)


def tn(a, b):
    return lax.dot_general(a, b, (((0,), (0,)), ((), ())), preferred_element_type=F32)


def stats(state):
    centred = state - jnp.mean(state, -1, keepdims=True)
    scale = lax.rsqrt(jnp.mean(centred * centred, -1, keepdims=True) + EPSILON)
    return centred * scale, scale


def sigmoid(value):
    return 1.0 / (1.0 + jnp.exp(-value))


def head_mask(rows):
    row = lax.broadcasted_iota(jnp.int32, (rows, 128), 0) // QBLK
    lane = lax.broadcasted_iota(jnp.int32, (rows, 128), 1) // 32
    return row == lane


def stacked(block, mask):
    return jnp.where(mask, jnp.concatenate([block.astype(F32)] * HEADS, 0), 0.0).astype(BF16)


def picked(wide, mask):
    wide = jnp.where(mask, wide, 0.0)
    return (wide[0:32] + wide[32:64]) + (wide[64:96] + wide[96:128])


def odd_core():
    return lax.rem(lax.axis_index("seq"), 2) == 1


def project_into(state, gain, weight, normed_ref, q_ref, kv_ref, gate_ref, near_ref, far_ref):
    unit, _ = stats(state)
    normed = (unit * gain).astype(BF16)
    normed_ref[...] = normed
    projected = nn(normed, weight)
    q_ref[...] = projected[:, 0:128].astype(BF16)
    kv = projected[:, 128:384]
    kv_ref[...] = kv.astype(BF16)
    gate_ref[...] = sigmoid(projected[:, 384:512])
    rows = kv.shape[0]
    head, tail = kv[0:HALO], kv[rows - HALO : rows]
    near_ref[0:HALO, :] = jnp.where(odd_core(), head, tail).astype(BF16)
    far_ref[0:HALO, :] = jnp.where(odd_core(), tail, head).astype(BF16)


def from_before(near, far):
    return jnp.where(odd_core(), near.astype(F32), far.astype(F32))


def from_after(near, far):
    return jnp.where(odd_core(), far.astype(F32), near.astype(F32))


def count_rows(counts):
    size = counts.shape[1]
    row = lax.broadcasted_iota(jnp.int32, (size, size), 0)
    lane = lax.broadcasted_iota(jnp.int32, (size, size), 1)
    column = jnp.sum(jnp.where(row == lane, counts.astype(F32), 0.0), -1, keepdims=True)
    return jnp.broadcast_to(column, (size, 128))


def first_kernel(
    atoms_far,
    gain_far,
    weight_far,
    grad_far,
    counts_far,
    normed,
    q,
    kv,
    gate,
    near,
    far,
    atoms,
    gain,
    weight,
    grad,
    counts,
    sems,
):
    pairs = (
        (atoms_far, atoms),
        (weight_far, weight),
        (gain_far, gain),
        (grad_far, grad),
        (counts_far, counts),
    )
    copies = [pltpu.make_async_copy(a, b, sems.at[i]) for i, (a, b) in enumerate(pairs)]
    for copy in copies:
        copy.start()
    for copy in copies:
        copy.wait()
    project_into(atoms[...].astype(F32), gain[0:1, :], weight[0], normed, q, kv, gate, near, far)
    last = lax.broadcasted_iota(jnp.int32, (16, 384), 0) == 15
    row = jnp.where(last, grad[16:32, :].astype(F32), 0.0).astype(BF16)
    many = jnp.where(last[:, :128], count_rows(counts[...])[16:32], 0.0).astype(BF16)
    for ref in (near, far):
        ref[HALO : HALO + 16, :] = row[:, 0:256]
        ref[HALO + 16 : HALO + 32, 0:128] = row[:, 256:384]
        ref[HALO + 16 : HALO + 32, 128:256] = many


def bias_kernel(layer, weight, pair_far, *rest):
    bias, pair, sems = rest[-3:]
    blocks = pair.shape[0]

    def fetch(j):
        return pltpu.make_async_copy(pair_far.at[j], pair.at[j], sems.at[j])

    for j in range(blocks):
        fetch(j).start()

    def block(j, carry):
        fetch(j).wait()
        totals = [None] * HEADS
        for c in range(16):
            part = pair[j, c * 32 : (c + 1) * 32, :].astype(F32)
            for h in range(HEADS):
                term = part * weight[layer, h, c]
                totals[h] = term if c == 0 else totals[h] + term
        for h in range(HEADS):
            bias[j, h * 32 : (h + 1) * 32, :] = totals[h]
        return carry

    lax.fori_loop(0, blocks, block, 0)


def load_window(kv, near, far, keys, values):
    rows = kv.shape[0]
    for ref, at in ((keys, 0), (values, 128)):
        beside, across = near[0:HALO, at : at + 128], far[0:HALO, at : at + 128]
        ref[0:HALO, :] = from_before(beside, across)
        ref[HALO : HALO + rows, :] = kv[:, at : at + 128].astype(F32)
        ref[HALO + rows : HALO + rows + HALO, :] = from_after(beside, across)


def windows(shift, q, keys, values):
    mask = head_mask(128)
    spans = [pl.ds(j * QBLK + shift[j] + HALO, KWIN) for j in range(q.shape[0] // QBLK)]
    wide = [stacked(q[j * QBLK : (j + 1) * QBLK, :], mask) for j in range(len(spans))]
    key = [keys[span, :].astype(BF16) for span in spans]
    value = [values[span, :].astype(BF16) for span in spans]
    return spans, wide, key, value


def attention_forward(shift, found, bias, att, rows, atom_total):
    _, wide, key, value = found
    count = len(wide)
    mask = head_mask(128)
    first = lax.axis_index("seq") * rows
    lane = lax.broadcasted_iota(jnp.int32, (1, KWIN), 1)
    scores = [nt(wide[j], key[j]) for j in range(count)]
    chances = []
    for j in range(count):
        place = first + (j * QBLK + shift[j]) + lane
        inside = jnp.logical_and(place >= 0, place < atom_total)
        weights = jnp.where(inside, jnp.exp(scores[j] * (32.0**-0.5) + bias[j]), 0.0)
        chances.append(weights * (1.0 / jnp.sum(weights, -1, keepdims=True)))
    out = [nn(chances[j].astype(BF16), value[j]) for j in range(count)]
    for j in range(count):
        att[j * QBLK : (j + 1) * QBLK, :] = picked(out[j], mask).astype(BF16)
    return chances


def attention_backward(found, chances, grad_att, grad_q, grad_keys, grad_values, score_grad):
    spans, wide, key, value = found
    count = len(wide)
    mask = head_mask(128)
    out = [stacked(grad_att[j * QBLK : (j + 1) * QBLK, :], mask) for j in range(count)]
    rising = [nt(out[j], value[j]) for j in range(count)]
    value_back = [tn(chances[j].astype(BF16), out[j]) for j in range(count)]
    scaled = []
    for j in range(count):
        term = chances[j] * rising[j].astype(BF16).astype(F32)
        grad_score = term - chances[j] * jnp.sum(term, -1, keepdims=True)
        score_grad[j] = grad_score.astype(BF16)
        scaled.append((grad_score * (32.0**-0.5)).astype(BF16))
    query_back = [nn(scaled[j], key[j]) for j in range(count)]
    key_back = [tn(scaled[j], wide[j]) for j in range(count)]
    for j in range(count):
        grad_q[j * QBLK : (j + 1) * QBLK, :] = picked(query_back[j], mask).astype(BF16)
    grad_keys[...] = jnp.zeros_like(grad_keys)
    grad_values[...] = jnp.zeros_like(grad_values)
    for j in range(count):
        grad_keys[spans[j], :] += key_back[j].astype(BF16).astype(F32)
        grad_values[spans[j], :] += value_back[j].astype(BF16).astype(F32)


def share_scores(score_grad, own, one, two, three):
    y = lax.axis_index("samp") // 2
    for k, ref in enumerate((own, one, two, three)):
        ref[...] = score_grad[pl.ds(lax.rem(y + k, 4) * 2, 2)]


def forward_kernel(
    atom_total,
    shift,
    q,
    kv,
    near,
    far,
    bias,
    gate,
    atoms,
    weight_out,
    gain,
    weight_in,
    state,
    chances,
    att,
    normed,
    q_next,
    kv_next,
    gate_next,
    near_next,
    far_next,
    keys,
    values,
):
    load_window(kv, near, far, keys, values)
    found = windows(shift, q, keys, values)
    kept = attention_forward(shift, found, bias, att, q.shape[0], atom_total)
    for j, chance in enumerate(kept):
        chances[j] = chance
    after = atoms[...].astype(F32) + gate[...] * nn(att[...], weight_out[0])
    state[...] = after
    project_into(
        after, gain[1:2, :], weight_in[1], normed, q_next, kv_next, gate_next, near_next, far_next
    )


def layer_back(
    grad_state, gate, att, weight_out, layer, grad_gate, grad_update, grad_att, update=None
):
    if update is None:
        update = nn(att[...], weight_out[layer])
    gates = gate[...]
    grad_gate[...] = (grad_state * update * gates * (1.0 - gates)).astype(BF16)
    change = (grad_state * gates).astype(BF16)
    grad_update[...] = change
    grad_att[...] = nt(change, weight_out[layer]).astype(BF16)


def send_halo(grad_keys, grad_values, center, near, far):
    rows = center.shape[0]
    odd = odd_core()
    for ref, at in ((grad_keys, 0), (grad_values, 128)):
        before, after = ref[0:HALO, :], ref[HALO + rows : HALO + rows + HALO, :]
        near[:, at : at + 128] = jnp.where(odd, before, after).astype(BF16)
        far[:, at : at + 128] = jnp.where(odd, after, before).astype(BF16)
        center[:, at : at + 128] = ref[HALO : HALO + rows, :]


def middle_kernel(
    atom_total,
    shift,
    q,
    kv,
    near,
    far,
    bias,
    gate,
    state,
    weight_out,
    weight_token,
    grad,
    counts,
    atom_token,
    near_first,
    far_first,
    att,
    grad_update,
    narrow_state,
    grad_hidden,
    grad_state,
    grad_gate,
    grad_q,
    center,
    grad_near,
    grad_far,
    score_own,
    score_one,
    score_two,
    score_three,
    keys,
    values,
    grad_att,
    grad_keys,
    grad_values,
    score_grad,
):
    load_window(kv, near, far, keys, values)
    found = windows(shift, q, keys, values)
    chances = attention_forward(shift, found, bias, att, q.shape[0], atom_total)
    update = nn(att[...], weight_out[1])
    after = (state[...] + gate[...] * update).astype(BF16)
    narrow_state[...] = after
    tokens = grad.shape[0]
    atoms = q.shape[0]
    place = atom_token[...] - lax.axis_index("seq") * tokens
    place = jnp.where(place < 0, tokens + 15, place)
    chosen = lax.broadcasted_iota(jnp.int32, (tokens + 16, atoms), 0) == place
    chosen = jnp.where(chosen, 1.0, 0.0).astype(BF16)
    own = jnp.concatenate([grad[...], count_rows(counts[...]).astype(BF16)], 1)
    before = from_before(near_first[HALO : HALO + 32, :], far_first[HALO : HALO + 32, :])
    before = jnp.concatenate([before[0:16], before[16:32]], 1).astype(BF16)
    taken = tn(chosen, jnp.concatenate([own, before], 0))
    many = taken[:, 384:512]
    cotangent = taken[:, 0:384] / jnp.concatenate([many] * 3, 1)
    hidden = nn(after, weight_token[...])
    open_ = sigmoid(hidden)
    back = (cotangent * (open_ * (1.0 + hidden * (1.0 - open_)))).astype(BF16)
    grad_hidden[...] = back
    rising = nt(back, weight_token[...]).astype(BF16).astype(F32)
    grad_state[...] = rising
    layer_back(rising, gate, att, weight_out, 1, grad_gate, grad_update, grad_att, update)
    attention_backward(found, chances, grad_att, grad_q, grad_keys, grad_values, score_grad)
    send_halo(grad_keys, grad_values, center, grad_near, grad_far)
    share_scores(score_grad, score_own, score_one, score_two, score_three)


def pair_weight_grad(pair, scores, out):
    left = [pair[block] for block, _ in scores]
    product = nt(jnp.concatenate(left, 1), jnp.concatenate([piece for _, piece in scores], 1))
    row = lax.rem(lax.broadcasted_iota(jnp.int32, product.shape, 0), QBLK)
    lane = lax.rem(lax.broadcasted_iota(jnp.int32, product.shape, 1), QBLK)
    product = jnp.where(row == lane, product, 0.0)
    for c in range(16):
        out[c : c + 1, :] = jnp.sum(product[c * 32 : (c + 1) * 32], 0, keepdims=True)


def middle_weights_kernel(
    pair, own, one, two, three, narrow_state, grad_hidden, att, grad_update, token, out, bias
):
    y = lax.axis_index("samp") // 2
    pair_weight_grad(
        pair,
        [
            (lax.rem(y + k, 4) * 2 + m, ref[m])
            for k, ref in enumerate((own, one, two, three))
            for m in range(2)
        ],
        bias,
    )
    product = tn(narrow_state[...], grad_hidden[...])
    for m in range(3):
        token[m * 128 : (m + 1) * 128, :] = product[:, m * 128 : (m + 1) * 128]
    out[...] = tn(att[...], grad_update[...])


def join_projected(grad_q, center, near, far, grad_gate, joined):
    rows = center.shape[0]
    joined[:, 0:128] = grad_q[...]
    joined[:, 384:512] = grad_gate[...]
    below, above = from_before(near[...], far[...]), from_after(near[...], far[...])
    joined[0:HALO, 128:384] = (center[0:HALO, :] + below).astype(BF16)
    joined[HALO : rows - HALO, 128:384] = center[HALO : rows - HALO, :].astype(BF16)
    joined[rows - HALO : rows, 128:384] = (center[rows - HALO : rows, :] + above).astype(BF16)


def norm_back(grad_normed, state, gain):
    unit, scale = stats(state)
    grad_gain = jnp.sum(grad_normed * unit, 0, keepdims=True)
    back = grad_normed * gain
    back = scale * (
        back - jnp.mean(back, -1, keepdims=True) - unit * jnp.mean(back * unit, -1, keepdims=True)
    )
    return back, grad_gain


def backward_kernel(
    shift,
    grad_q_later,
    center_later,
    near_later,
    far_later,
    grad_gate_later,
    state,
    gain,
    weight_in,
    grad_state_later,
    q,
    kv,
    near,
    far,
    gate,
    att,
    weight_out,
    chances,
    joined,
    grad_gain,
    grad_update,
    grad_state,
    grad_gate,
    grad_q,
    center,
    grad_near,
    grad_far,
    score_grad,
    keys,
    values,
    grad_att,
    grad_keys,
    grad_values,
):
    load_window(kv, near, far, keys, values)
    found = windows(shift, q, keys, values)
    join_projected(grad_q_later, center_later, near_later, far_later, grad_gate_later, joined)
    grad_normed = nt(joined[...], weight_in[1]).astype(BF16).astype(F32)
    back, gained = norm_back(grad_normed, state[...], gain[1:2, :])
    grad_gain[...] = gained
    rising = grad_state_later[...] + back
    grad_state[...] = rising
    layer_back(rising, gate, att, weight_out, 0, grad_gate, grad_update, grad_att)
    kept = [chances[j] for j in range(chances.shape[0])]
    attention_backward(found, kept, grad_att, grad_q, grad_keys, grad_values, score_grad)
    send_halo(grad_keys, grad_values, center, grad_near, grad_far)


EARLY = 144
EXTRA = 160
SPAN = 224


def backward_weights_kernel(
    pair,
    scores,
    normed,
    joined,
    att,
    grad_update,
    token,
    out_later,
    bias_later,
    gain_later,
    keep,
    send,
    whole,
):
    def put(row, value):
        whole[row // EARLY, row % EARLY : row % EARLY + 16, :] = value

    for r in range(0, 384, 16):
        put(r, token[r : r + 16, :])
    for r in range(0, 128, 16):
        put(384 + r, out_later[r : r + 16, :])
    inner = tn(normed[...], joined[...])
    for m in range(4):
        for r in range(0, 128, 16):
            put(512 + m * 128 + r, inner[r : r + 16, m * 128 : (m + 1) * 128])
    out = tn(att[...], grad_update[...])
    for r in range(0, 128, 16):
        put(1024 + r, out[r : r + 16, :])
    for m in range(2, 8):
        whole[m, EARLY:EXTRA, :] = jnp.zeros((16, 128), F32)
    pair_weight_grad(
        pair, [(j, scores[j]) for j in range(pair.shape[0])], whole.at[0, EARLY:EXTRA]
    )
    whole[1, EARLY:EXTRA, :] = bias_later[...]
    whole[3, EARLY : EARLY + 1, :] = gain_later[...]
    core = lax.rem(lax.axis_index("seq"), 2)
    keep[...] = whole[pl.ds(core * 4, 4)]
    send[...] = whole[pl.ds((1 - core) * 4, 4)]


def last_kernel(
    grad_q,
    center,
    near,
    far,
    grad_gate,
    atoms,
    gain,
    weight_in,
    grad_state,
    normed,
    keep_early,
    send_early,
    grad_atoms,
    keep,
    send,
    joined,
    late,
):
    join_projected(grad_q, center, near, far, grad_gate, joined)
    grad_normed = nt(joined[...], weight_in[0]).astype(BF16).astype(F32)
    product = tn(normed[...], joined[...])
    back, gained = norm_back(grad_normed, atoms[...].astype(F32), gain[0:1, :])
    grad_atoms[...] = (grad_state[...] + back).astype(BF16)
    for m in range(8):
        late[m, 0:16, :] = jnp.zeros((16, 128), F32)
        half = (m % 2) * 64
        late[m, 16:80, :] = product[half : half + 64, (m // 2) * 128 : (m // 2 + 1) * 128]
    late[2, 0:1, :] = gained
    core = lax.rem(lax.axis_index("seq"), 2)
    for ref, early, at in ((keep, keep_early, core), (send, send_early, 1 - core)):
        piece = late[pl.ds(at * 4, 4)]
        ref[:, 0:EARLY, :] = early[:, 0:EARLY, :].astype(ref.dtype)
        ref[:, EARLY:EXTRA, :] = (early[:, EARLY:EXTRA, :] + piece[:, 0:16]).astype(ref.dtype)
        ref[:, EXTRA:SPAN, :] = piece[:, 16:80].astype(ref.dtype)


def core_kernel(keep, got, scores, own, own_scores, one, two, three, whole):
    whole[...] = keep[...] + got[...].astype(F32)
    y = lax.axis_index("samp") // 2
    own[...] = whole[y]
    own_scores[...] = scores[pl.ds(y * 2, 2)]
    for k, ref in enumerate((one, two, three)):
        at = lax.rem(y + k + 1, 4)
        ref[0:SPAN, :] = whole[at].astype(BF16)
        for m in range(2):
            ref[SPAN + m * 128 : SPAN + (m + 1) * 128, :] = scores[at * 2 + m]


def far_kernel(
    own,
    own_scores,
    one,
    two,
    three,
    later,
    later_one,
    later_two,
    later_three,
    message,
    kept,
    both,
):
    got = [ref[...].astype(F32) for ref in (one, two, three)]
    message[0:SPAN, :] = pair_up(own[...], [v[0:SPAN] for v in got]).astype(BF16)
    for m in range(2):
        rows = slice(SPAN + m * 128, SPAN + (m + 1) * 128)
        both[m, 0] = pair_up(own_scores[m].astype(F32), [v[rows] for v in got])
        pieces = [ref[m].astype(F32) for ref in (later_one, later_two, later_three)]
        both[m, 1] = pair_up(later[m].astype(F32), pieces)
    side = lax.rem(lax.axis_index("samp"), 2)
    kept[...] = both[side]
    away = both[1 - side].astype(BF16)
    message[SPAN : SPAN + 128, :] = away[0]
    message[SPAN + 128 : SPAN + 256, :] = away[1]


def quarter_kernel(own, one, two, three, half):
    y = lax.axis_index("samp") // 2
    half[y] = own[...]
    for k, ref in enumerate((one, two, three)):
        half[lax.rem(y + 3 - k, 4)] = ref[...]


def finish_kernel(half, got, grad_gain, inner, out, bias, token):
    def finish(lower, upper):
        def chunk(m):
            return (lower if m < 4 else upper).at[m % 4]

        def rows(row):
            return chunk(row // EARLY)[row % EARLY : row % EARLY + 16, :].astype(F32)

        def take(ref, base, blocks):
            for m in range(blocks):
                for r in range(0, 128, 16):
                    ref[r : r + 16, m * 128 : (m + 1) * 128] = rows(base + m * 128 + r)

        take(token, 0, 3)
        take(out.at[1], 384, 1)
        take(inner.at[1], 512, 4)
        take(out.at[0], 1024, 1)
        for m in range(8):
            half_rows = (m % 2) * 64
            inner[0, half_rows : half_rows + 64, (m // 2) * 128 : (m // 2 + 1) * 128] = chunk(m)[
                EXTRA:SPAN, :
            ].astype(F32)
        for layer in range(2):
            grad_gain[layer : layer + 1, :] = chunk(2 + layer)[EARLY:EXTRA, :].astype(F32)[0:1]
            head = lax.broadcasted_iota(jnp.int32, (HEADS, 128), 0)
            lane = lax.broadcasted_iota(jnp.int32, (HEADS, 128), 1) // QBLK
            choose = jnp.where(head == lane, 1.0, 0.0).astype(BF16)
            bias[layer] = nt(choose, chunk(layer)[EARLY:EXTRA, :])

    odd = odd_core()

    @pl.when(jnp.logical_not(odd))
    def _():
        finish(half, got)

    @pl.when(odd)
    def _():
        finish(got, half)


def expand_kernel(weight, kept, got, pair):
    first = kept[0] + got[SPAN : SPAN + 128, :].astype(F32)
    later = kept[1] + got[SPAN + 128 : SPAN + 256, :].astype(F32)
    for c in range(16):
        value = None
        for layer, ref in enumerate((first, later)):
            for h in range(HEADS):
                term = ref[h * 32 : (h + 1) * 32, :] * weight[layer, h, c]
                value = term if value is None else value + term
        pair[c * 32 : (c + 1) * 32, :] = value.astype(BF16)


def body(
    atoms_in,
    pair_feats,
    window_shift,
    atom_token,
    token_counts,
    token_grad,
    norm_gain,
    weight_in,
    weight_out,
    weight_bias,
    weight_token,
):
    rows = atoms_in.shape[1]
    blocks = pair_feats.shape[0]
    atom_total = rows * lax.axis_size("seq")
    atoms = atoms_in[0]
    grad = token_grad[0]
    pair = pair_feats.reshape(blocks, 512, 128)
    counts = token_counts.reshape(1, -1)
    token_row = atom_token.reshape(1, -1)
    ext = rows + 2 * HALO
    window = [pltpu.VMEM((ext, 128), F32), pltpu.VMEM((ext, 128), F32)]
    square = ((blocks, 128, 128), F32)
    wide = ((rows, 128), BF16)
    full = ((rows, 128), F32)
    kv_shape = ((rows, 256), BF16)
    first_rim = ((HALO + 32, 256), BF16)
    rim = ((HALO, 256), BF16)
    score_piece = ((2, 128, 128), BF16)
    channel_weight = weight_bias.transpose(0, 2, 1)

    def pair_bias(layer, *after):
        (bias,) = run(
            partial(bias_kernel, layer),
            [square],
            (channel_weight, pair, *after),
            smem=(0,),
            hbm=range(1, 2 + len(after)),
            scratch=[
                pltpu.VMEM((blocks, 512, 128), BF16),
                pltpu.SemaphoreType.DMA((blocks,)),
            ],
        )
        return bias

    inputs = (atoms, norm_gain, weight_in, grad, counts)
    normed0, q0, kv0, gate0, *rims0 = run(
        first_kernel,
        [wide, wide, kv_shape, full, first_rim, first_rim],
        inputs,
        hbm=range(5),
        scratch=[pltpu.VMEM(v.shape, v.dtype) for v in inputs]
        + [pltpu.SemaphoreType.DMA((len(inputs),))],
    )
    rims0 = swapped(*rims0)
    bias0 = pair_bias(0)
    state1, chances0, att0, normed1, q1, kv1, gate1, *rims1 = run(
        partial(forward_kernel, atom_total),
        [full, square, wide, wide, wide, kv_shape, full, rim, rim],
        (window_shift, q0, kv0, *rims0, bias0, gate0, atoms, weight_out, norm_gain, weight_in),
        smem=(0,),
        scratch=window,
    )
    bias1 = pair_bias(1, att0)
    rims1 = swapped(*rims1)
    back_scratch = [
        pltpu.VMEM((rows, 128), BF16),
        pltpu.VMEM((ext, 128), F32),
        pltpu.VMEM((ext, 128), F32),
    ]
    (
        att1,
        grad_update1,
        narrow_state,
        grad_hidden,
        grad_state2,
        grad_gate1,
        grad_q1,
        center1,
        near1,
        far1,
        *scores1,
    ) = run(
        partial(middle_kernel, atom_total),
        [
            wide,
            wide,
            wide,
            ((rows, 384), BF16),
            full,
            wide,
            wide,
            ((rows, 256), F32),
            rim,
            rim,
            score_piece,
            score_piece,
            score_piece,
            score_piece,
        ],
        (
            window_shift,
            q1,
            kv1,
            *rims1,
            bias1,
            gate1,
            state1,
            weight_out,
            weight_token,
            grad,
            counts,
            token_row,
            *rims0,
        ),
        smem=(0,),
        scratch=window + back_scratch + [pltpu.VMEM((blocks, 128, 128), BF16)],
    )
    rims1 = swapped(near1, far1)
    got_one = hop(scores1[1], 3, 1)
    grad_token, grad_out1, grad_bias1 = run(
        middle_weights_kernel,
        [((384, 128), F32), ((128, 128), F32), ((16, 128), F32)],
        (pair, *scores1, narrow_state, grad_hidden, att1, grad_update1),
    )
    *rims1, got_one, grad_token = lax.optimization_barrier((*rims1, got_one, grad_token))
    (
        joined1,
        grad_gain1,
        grad_update0,
        grad_state1,
        grad_gate0,
        grad_q0,
        center0,
        near0,
        far0,
        scores0,
    ) = run(
        backward_kernel,
        [
            ((rows, 512), BF16),
            ((1, 128), F32),
            wide,
            full,
            wide,
            wide,
            ((rows, 256), F32),
            rim,
            rim,
            ((blocks, 128, 128), BF16),
        ],
        (
            window_shift,
            grad_q1,
            center1,
            *rims1,
            grad_gate1,
            state1,
            norm_gain,
            weight_in,
            grad_state2,
            q0,
            kv0,
            *rims0,
            gate0,
            att0,
            weight_out,
            chances0,
        ),
        smem=(0,),
        scratch=window + back_scratch,
    )
    last_rims = swapped(near0, far0)
    keep, send = run(
        backward_weights_kernel,
        [((4, EXTRA, 128), F32), ((4, EXTRA, 128), F32)],
        (
            pair,
            scores0,
            normed1,
            joined1,
            att0,
            grad_update0,
            grad_token,
            grad_out1,
            grad_bias1,
            grad_gain1,
        ),
        scratch=[pltpu.VMEM((8, EXTRA, 128), F32)],
    )
    got_two, got_three = hop(scores1[2], 3, 2), hop(scores1[3], 3, 3)
    *last_rims, got_two, got_three = lax.optimization_barrier((*last_rims, got_two, got_three))
    grad_atoms, keep, send = run(
        last_kernel,
        [wide, ((4, SPAN, 128), F32), ((4, SPAN, 128), BF16)],
        (
            grad_q0,
            center0,
            *last_rims,
            grad_gate0,
            atoms,
            norm_gain,
            weight_in,
            grad_state1,
            normed0,
            keep,
            send,
        ),
        scratch=[pltpu.VMEM((rows, 512), BF16), pltpu.VMEM((8, 80, 128), F32)],
    )
    message = ((SPAN + 256, 128), BF16)
    own, own_scores, *pieces = run(
        core_kernel,
        [((SPAN, 128), F32), score_piece, message, message, message],
        (keep, hop(send, 2, 1), scores0),
        scratch=[pltpu.VMEM((4, SPAN, 128), F32)],
    )
    pieces = [hop(v, 3, k + 1) for k, v in enumerate(pieces)]
    out, kept = run(
        far_kernel,
        [message, ((2, 128, 128), F32)],
        (own, own_scores, *pieces, scores1[0], got_one, got_two, got_three),
        scratch=[pltpu.VMEM((2, 2, 128, 128), F32)],
    )
    got = hop(out, 4, 1)
    total = (out[0:SPAN].astype(F32) + got[0:SPAN].astype(F32)).astype(BF16)
    total = everyone(total, 1)
    (pair_sum,) = run(expand_kernel, [((512, 128), BF16)], (channel_weight, kept, got), smem=(0,))
    total, pair_sum = lax.optimization_barrier((total, pair_sum))
    total = everyone(total, 0)
    (half,) = run(
        quarter_kernel,
        [((4, SPAN, 128), BF16)],
        (total, *[hop(total, 3, k) for k in range(1, 4)]),
    )
    grad_gain, grad_in, grad_out, grad_bias, grad_token = run(
        finish_kernel,
        [
            ((2, 128), F32),
            ((2, 128, 512), F32),
            ((2, 128, 128), F32),
            ((2, 4, 16), F32),
            ((128, 384), F32),
        ],
        (half, hop(half, 2, 1)),
    )
    return (
        grad_atoms[None],
        pair_sum.reshape(1, 16, 32, 128),
        grad_gain,
        grad_in,
        grad_out,
        grad_bias.transpose(0, 2, 1),
        grad_token,
    )


def solution(mesh):
    return jax.shard_map(
        body,
        mesh=mesh,
        in_specs=(
            P("samp", "seq", None),
            P("seq", None, None, None),
            P("seq"),
            P("seq"),
            P("seq"),
            P("samp", "seq", None),
            P(),
            P(),
            P(),
            P(),
            P(),
        ),
        out_specs=(
            P("samp", "seq", None),
            P(("seq", "samp"), None, None, None),
            P(),
            P(),
            P(),
            P(),
            P(),
        ),
        check_vma=False,
    )
```

time: 122 us -> 99.4 us (0.81); the launches traced: 120 us -> 99 us
  starting transfers between devices: 75.4 us -> 54.8 us
  waiting for transfers between devices: 17.7 us -> 21.2 us
  Pallas kernels: 19.2 us -> 16.9 us
  local copies, waits for them, and re-layouts: 6.53 us -> 5.11 us
    ppermute x23 -> x18, starting transfers between devices: 54.6 us -> 38.6 us  [hop(): return lax.ppermute(value, WORLD, moves(part, step))]
    ppermute x23 -> x18, waiting for transfers between devices: 9.79 us -> 20.2 us  [hop(): return lax.ppermute(value, WORLD, moves(part, step))]
    ppermute x8, waiting for transfers between devices: 7.91 us -> 0.97 us  [the longest x4 0.96 us: swapped(): far = lax.ppermute(far, 'seq', across)]
    ppermute x8, starting transfers between devices: 20.8 us -> 16.2 us  [the longest x4 12.7 us: swapped(): far = lax.ppermute(far, 'seq', across)]
    pallas_call x12 -> x14, Pallas kernels: 19.2 us -> 16.9 us  [run(): pl.pallas_call(body, out_shape=[jax.ShapeDtypeStruct(s, d) for s, d in ou...]
    unnamed x32 -> x30, local copies, waits for them, and re-layouts: 6.5 us -> 5.11 us
  transfers between devices with their start and end apart: 31 -> 26, of which waited for: 8 -> 12; matrix products, arithmetic and copies ran while one was open for 0% -> 0% of each run, Pallas kernels for 4% -> 10%
where the time goes in v2:
time: 99.4 us; the launch traced here: 99 us
  starting transfers between devices  54.8 us (55%)
  waiting for transfers between devices  21.2 us (21%)
  Pallas kernels  16.9 us (17%)
  local copies, waits for them, and re-layouts  5.11 us (5%)
    ppermute x18, starting transfers between devices, hop(): return lax.ppermute(value, WORLD, moves(part, step))  38.6 us
    ppermute x18, waiting for transfers between devices, hop(): return lax.ppermute(value, WORLD, moves(part, step))  20.2 us
    pallas_call x14, Pallas kernels, run(): pl.pallas_call(body, out_shape=[jax.ShapeDtypeStruct(s, d) for s, d in ou...  16.9 us
    ppermute x4, starting transfers between devices, swapped(): far = lax.ppermute(far, 'seq', across)  12.7 us
    unnamed x30, local copies, waits for them, and re-layouts  5.11 us
    ppermute x4, starting transfers between devices, swapped(): return (lax.ppermute(near, 'seq', chip), far)  3.52 us
  transfers between devices with their start and end apart: 26, of which 12 were waited for; matrix products, arithmetic and copies ran while one was open for 0% of the time, Pallas kernels for 10%

profile of v2, /device:TPU:1, one launch (start us, length us, event | category | flops | bytes accessed | tf_op | source)
XLA Modules:
  0.0 99.0 jit_solution(5387108005577015512)
XLA Ops:
  4.4 3.3 %collective-permute-start = (bf16[96,256]{1,0:T(8,128)(2,1)S(1)}, bf16[96,256]{1,0:T(8,128)(2,1)S(1)}, u32[]{:S(2)}, u32[]{:S(2)}) collective-permute-start(bf16[96,256]{1,0:T(8,128)(2,1)S(1)} %get-tuple-element.78), channel_id=1, source_target_pairs={{0,8},{8,0},{16,24},{24,16},{32,40},{40,32},{48,56},{56,48},{64,72... | collective-permute-start | bytes 147464 | tf_op jit(solution)/shard_map/ppermute | solution.py:47
  7.8 1.9 %collective-permute-start.1 = (bf16[96,256]{1,0:T(8,128)(2,1)S(1)}, bf16[96,256]{1,0:T(8,128)(2,1)S(1)}, u32[]{:S(2)}, u32[]{:S(2)}) collective-permute-start(bf16[96,256]{1,0:T(8,128)(2,1)S(1)} %get-tuple-element.79), channel_id=1, source_target_pairs={{8,16},{16,8},{24,32},{32,24},{40,48},{48,40},{56,64},{64,56},{72,... | collective-permute-start | bytes 147464 | tf_op jit(solution)/shard_map/ppermute | solution.py:46
  10.9 2.8 %shard_map.163.bias = f32[8,128,128]{2,1,0:T(8,128)S(1)} custom-call(f32[2,4,16]{2,1,0:T(4,128)S(1)} %bitcast.16, bf16[8,512,128]{2,1,0:T(8,128)(2,1)S(1)} %bitcast.9), custom_call_target="tpu_custom_call" | custom-call | flops 100000000 | bytes 1000000 | tf_op jit(solution)/shard_map/pallas_call | solution.py:68
  13.8 1.6 %shard_map.164 = (f32[256,128]{1,0:T(8,128)S(1)}, f32[8,128,128]{2,1,0:T(8,128)S(1)}, bf16[256,128]{1,0:T(8,128)(2,1)S(1)}, bf16[256,128]{1,0:T(8,128)(2,1)S(1)}...) custom-call(s32[8]{0:T(128)S(1)} %copy-done.12, ...), custom_call_target="tpu_custom_call" | custom-call | flops 100000000 | bytes 1000000 | tf_op jit(solution)/shard_map/pallas_call | solution.py:68
  15.5 3.6 %collective-permute-start.3 = (bf16[64,256]{1,0:T(8,128)(2,1)S(1)}, bf16[64,256]{1,0:T(8,128)(2,1)S(1)}, u32[]{:S(2)}, u32[]{:S(2)}) collective-permute-start(bf16[64,256]{1,0:T(8,128)(2,1)S(1)} %get-tuple-element.84), channel_id=1, source_target_pairs={{8,16},{16,8},{24,32},{32,24},{40,48},{48,40},{56,64},{64,56},{72,... | collective-permute-start | bytes 98312 | tf_op jit(solution)/shard_map/ppermute | solution.py:46
  19.2 2.8 %shard_map.165.bias = f32[8,128,128]{2,1,0:T(8,128)S(1)} custom-call(f32[2,4,16]{2,1,0:T(4,128)S(1)} %bitcast.17, bf16[8,512,128]{2,1,0:T(8,128)(2,1)S(1)} %bitcast.10, bf16[256,128]{1,0:T(8,128)(2,1)S(1)} %get-tuple-element.85.rest_0_.att), custom_call_target="tpu_custom_call" | custom-call | flops 100000000 | bytes 1000000 | tf_op jit(solution)/shard_map/pallas_call | solution.py:68
  22.6 2.4 %shard_map.166 = (bf16[256,128]{1,0:T(8,128)(2,1)S(1)}, bf16[256,128]{1,0:T(8,128)(2,1)S(1)}, bf16[256,128]{1,0:T(8,128)(2,1)S(1)}, bf16[256,384]{1,0:T(8,128)(2...) custom-call(s32[8]{0:T(128)S(1)} %copy-done.12, ...), custom_call_target="tpu_custom_call" | custom-call | flops 100000000 | bytes 1000000 | tf_op jit(solution)/shard_map/pallas_call | solution.py:68
  25.7 3.2 %collective-permute-start.5 = (bf16[64,256]{1,0:T(8,128)(2,1)S(1)}, bf16[64,256]{1,0:T(8,128)(2,1)S(1)}, u32[]{:S(2)}, u32[]{:S(2)}) collective-permute-start(bf16[64,256]{1,0:T(8,128)(2,1)S(1)} %get-tuple-element.91), channel_id=1, source_target_pairs={{8,16},{16,8},{24,32},{32,24},{40,48},{48,40},{56,64},{64,56},{72,... | collective-permute-start | bytes 98312 | tf_op jit(solution)/shard_map/ppermute | solution.py:46
  28.9 2.7 %collective-permute-start.9 = (bf16[2,128,128]{2,1,0:T(8,128)(2,1)S(1)}, bf16[2,128,128]{2,1,0:T(8,128)(2,1)S(1)}, u32[]{:S(2)}, u32[]{:S(2)}) collective-permute-start(bf16[2,128,128]{2,1,0:T(8,128)(2,1)S(1)} %get-tuple-element.94.two), channel_id=1, source_target_pairs={{0,4},{1,5},{2,6},{3,7},{4,0},{5,1},{6,2},{7,3},{8,12},{9,13},{10,... | collective-permute-start | bytes 196616 | tf_op jit(solution)/shard_map/ppermute | solution.py:38
  33.2 1.8 %shard_map.168 = (bf16[256,512]{1,0:T(8,128)(2,1)S(1)}, f32[1,128]{1,0:T(1,128)S(1)}, bf16[256,128]{1,0:T(8,128)(2,1)S(1)}, f32[256,128]{1,0:T(8,128)S(1)}, bf16...) custom-call(s32[8]{0:T(128)S(1)} %copy-done.12, ...), custom_call_target="tpu_custom_call" | custom-call | flops 100000000 | bytes 1000000 | tf_op jit(solution)/shard_map/pallas_call | solution.py:68
  35.1 3.9 %collective-permute-start.8 = (bf16[64,256]{1,0:T(8,128)(2,1)S(1)}, bf16[64,256]{1,0:T(8,128)(2,1)S(1)}, u32[]{:S(2)}, u32[]{:S(2)}) collective-permute-start(bf16[64,256]{1,0:T(8,128)(2,1)S(1)} %get-tuple-element.109), channel_id=1, source_target_pairs={{8,16},{16,8},{24,32},{32,24},{40,48},{48,40},{56,64},{64,56},{72,... | collective-permute-start | bytes 98312 | tf_op jit(solution)/shard_map/ppermute | solution.py:46
  41.7 1.5 %collective-permute-done.11.got = bf16[4,224,128]{2,1,0:T(8,128)(2,1)S(1)} collective-permute-done((bf16[4,224,128]{2,1,0:T(8,128)(2,1)S(1)}, bf16[4,224,128]{2,1,0:T(8,128)(2,1)S(1)}, u32[]{:S(2)}, u32[]{:S(2)}) %collective-permute-start.11) | collective-permute-done | bytes 229408 | tf_op jit(solution)/shard_map/ppermute | solution.py:38
  44.6 1.7 %collective-permute-start.14 = (bf16[480,128]{1,0:T(8,128)(2,1)S(1)}, bf16[480,128]{1,0:T(8,128)(2,1)S(1)}, u32[]{:S(2)}, u32[]{:S(2)}) collective-permute-start(bf16[480,128]{1,0:T(8,128)(2,1)S(1)} %get-tuple-element.132), channel_id=1, source_target_pairs={{0,6},{1,7},{2,0},{3,1},{4,2},{5,3},{6,4},{7,5},{8,14},{9,15},{10,... | collective-permute-start | bytes 368648 | tf_op jit(solution)/shard_map/ppermute | solution.py:38
  46.3 5.7 %collective-permute-done.12.one = bf16[480,128]{1,0:T(8,128)(2,1)S(1)} collective-permute-done((bf16[480,128]{1,0:T(8,128)(2,1)S(1)}, bf16[480,128]{1,0:T(8,128)(2,1)S(1)}, u32[]{:S(2)}, u32[]{:S(2)}) %collective-permute-start.12) | collective-permute-done | bytes 122912 | tf_op jit(solution)/shard_map/ppermute | solution.py:38
  52.5 7.0 %collective-permute-start.15 = (bf16[480,128]{1,0:T(8,128)(2,1)S(1)}, bf16[480,128]{1,0:T(8,128)(2,1)S(1)}, u32[]{:S(2)}, u32[]{:S(2)}) collective-permute-start(bf16[480,128]{1,0:T(8,128)(2,1)S(1)} %get-tuple-element.136), channel_id=1, source_target_pairs={{0,1},{1,0},{2,3},{3,2},{4,5},{5,4},{6,7},{7,6},{8,9},{9,8},{10,11... | collective-permute-start | bytes 368648 | tf_op jit(solution)/shard_map/ppermute | solution.py:38
  59.4 2.3 %collective-permute-done.15.got = bf16[480,128]{1,0:T(8,128)(2,1)S(1)} collective-permute-done((bf16[480,128]{1,0:T(8,128)(2,1)S(1)}, bf16[480,128]{1,0:T(8,128)(2,1)S(1)}, u32[]{:S(2)}, u32[]{:S(2)}) %collective-permute-start.15) | collective-permute-done | bytes 122912 | tf_op jit(solution)/shard_map/ppermute | solution.py:38
  61.7 7.2 %collective-permute-start.18 = (bf16[224,128]{1,0:T(8,128)(2,1)S(1)}, bf16[224,128]{1,0:T(8,128)(2,1)S(1)}, u32[]{:S(2)}, u32[]{:S(2)}) collective-permute-start(bf16[224,128]{1,0:T(8,128)(2,1)S(1)} %add_convert_fusion.2), channel_id=1, source_target_pairs={{0,48},{1,49},{2,50},{3,51},{4,52},{5,53},{6,54},{7,55},{8,56},{9,... | collective-permute-start | bytes 172040 | tf_op jit(solution)/shard_map/ppermute | solution.py:38
  70.2 1.4 %shard_map.173 = bf16[512,128]{1,0:T(8,128)(2,1)} custom-call(f32[2,4,16]{2,1,0:T(4,128)S(1)} %bitcast.18, f32[2,128,128]{2,1,0:T(8,128)S(1)} %get-tuple-element.137.kept, bf16[480,128]{1,0:T(8,128)(2,1)S(1)} %collective-permute-done.15.got), custom_call_target="tpu_custom_call" | custom-call | flops 100000000 | bytes 1000000 | tf_op jit(solution)/shard_map/pallas_call | solution.py:68
  71.6 2.2 %collective-permute-done.17 = bf16[224,128]{1,0:T(8,128)(2,1)S(1)} collective-permute-done((bf16[224,128]{1,0:T(8,128)(2,1)S(1)}, bf16[224,128]{1,0:T(8,128)(2,1)S(1)}, u32[]{:S(2)}, u32[]{:S(2)}) %collective-permute-start.17) | collective-permute-done | bytes 57376 | tf_op jit(solution)/shard_map/ppermute | solution.py:38
  75.4 5.0 %collective-permute-start.19 = (bf16[224,128]{1,0:T(8,128)(2,1)S(1)}, bf16[224,128]{1,0:T(8,128)(2,1)S(1)}, u32[]{:S(2)}, u32[]{:S(2)}) collective-permute-start(bf16[224,128]{1,0:T(8,128)(2,1)S(1)} %add_convert_fusion.1), channel_id=1, source_target_pairs={{0,128},{1,129},{2,130},{3,131},{4,132},{5,133},{6,134},{7,135},{8... | collective-permute-start | bytes 172040 | tf_op jit(solution)/shard_map/ppermute | solution.py:38
  80.4 2.1 %collective-permute-done.20 = bf16[224,128]{1,0:T(8,128)(2,1)S(1)} collective-permute-done((bf16[224,128]{1,0:T(8,128)(2,1)S(1)}, bf16[224,128]{1,0:T(8,128)(2,1)S(1)}, u32[]{:S(2)}, u32[]{:S(2)}) %collective-permute-start.20) | collective-permute-done | bytes 57376 | tf_op jit(solution)/shard_map/ppermute | solution.py:38
  83.3 3.4 %collective-permute-start.24 = (bf16[224,128]{1,0:T(8,128)(2,1)S(1)}, bf16[224,128]{1,0:T(8,128)(2,1)S(1)}, u32[]{:S(2)}, u32[]{:S(2)}) collective-permute-start(bf16[224,128]{1,0:T(8,128)(2,1)S(1)} %add_convert_fusion.own), channel_id=1, source_target_pairs={{0,6},{1,7},{2,0},{3,1},{4,2},{5,3},{6,4},{7,5},{8,14},{9,15},{10,... | collective-permute-start | bytes 172040 | tf_op jit(solution)/shard_map/ppermute | solution.py:38
  88.0 3.4 %collective-permute-done.23.two = bf16[224,128]{1,0:T(8,128)(2,1)S(1)} collective-permute-done((bf16[224,128]{1,0:T(8,128)(2,1)S(1)}, bf16[224,128]{1,0:T(8,128)(2,1)S(1)}, u32[]{:S(2)}, u32[]{:S(2)}) %collective-permute-start.23) | collective-permute-done | bytes 57376 | tf_op jit(solution)/shard_map/ppermute | solution.py:38
  91.6 5.2 %collective-permute-start.25 = (bf16[4,224,128]{2,1,0:T(8,128)(2,1)S(1)}, bf16[4,224,128]{2,1,0:T(8,128)(2,1)S(1)}, u32[]{:S(2)}, u32[]{:S(2)}) collective-permute-start(bf16[4,224,128]{2,1,0:T(8,128)(2,1)S(1)} %shard_map.174.half), channel_id=1, source_target_pairs={{0,8},{1,9},{2,10},{3,11},{4,12},{5,13},{6,14},{7,15},{8,0},{9,1},... | collective-permute-start | bytes 688136 | tf_op jit(solution)/shard_map/ppermute | solution.py:38
  (75 shorter events, 19.9 us)
Async XLA Ops:
  4.4 9.3 %collective-permute-start = (bf16[96,256]{1,0:T(8,128)(2,1)S(1)}, bf16[96,256]{1,0:T(8,128)(2,1)S(1)}, u32[]{:S(2)}, u32[]{:S(2)}) collective-permute-start(bf16[96,256]{1,0:T(8,128)(2,1)S(1)} %get-tuple-element.78), channel_id=1, source_target_pairs={{0,8},{8,0},{16,24},{24,16},{32,40},{40,32},{48,56},{56,48},{64,72... | collective-permute-start | bytes 147464 | tf_op jit(solution)/shard_map/ppermute | solution.py:47
  7.8 6.0 %collective-permute-start.1 = (bf16[96,256]{1,0:T(8,128)(2,1)S(1)}, bf16[96,256]{1,0:T(8,128)(2,1)S(1)}, u32[]{:S(2)}, u32[]{:S(2)}) collective-permute-start(bf16[96,256]{1,0:T(8,128)(2,1)S(1)} %get-tuple-element.79), channel_id=1, source_target_pairs={{8,16},{16,8},{24,32},{32,24},{40,48},{48,40},{56,64},{64,56},{72,... | collective-permute-start | bytes 147464 | tf_op jit(solution)/shard_map/ppermute | solution.py:46
  15.4 6.6 %collective-permute-start.2 = (bf16[64,256]{1,0:T(8,128)(2,1)S(1)}, bf16[64,256]{1,0:T(8,128)(2,1)S(1)}, u32[]{:S(2)}, u32[]{:S(2)}) collective-permute-start(bf16[64,256]{1,0:T(8,128)(2,1)S(1)} %get-tuple-element.83), channel_id=1, source_target_pairs={{0,8},{8,0},{16,24},{24,16},{32,40},{40,32},{48,56},{56,48},{64,72... | collective-permute-start | bytes 98312 | tf_op jit(solution)/shard_map/ppermute | solution.py:47
  15.5 6.5 %collective-permute-start.3 = (bf16[64,256]{1,0:T(8,128)(2,1)S(1)}, bf16[64,256]{1,0:T(8,128)(2,1)S(1)}, u32[]{:S(2)}, u32[]{:S(2)}) collective-permute-start(bf16[64,256]{1,0:T(8,128)(2,1)S(1)} %get-tuple-element.84), channel_id=1, source_target_pairs={{8,16},{16,8},{24,32},{32,24},{40,48},{48,40},{56,64},{64,56},{72,... | collective-permute-start | bytes 98312 | tf_op jit(solution)/shard_map/ppermute | solution.py:46
  25.1 8.1 %collective-permute-start.6 = (bf16[2,128,128]{2,1,0:T(8,128)(2,1)S(1)}, bf16[2,128,128]{2,1,0:T(8,128)(2,1)S(1)}, u32[]{:S(2)}, u32[]{:S(2)}) collective-permute-start(bf16[2,128,128]{2,1,0:T(8,128)(2,1)S(1)} %get-tuple-element.92.one), channel_id=1, source_target_pairs={{0,2},{1,3},{2,4},{3,5},{4,6},{5,7},{6,0},{7,1},{8,10},{9,11},{10,... | collective-permute-start | bytes 196616 | tf_op jit(solution)/shard_map/ppermute | solution.py:38
  25.7 7.5 %collective-permute-start.4 = (bf16[64,256]{1,0:T(8,128)(2,1)S(1)}, bf16[64,256]{1,0:T(8,128)(2,1)S(1)}, u32[]{:S(2)}, u32[]{:S(2)}) collective-permute-start(bf16[64,256]{1,0:T(8,128)(2,1)S(1)} %get-tuple-element.90), channel_id=1, source_target_pairs={{0,8},{8,0},{16,24},{24,16},{32,40},{40,32},{48,56},{56,48},{64,72... | collective-permute-start | bytes 98312 | tf_op jit(solution)/shard_map/ppermute | solution.py:47
  25.7 7.5 %collective-permute-start.5 = (bf16[64,256]{1,0:T(8,128)(2,1)S(1)}, bf16[64,256]{1,0:T(8,128)(2,1)S(1)}, u32[]{:S(2)}, u32[]{:S(2)}) collective-permute-start(bf16[64,256]{1,0:T(8,128)(2,1)S(1)} %get-tuple-element.91), channel_id=1, source_target_pairs={{8,16},{16,8},{24,32},{32,24},{40,48},{48,40},{56,64},{64,56},{72,... | collective-permute-start | bytes 98312 | tf_op jit(solution)/shard_map/ppermute | solution.py:46
  28.9 10.8 %collective-permute-start.9 = (bf16[2,128,128]{2,1,0:T(8,128)(2,1)S(1)}, bf16[2,128,128]{2,1,0:T(8,128)(2,1)S(1)}, u32[]{:S(2)}, u32[]{:S(2)}) collective-permute-start(bf16[2,128,128]{2,1,0:T(8,128)(2,1)S(1)} %get-tuple-element.94.two), channel_id=1, source_target_pairs={{0,4},{1,5},{2,6},{3,7},{4,0},{5,1},{6,2},{7,3},{8,12},{9,13},{10,... | collective-permute-start | bytes 196616 | tf_op jit(solution)/shard_map/ppermute | solution.py:38
  31.6 8.1 %collective-permute-start.10 = (bf16[2,128,128]{2,1,0:T(8,128)(2,1)S(1)}, bf16[2,128,128]{2,1,0:T(8,128)(2,1)S(1)}, u32[]{:S(2)}, u32[]{:S(2)}) collective-permute-start(bf16[2,128,128]{2,1,0:T(8,128)(2,1)S(1)} %get-tuple-element.95.three), channel_id=1, source_target_pairs={{0,6},{1,7},{2,0},{3,1},{4,2},{5,3},{6,4},{7,5},{8,14},{9,15},{10,... | collective-permute-start | bytes 196616 | tf_op jit(solution)/shard_map/ppermute | solution.py:38
  35.0 4.6 %collective-permute-start.7 = (bf16[64,256]{1,0:T(8,128)(2,1)S(1)}, bf16[64,256]{1,0:T(8,128)(2,1)S(1)}, u32[]{:S(2)}, u32[]{:S(2)}) collective-permute-start(bf16[64,256]{1,0:T(8,128)(2,1)S(1)} %get-tuple-element.108), channel_id=1, source_target_pairs={{0,8},{8,0},{16,24},{24,16},{32,40},{40,32},{48,56},{56,48},{64,72... | collective-permute-start | bytes 98312 | tf_op jit(solution)/shard_map/ppermute | solution.py:47
  35.1 5.5 %collective-permute-start.8 = (bf16[64,256]{1,0:T(8,128)(2,1)S(1)}, bf16[64,256]{1,0:T(8,128)(2,1)S(1)}, u32[]{:S(2)}, u32[]{:S(2)}) collective-permute-start(bf16[64,256]{1,0:T(8,128)(2,1)S(1)} %get-tuple-element.109), channel_id=1, source_target_pairs={{8,16},{16,8},{24,32},{32,24},{40,48},{48,40},{56,64},{64,56},{72,... | collective-permute-start | bytes 98312 | tf_op jit(solution)/shard_map/ppermute | solution.py:46
  43.3 8.7 %collective-permute-start.12 = (bf16[480,128]{1,0:T(8,128)(2,1)S(1)}, bf16[480,128]{1,0:T(8,128)(2,1)S(1)}, u32[]{:S(2)}, u32[]{:S(2)}) collective-permute-start(bf16[480,128]{1,0:T(8,128)(2,1)S(1)} %get-tuple-element.130), channel_id=1, source_target_pairs={{0,2},{1,3},{2,4},{3,5},{4,6},{5,7},{6,0},{7,1},{8,10},{9,11},{10,... | collective-permute-start | bytes 368648 | tf_op jit(solution)/shard_map/ppermute | solution.py:38
  43.8 8.2 %collective-permute-start.13 = (bf16[480,128]{1,0:T(8,128)(2,1)S(1)}, bf16[480,128]{1,0:T(8,128)(2,1)S(1)}, u32[]{:S(2)}, u32[]{:S(2)}) collective-permute-start(bf16[480,128]{1,0:T(8,128)(2,1)S(1)} %get-tuple-element.131), channel_id=1, source_target_pairs={{0,4},{1,5},{2,6},{3,7},{4,0},{5,1},{6,2},{7,3},{8,12},{9,13},{10,... | collective-permute-start | bytes 368648 | tf_op jit(solution)/shard_map/ppermute | solution.py:38
  44.6 7.7 %collective-permute-start.14 = (bf16[480,128]{1,0:T(8,128)(2,1)S(1)}, bf16[480,128]{1,0:T(8,128)(2,1)S(1)}, u32[]{:S(2)}, u32[]{:S(2)}) collective-permute-start(bf16[480,128]{1,0:T(8,128)(2,1)S(1)} %get-tuple-element.132), channel_id=1, source_target_pairs={{0,6},{1,7},{2,0},{3,1},{4,2},{5,3},{6,4},{7,5},{8,14},{9,15},{10,... | collective-permute-start | bytes 368648 | tf_op jit(solution)/shard_map/ppermute | solution.py:38
  52.5 9.3 %collective-permute-start.15 = (bf16[480,128]{1,0:T(8,128)(2,1)S(1)}, bf16[480,128]{1,0:T(8,128)(2,1)S(1)}, u32[]{:S(2)}, u32[]{:S(2)}) collective-permute-start(bf16[480,128]{1,0:T(8,128)(2,1)S(1)} %get-tuple-element.136), channel_id=1, source_target_pairs={{0,1},{1,0},{2,3},{3,2},{4,5},{5,4},{6,7},{7,6},{8,9},{9,8},{10,11... | collective-permute-start | bytes 368648 | tf_op jit(solution)/shard_map/ppermute | solution.py:38
  61.7 9.9 %collective-permute-start.18 = (bf16[224,128]{1,0:T(8,128)(2,1)S(1)}, bf16[224,128]{1,0:T(8,128)(2,1)S(1)}, u32[]{:S(2)}, u32[]{:S(2)}) collective-permute-start(bf16[224,128]{1,0:T(8,128)(2,1)S(1)} %add_convert_fusion.2), channel_id=1, source_target_pairs={{0,48},{1,49},{2,50},{3,51},{4,52},{5,53},{6,54},{7,55},{8,56},{9,... | collective-permute-start | bytes 172040 | tf_op jit(solution)/shard_map/ppermute | solution.py:38
  68.9 4.9 %collective-permute-start.17 = (bf16[224,128]{1,0:T(8,128)(2,1)S(1)}, bf16[224,128]{1,0:T(8,128)(2,1)S(1)}, u32[]{:S(2)}, u32[]{:S(2)}) collective-permute-start(bf16[224,128]{1,0:T(8,128)(2,1)S(1)} %add_convert_fusion.2), channel_id=1, source_target_pairs={{0,16},{1,17},{2,18},{3,19},{4,20},{5,21},{6,22},{7,23},{8,24},{9,... | collective-permute-start | bytes 172040 | tf_op jit(solution)/shard_map/ppermute | solution.py:38
  68.9 4.9 %collective-permute-start.16 = (bf16[224,128]{1,0:T(8,128)(2,1)S(1)}, bf16[224,128]{1,0:T(8,128)(2,1)S(1)}, u32[]{:S(2)}, u32[]{:S(2)}) collective-permute-start(bf16[224,128]{1,0:T(8,128)(2,1)S(1)} %add_convert_fusion.2), channel_id=1, source_target_pairs={{0,32},{1,33},{2,34},{3,35},{4,36},{5,37},{6,38},{7,39},{8,40},{9,... | collective-permute-start | bytes 172040 | tf_op jit(solution)/shard_map/ppermute | solution.py:38
  73.8 6.6 %collective-permute-start.21 = (bf16[224,128]{1,0:T(8,128)(2,1)S(1)}, bf16[224,128]{1,0:T(8,128)(2,1)S(1)}, u32[]{:S(2)}, u32[]{:S(2)}) collective-permute-start(bf16[224,128]{1,0:T(8,128)(2,1)S(1)} %add_convert_fusion.1), channel_id=1, source_target_pairs={{0,192},{1,193},{2,194},{3,195},{4,196},{5,197},{6,198},{7,199},{8... | collective-permute-start | bytes 172040 | tf_op jit(solution)/shard_map/ppermute | solution.py:38
  75.1 7.3 %collective-permute-start.20 = (bf16[224,128]{1,0:T(8,128)(2,1)S(1)}, bf16[224,128]{1,0:T(8,128)(2,1)S(1)}, u32[]{:S(2)}, u32[]{:S(2)}) collective-permute-start(bf16[224,128]{1,0:T(8,128)(2,1)S(1)} %add_convert_fusion.1), channel_id=1, source_target_pairs={{0,64},{1,65},{2,66},{3,67},{4,68},{5,69},{6,70},{7,71},{8,72},{9,... | collective-permute-start | bytes 172040 | tf_op jit(solution)/shard_map/ppermute | solution.py:38
  75.4 7.9 %collective-permute-start.19 = (bf16[224,128]{1,0:T(8,128)(2,1)S(1)}, bf16[224,128]{1,0:T(8,128)(2,1)S(1)}, u32[]{:S(2)}, u32[]{:S(2)}) collective-permute-start(bf16[224,128]{1,0:T(8,128)(2,1)S(1)} %add_convert_fusion.1), channel_id=1, source_target_pairs={{0,128},{1,129},{2,130},{3,131},{4,132},{5,133},{6,134},{7,135},{8... | collective-permute-start | bytes 172040 | tf_op jit(solution)/shard_map/ppermute | solution.py:38
  83.3 4.7 %collective-permute-start.24 = (bf16[224,128]{1,0:T(8,128)(2,1)S(1)}, bf16[224,128]{1,0:T(8,128)(2,1)S(1)}, u32[]{:S(2)}, u32[]{:S(2)}) collective-permute-start(bf16[224,128]{1,0:T(8,128)(2,1)S(1)} %add_convert_fusion.own), channel_id=1, source_target_pairs={{0,6},{1,7},{2,0},{3,1},{4,2},{5,3},{6,4},{7,5},{8,14},{9,15},{10,... | collective-permute-start | bytes 172040 | tf_op jit(solution)/shard_map/ppermute | solution.py:38
  86.8 4.9 %collective-permute-start.22 = (bf16[224,128]{1,0:T(8,128)(2,1)S(1)}, bf16[224,128]{1,0:T(8,128)(2,1)S(1)}, u32[]{:S(2)}, u32[]{:S(2)}) collective-permute-start(bf16[224,128]{1,0:T(8,128)(2,1)S(1)} %add_convert_fusion.own), channel_id=1, source_target_pairs={{0,2},{1,3},{2,4},{3,5},{4,6},{5,7},{6,0},{7,1},{8,10},{9,11},{10,... | collective-permute-start | bytes 172040 | tf_op jit(solution)/shard_map/ppermute | solution.py:38
  91.6 6.3 %collective-permute-start.25 = (bf16[4,224,128]{2,1,0:T(8,128)(2,1)S(1)}, bf16[4,224,128]{2,1,0:T(8,128)(2,1)S(1)}, u32[]{:S(2)}, u32[]{:S(2)}) collective-permute-start(bf16[4,224,128]{2,1,0:T(8,128)(2,1)S(1)} %shard_map.174.half), channel_id=1, source_target_pairs={{0,8},{1,9},{2,10},{3,11},{4,12},{5,13},{6,14},{7,15},{8,0},{9,1},... | collective-permute-start | bytes 688136 | tf_op jit(solution)/shard_map/ppermute | solution.py:38
  (17 other events, 39.6 us)

commit v3 on v2

--- a/solution.py
+++ b/solution.py
@@ -58,7 +58,7 @@
     return pair_up(value.astype(F32), got).astype(BF16)
 
 
-def run(body, outs, args, smem=(), hbm=(), scratch=(), flops=10**8, nbytes=10**6):
+def run(body, outs, args, smem=(), hbm=(), scratch=(), vmem=24, flops=10**8, nbytes=10**6):
     spaces = [pltpu.VMEM] * len(args)
     for i in smem:
         spaces[i] = pltpu.SMEM
@@ -71,7 +71,7 @@
         in_specs=specs,
         out_specs=[pl.BlockSpec(memory_space=pltpu.VMEM) for _ in outs],
         scratch_shapes=list(scratch),
-        compiler_params=pltpu.CompilerParams(vmem_limit_bytes=24 * 2**20),
+        compiler_params=pltpu.CompilerParams(vmem_limit_bytes=int(vmem * 2**20)),
         cost_estimate=pl.CostEstimate(flops=flops, bytes_accessed=nbytes, transcendentals=0),
     )(*args)
 
@@ -115,21 +115,6 @@
 
 def odd_core():
     return lax.rem(lax.axis_index("seq"), 2) == 1
-
-
-def project_into(state, gain, weight, normed_ref, q_ref, kv_ref, gate_ref, near_ref, far_ref):
-    unit, _ = stats(state)
-    normed = (unit * gain).astype(BF16)
-    normed_ref[...] = normed
-    projected = nn(normed, weight)
-    q_ref[...] = projected[:, 0:128].astype(BF16)
-    kv = projected[:, 128:384]
-    kv_ref[...] = kv.astype(BF16)
-    gate_ref[...] = sigmoid(projected[:, 384:512])
-    rows = kv.shape[0]
-    head, tail = kv[0:HALO], kv[rows - HALO : rows]
-    near_ref[0:HALO, :] = jnp.where(odd_core(), head, tail).astype(BF16)
-    far_ref[0:HALO, :] = jnp.where(odd_core(), tail, head).astype(BF16)
 
 
 def from_before(near, far):
@@ -148,107 +133,128 @@
     return jnp.broadcast_to(column, (size, 128))
 
 
-def first_kernel(
-    atoms_far,
-    gain_far,
-    weight_far,
-    grad_far,
-    counts_far,
-    normed,
-    q,
-    kv,
-    gate,
-    near,
-    far,
-    atoms,
-    gain,
-    weight,
-    grad,
-    counts,
-    sems,
+FIRST_VMEM = 62
+PAIR_ROWS = 1024
+ATOM_ROWS = PAIR_ROWS + 2 * HALO
+MESSAGE = ATOM_ROWS + 16
+
+
+def message_kernel(
+    shift_far, pair, atoms, grad_far, counts_far, near, far, shift_row, shift, grad, counts, sems
 ):
-    pairs = (
-        (atoms_far, atoms),
-        (weight_far, weight),
-        (gain_far, gain),
-        (grad_far, grad),
-        (counts_far, counts),
-    )
-    copies = [pltpu.make_async_copy(a, b, sems.at[i]) for i, (a, b) in enumerate(pairs)]
+    blocks, rows = pair.shape[0], atoms.shape[0]
+    odd = odd_core()
+    copies = [
+        pltpu.make_async_copy(a, b, sems.at[i])
+        for i, (a, b) in enumerate(((shift_far, shift), (grad_far, grad), (counts_far, counts)))
+    ]
+    bases = (jnp.where(odd, 0, blocks - 2), jnp.where(odd, blocks - 2, 0))
+    for n, ref in enumerate((near, far)):
+        for m in range(2):
+            copies.append(
+                pltpu.make_async_copy(
+                    pair.at[bases[n] + m], ref.at[pl.ds(m * 512, 512)], sems.at[3 + n * 3 + m]
+                )
+            )
+        first = pl.multiple_of(bases[n] * QBLK // (rows // 2) * (rows // 2), 128)
+        copies.append(
+            pltpu.make_async_copy(
+                atoms.at[pl.ds(first, 2 * HALO)],
+                ref.at[pl.ds(PAIR_ROWS, 2 * HALO)],
+                sems.at[3 + n * 3 + 2],
+            )
+        )
     for copy in copies:
         copy.start()
-    for copy in copies:
+    for copy in copies[:3]:
         copy.wait()
-    project_into(atoms[...].astype(F32), gain[0:1, :], weight[0], normed, q, kv, gate, near, far)
-    last = lax.broadcasted_iota(jnp.int32, (16, 384), 0) == 15
-    row = jnp.where(last, grad[16:32, :].astype(F32), 0.0).astype(BF16)
-    many = jnp.where(last[:, :128], count_rows(counts[...])[16:32], 0.0).astype(BF16)
-    for ref in (near, far):
-        ref[HALO : HALO + 16, :] = row[:, 0:256]
-        ref[HALO + 16 : HALO + 32, 0:128] = row[:, 256:384]
-        ref[HALO + 16 : HALO + 32, 128:256] = many
-
-
-def bias_kernel(layer, weight, pair_far, *rest):
-    bias, pair, sems = rest[-3:]
-    blocks = pair.shape[0]
-
-    def fetch(j):
-        return pltpu.make_async_copy(pair_far.at[j], pair.at[j], sems.at[j])
-
+    size = counts.shape[1]
+    lanes = lax.broadcasted_iota(jnp.int32, (1, size), 1)
+    many = jnp.where(lanes == size - 1, counts[...].astype(F32), 0.0)
+    many = jnp.sum(many, -1, keepdims=True)
+    last = grad[16:32, :].astype(F32)[15:16, :]
+    row = lax.broadcasted_iota(jnp.int32, (16, 128), 0)
+    lane = lax.broadcasted_iota(jnp.int32, (16, 128), 1)
+    group = jnp.where(row == 3, jnp.broadcast_to(many, (16, 128)), 0.0)
+    for k in range(3):
+        piece = jnp.broadcast_to(last[:, k * 128 : (k + 1) * 128], (16, 128))
+        group = jnp.where(row == k, piece, group)
+    for n, ref in enumerate((near, far)):
+        value = group
+        for m in range(2):
+            place = jnp.logical_and(row == 4, lane == m)
+            value = jnp.where(place, shift[bases[n] + m].astype(F32), value)
+        ref[ATOM_ROWS:MESSAGE, :] = value.astype(BF16)
+    lane = lax.broadcasted_iota(jnp.int32, (1, 128), 1)
+    shifts = jnp.zeros((1, 128), jnp.int32)
     for j in range(blocks):
-        fetch(j).start()
-
+        shifts = jnp.where(lane == j, shift[j], shifts)
+    shift_row[...] = shifts
+    for copy in copies[3:]:
+        copy.wait()
+
+
+def first_kernel(atoms, gain, weight, normed, q, kv, gate):
+    unit, _ = stats(atoms[...].astype(F32))
+    normed[...] = (unit * gain[0:1, :]).astype(BF16)
+    projected = nn(normed[...], weight[0])
+    q[...] = projected[:, 0:128].astype(BF16)
+    kv[...] = projected[:, 128:384].astype(BF16)
+    gate[...] = sigmoid(projected[:, 384:512])
+
+
+def block_bias(weight, layers, part):
+    totals = [[None] * HEADS for _ in layers]
+    for c in range(16):
+        value = part(c)
+        for n, layer in enumerate(layers):
+            for h in range(HEADS):
+                term = value * weight[layer, h, c]
+                totals[n][h] = term if c == 0 else totals[n][h] + term
+    return totals
+
+
+def bias_kernel(weight, pair, first, later):
     def block(j, carry):
-        fetch(j).wait()
-        totals = [None] * HEADS
-        for c in range(16):
-            part = pair[j, c * 32 : (c + 1) * 32, :].astype(F32)
+        totals = block_bias(
+            weight, (0, 1), lambda c: pair[j, c * 32 : (c + 1) * 32, :].astype(F32)
+        )
+        for ref, total in zip((first, later), totals):
             for h in range(HEADS):
-                term = part * weight[layer, h, c]
-                totals[h] = term if c == 0 else totals[h] + term
-        for h in range(HEADS):
-            bias[j, h * 32 : (h + 1) * 32, :] = totals[h]
+                ref[j, h * 32 : (h + 1) * 32, :] = total[h]
         return carry
 
-    lax.fori_loop(0, blocks, block, 0)
-
-
-def load_window(kv, near, far, keys, values):
-    rows = kv.shape[0]
-    for ref, at in ((keys, 0), (values, 128)):
-        beside, across = near[0:HALO, at : at + 128], far[0:HALO, at : at + 128]
-        ref[0:HALO, :] = from_before(beside, across)
-        ref[HALO : HALO + rows, :] = kv[:, at : at + 128].astype(F32)
-        ref[HALO + rows : HALO + rows + HALO, :] = from_after(beside, across)
-
-
-def windows(shift, q, keys, values):
+    lax.fori_loop(0, pair.shape[0], block, 0)
+
+
+def load_window(kv, keys, values):
+    keys[...] = kv[:, 0:128].astype(F32)
+    values[...] = kv[:, 128:256].astype(F32)
+
+
+def windows(shifts, q, keys, values, margin):
     mask = head_mask(128)
-    spans = [pl.ds(j * QBLK + shift[j] + HALO, KWIN) for j in range(q.shape[0] // QBLK)]
+    spans = [pl.ds(j * QBLK + shift + margin, KWIN) for j, shift in enumerate(shifts)]
     wide = [stacked(q[j * QBLK : (j + 1) * QBLK, :], mask) for j in range(len(spans))]
     key = [keys[span, :].astype(BF16) for span in spans]
     value = [values[span, :].astype(BF16) for span in spans]
     return spans, wide, key, value
 
 
-def attention_forward(shift, found, bias, att, rows, atom_total):
+def attention_forward(shifts, found, bias, first, atom_total):
     _, wide, key, value = found
     count = len(wide)
     mask = head_mask(128)
-    first = lax.axis_index("seq") * rows
     lane = lax.broadcasted_iota(jnp.int32, (1, KWIN), 1)
     scores = [nt(wide[j], key[j]) for j in range(count)]
     chances = []
     for j in range(count):
-        place = first + (j * QBLK + shift[j]) + lane
+        place = first + (j * QBLK + shifts[j]) + lane
         inside = jnp.logical_and(place >= 0, place < atom_total)
         weights = jnp.where(inside, jnp.exp(scores[j] * (32.0**-0.5) + bias[j]), 0.0)
         chances.append(weights * (1.0 / jnp.sum(weights, -1, keepdims=True)))
     out = [nn(chances[j].astype(BF16), value[j]) for j in range(count)]
-    for j in range(count):
-        att[j * QBLK : (j + 1) * QBLK, :] = picked(out[j], mask).astype(BF16)
-    return chances
+    return chances, jnp.concatenate([picked(v, mask) for v in out], 0).astype(BF16)
 
 
 def attention_backward(found, chances, grad_att, grad_q, grad_keys, grad_values, score_grad):
@@ -275,15 +281,17 @@
         grad_values[spans[j], :] += value_back[j].astype(BF16).astype(F32)
 
 
-def share_scores(score_grad, own, one, two, three):
+def share_scores(scores, parts):
     y = lax.axis_index("samp") // 2
-    for k, ref in enumerate((own, one, two, three)):
-        ref[...] = score_grad[pl.ds(lax.rem(y + k, 4) * 2, 2)]
+    for k, ref in enumerate(parts):
+        for n, score in enumerate(scores):
+            ref[n * 2 : n * 2 + 2] = score[pl.ds(lax.rem(y + k, 4) * 2, 2)]
 
 
 def forward_kernel(
     atom_total,
     shift,
+    channel_weight,
     q,
     kv,
     near,
@@ -297,25 +305,69 @@
     state,
     chances,
     att,
+    kv_all,
     normed,
     q_next,
     kv_next,
     gate_next,
-    near_next,
-    far_next,
     keys,
     values,
 ):
-    load_window(kv, near, far, keys, values)
-    found = windows(shift, q, keys, values)
-    kept = attention_forward(shift, found, bias, att, q.shape[0], atom_total)
-    for j, chance in enumerate(kept):
-        chances[j] = chance
-    after = atoms[...].astype(F32) + gate[...] * nn(att[...], weight_out[0])
-    state[...] = after
-    project_into(
-        after, gain[1:2, :], weight_in[1], normed, q_next, kv_next, gate_next, near_next, far_next
-    )
+    blocks, rows = bias.shape[0], q.shape[0]
+    edge = HALO // QBLK
+    first = lax.axis_index("seq") * rows
+    there = slice(PAIR_ROWS, ATOM_ROWS)
+    before, after = from_before(near[there], far[there]), from_after(near[there], far[there])
+    beside = jnp.concatenate([before, after], 0)
+    unit, _ = stats(beside)
+    projected = nn((unit * gain[0:1, :]).astype(BF16), weight_in[0])
+    for ref, at in ((keys, 128), (values, 256)):
+        ref[0 : 2 * HALO, :] = projected[0 : 2 * HALO, at : at + 128].astype(BF16).astype(F32)
+        ref[2 * HALO : 2 * HALO + rows, :] = kv[:, at - 128 : at].astype(F32)
+        ref[2 * HALO + rows :, :] = projected[2 * HALO :, at : at + 128].astype(BF16).astype(F32)
+    kv_all[:, 0:128] = keys[HALO : 3 * HALO + rows, :].astype(BF16)
+    kv_all[:, 128:256] = values[HALO : 3 * HALO + rows, :].astype(BF16)
+    ends = slice(HALO, 2 * HALO), slice(2 * HALO, 3 * HALO)
+    queries = [projected[end, 0:128].astype(BF16) for end in ends]
+    queries = jnp.concatenate([queries[0], q[...], queries[1]], 0)
+    gates = [sigmoid(projected[end, 384:512]) for end in ends]
+    gates = jnp.concatenate([gates[0], gate[...], gates[1]], 0)
+    began = jnp.concatenate([beside[ends[0]], atoms[...].astype(F32), beside[ends[1]]], 0)
+    biases, shifts = [], []
+    tail = slice(ATOM_ROWS, MESSAGE)
+    row = lax.broadcasted_iota(jnp.int32, (16, 128), 0)
+    lane = lax.broadcasted_iota(jnp.int32, (16, 128), 1)
+    for pick in (from_before, from_after):
+        group = pick(near[tail], far[tail])
+        for m in range(edge):
+            chosen = jnp.where(jnp.logical_and(row == 4, lane == m), group, 0.0)
+            value = jnp.sum(chosen).astype(jnp.int32)
+            shifts.append(jnp.clip(value, -HALO, QBLK + HALO - KWIN))
+
+            def part(c):
+                span = slice(m * 512 + c * 32, m * 512 + (c + 1) * 32)
+                return pick(near[span], far[span])
+
+            (total,) = block_bias(channel_weight, (0,), part)
+            biases.append(jnp.concatenate(total, 0))
+    biases = biases[:edge] + [bias[j] for j in range(blocks)] + biases[edge:]
+    shifts = shifts[:edge] + [shift[0, j] for j in range(blocks)] + shifts[edge:]
+    found = windows(shifts, queries, keys, values, 2 * HALO - HALO)
+    kept, attended = attention_forward(shifts, found, biases, first - HALO, atom_total)
+    for j in range(blocks):
+        chances[j] = kept[j + edge]
+    att[...] = attended[HALO : HALO + rows]
+    done = began + gates * nn(attended, weight_out[0])
+    state[...] = done[HALO : HALO + rows]
+    unit, _ = stats(done)
+    normed_all = (unit * gain[1:2, :]).astype(BF16)
+    normed[...] = normed_all[HALO : HALO + rows]
+    projected = nn(normed_all, weight_in[1])
+    place = first - HALO + lax.broadcasted_iota(jnp.int32, (rows + 2 * HALO, 1), 0)
+    inside = jnp.logical_and(place >= 0, place < atom_total)
+    kv_next[...] = jnp.where(inside, projected[:, 128:384], 0.0).astype(BF16)
+    q_next[...] = projected[HALO : HALO + rows, 0:128].astype(BF16)
+    gate_next[...] = sigmoid(projected[HALO : HALO + rows, 384:512])
 
 
 def layer_back(
@@ -345,8 +397,6 @@
     shift,
     q,
     kv,
-    near,
-    far,
     bias,
     gate,
     state,
@@ -367,21 +417,22 @@
     center,
     grad_near,
     grad_far,
-    score_own,
-    score_one,
-    score_two,
-    score_three,
+    score_grad,
     keys,
     values,
     grad_att,
     grad_keys,
     grad_values,
-    score_grad,
 ):
-    load_window(kv, near, far, keys, values)
-    found = windows(shift, q, keys, values)
-    chances = attention_forward(shift, found, bias, att, q.shape[0], atom_total)
-    update = nn(att[...], weight_out[1])
+    load_window(kv, keys, values)
+    shifts = [shift[0, j] for j in range(bias.shape[0])]
+    found = windows(shifts, q, keys, values, HALO)
+    first = lax.axis_index("seq") * q.shape[0]
+    chances, attended = attention_forward(
+        shifts, found, [bias[j] for j in range(bias.shape[0])], first, atom_total
+    )
+    att[...] = attended
+    update = nn(attended, weight_out[1])
     after = (state[...] + gate[...] * update).astype(BF16)
     narrow_state[...] = after
     tokens = grad.shape[0]
@@ -391,8 +442,9 @@
     chosen = lax.broadcasted_iota(jnp.int32, (tokens + 16, atoms), 0) == place
     chosen = jnp.where(chosen, 1.0, 0.0).astype(BF16)
     own = jnp.concatenate([grad[...], count_rows(counts[...]).astype(BF16)], 1)
-    before = from_before(near_first[HALO : HALO + 32, :], far_first[HALO : HALO + 32, :])
-    before = jnp.concatenate([before[0:16], before[16:32]], 1).astype(BF16)
+    group = from_before(near_first[ATOM_ROWS:MESSAGE, :], far_first[ATOM_ROWS:MESSAGE, :])
+    before = [jnp.broadcast_to(group[k : k + 1], (16, 128)) for k in range(4)]
+    before = jnp.concatenate(before, 1).astype(BF16)
     taken = tn(chosen, jnp.concatenate([own, before], 0))
     many = taken[:, 384:512]
     cotangent = taken[:, 0:384] / jnp.concatenate([many] * 3, 1)
@@ -405,7 +457,6 @@
     layer_back(rising, gate, att, weight_out, 1, grad_gate, grad_update, grad_att, update)
     attention_backward(found, chances, grad_att, grad_q, grad_keys, grad_values, score_grad)
     send_halo(grad_keys, grad_values, center, grad_near, grad_far)
-    share_scores(score_grad, score_own, score_one, score_two, score_three)
 
 
 def pair_weight_grad(pair, scores, out):
@@ -419,18 +470,9 @@
 
 
 def middle_weights_kernel(
-    pair, own, one, two, three, narrow_state, grad_hidden, att, grad_update, token, out, bias
+    pair, scores, narrow_state, grad_hidden, att, grad_update, token, out, bias
 ):
-    y = lax.axis_index("samp") // 2
-    pair_weight_grad(
-        pair,
-        [
-            (lax.rem(y + k, 4) * 2 + m, ref[m])
-            for k, ref in enumerate((own, one, two, three))
-            for m in range(2)
-        ],
-        bias,
-    )
+    pair_weight_grad(pair, [(j, scores[j]) for j in range(pair.shape[0])], bias)
     product = tn(narrow_state[...], grad_hidden[...])
     for m in range(3):
         token[m * 128 : (m + 1) * 128, :] = product[:, m * 128 : (m + 1) * 128]
@@ -470,8 +512,6 @@
     grad_state_later,
     q,
     kv,
-    near,
-    far,
     gate,
     att,
     weight_out,
@@ -492,8 +532,9 @@
     grad_keys,
     grad_values,
 ):
-    load_window(kv, near, far, keys, values)
-    found = windows(shift, q, keys, values)
+    load_window(kv, keys, values)
+    shifts = [shift[0, j] for j in range(chances.shape[0])]
+    found = windows(shifts, q, keys, values, HALO)
     join_projected(grad_q_later, center_later, near_later, far_later, grad_gate_later, joined)
     grad_normed = nt(joined[...], weight_in[1]).astype(BF16).astype(F32)
     back, gained = norm_back(grad_normed, state[...], gain[1:2, :])
@@ -522,10 +563,17 @@
     out_later,
     bias_later,
     gain_later,
+    scores_later,
     keep,
     send,
+    own,
+    one,
+    two,
+    three,
     whole,
 ):
+    share_scores((scores, scores_later), (own, one, two, three))
+
     def put(row, value):
         whole[row // EARLY, row % EARLY : row % EARLY + 16, :] = value
 
@@ -589,44 +637,26 @@
         ref[:, EXTRA:SPAN, :] = piece[:, 16:80].astype(ref.dtype)
 
 
-def core_kernel(keep, got, scores, own, own_scores, one, two, three, whole):
+def core_kernel(keep, got, own, one, two, three, whole):
     whole[...] = keep[...] + got[...].astype(F32)
     y = lax.axis_index("samp") // 2
     own[...] = whole[y]
-    own_scores[...] = scores[pl.ds(y * 2, 2)]
     for k, ref in enumerate((one, two, three)):
-        at = lax.rem(y + k + 1, 4)
-        ref[0:SPAN, :] = whole[at].astype(BF16)
+        ref[...] = whole[lax.rem(y + k + 1, 4)].astype(BF16)
+
+
+def far_kernel(own, one, two, three, score, score_one, score_two, score_three, message, kept, both):
+    got = [ref[...].astype(F32) for ref in (one, two, three)]
+    message[0:SPAN, :] = pair_up(own[...], got).astype(BF16)
+    for n in range(2):
         for m in range(2):
-            ref[SPAN + m * 128 : SPAN + (m + 1) * 128, :] = scores[at * 2 + m]
-
-
-def far_kernel(
-    own,
-    own_scores,
-    one,
-    two,
-    three,
-    later,
-    later_one,
-    later_two,
-    later_three,
-    message,
-    kept,
-    both,
-):
-    got = [ref[...].astype(F32) for ref in (one, two, three)]
-    message[0:SPAN, :] = pair_up(own[...], [v[0:SPAN] for v in got]).astype(BF16)
-    for m in range(2):
-        rows = slice(SPAN + m * 128, SPAN + (m + 1) * 128)
-        both[m, 0] = pair_up(own_scores[m].astype(F32), [v[rows] for v in got])
-        pieces = [ref[m].astype(F32) for ref in (later_one, later_two, later_three)]
-        both[m, 1] = pair_up(later[m].astype(F32), pieces)
+            got = [v[n * 2 + m].astype(F32) for v in (score_one, score_two, score_three)]
+            both[m, n] = pair_up(score[n * 2 + m].astype(F32), got)
     side = lax.rem(lax.axis_index("samp"), 2)
     kept[...] = both[side]
     away = both[1 - side].astype(BF16)
-    message[SPAN : SPAN + 128, :] = away[0]
-    message[SPAN + 128 : SPAN + 256, :] = away[1]
+    for n in range(2):
+        message[SPAN + n * 128 : SPAN + (n + 1) * 128, :] = away[n]
 
 
 def quarter_kernel(own, one, two, three, half):
@@ -683,7 +713,7 @@
         value = None
         for layer, ref in enumerate((first, later)):
             for h in range(HEADS):
-                term = ref[h * 32 : (h + 1) * 32, :] * weight[layer, h, c]
+                term = ref[h * 32 : (h + 1) * 32] * weight[layer, h, c]
                 value = term if value is None else value + term
         pair[c * 32 : (c + 1) * 32, :] = value.astype(BF16)
 
@@ -715,45 +745,49 @@
     wide = ((rows, 128), BF16)
     full = ((rows, 128), F32)
     kv_shape = ((rows, 256), BF16)
-    first_rim = ((HALO + 32, 256), BF16)
     rim = ((HALO, 256), BF16)
-    score_piece = ((2, 128, 128), BF16)
+    scores_shape = ((blocks, 128, 128), BF16)
     channel_weight = weight_bias.transpose(0, 2, 1)
 
-    def pair_bias(layer, *after):
-        (bias,) = run(
-            partial(bias_kernel, layer),
-            [square],
-            (channel_weight, pair, *after),
-            smem=(0,),
-            hbm=range(1, 2 + len(after)),
-            scratch=[
-                pltpu.VMEM((blocks, 512, 128), BF16),
-                pltpu.SemaphoreType.DMA((blocks,)),
-            ],
-        )
-        return bias
-
-    inputs = (atoms, norm_gain, weight_in, grad, counts)
-    normed0, q0, kv0, gate0, *rims0 = run(
-        first_kernel,
-        [wide, wide, kv_shape, full, first_rim, first_rim],
-        inputs,
+    begun = ((MESSAGE, 128), BF16)
+    *rims0, shift_row = run(
+        message_kernel,
+        [begun, begun, ((1, 128), jnp.int32)],
+        (window_shift, pair, atoms, grad, counts),
         hbm=range(5),
-        scratch=[pltpu.VMEM(v.shape, v.dtype) for v in inputs]
-        + [pltpu.SemaphoreType.DMA((len(inputs),))],
+        scratch=[
+            pltpu.SMEM(window_shift.shape, window_shift.dtype),
+            pltpu.VMEM(grad.shape, grad.dtype),
+            pltpu.VMEM(counts.shape, counts.dtype),
+            pltpu.SemaphoreType.DMA((9,)),
+        ],
+        vmem=FIRST_VMEM,
     )
     rims0 = swapped(*rims0)
-    bias0 = pair_bias(0)
-    state1, chances0, att0, normed1, q1, kv1, gate1, *rims1 = run(
+    normed0, q0, kv0, gate0 = run(
+        first_kernel, [wide, wide, kv_shape, full], (atoms, norm_gain, weight_in)
+    )
+    bias0, bias1 = run(bias_kernel, [square, square], (channel_weight, pair), smem=(0,))
+    ext_kv = ((ext, 256), BF16)
+    state1, chances0, att0, kv0, normed1, q1, kv1, gate1 = run(
         partial(forward_kernel, atom_total),
-        [full, square, wide, wide, wide, kv_shape, full, rim, rim],
-        (window_shift, q0, kv0, *rims0, bias0, gate0, atoms, weight_out, norm_gain, weight_in),
-        smem=(0,),
-        scratch=window,
-    )
-    bias1 = pair_bias(1, att0)
-    rims1 = swapped(*rims1)
+        [full, square, wide, ext_kv, wide, wide, ext_kv, full],
+        (
+            shift_row,
+            channel_weight,
+            q0,
+            kv0,
+            *rims0,
+            bias0,
+            gate0,
+            atoms,
+            weight_out,
+            norm_gain,
+            weight_in,
+        ),
+        smem=(0, 1),
+        scratch=[pltpu.VMEM((rows + 4 * HALO, 128), F32)] * 2,
+    )
     back_scratch = [
         pltpu.VMEM((rows, 128), BF16),
         pltpu.VMEM((ext, 128), F32),
@@ -770,7 +804,7 @@
         center1,
         near1,
         far1,
-        *scores1,
+        scores1,
     ) = run(
         partial(middle_kernel, atom_total),
         [
@@ -784,16 +818,12 @@
             ((rows, 256), F32),
             rim,
             rim,
-            score_piece,
-            score_piece,
-            score_piece,
-            score_piece,
+            scores_shape,
         ],
         (
-            window_shift,
+            shift_row,
             q1,
             kv1,
-            *rims1,
             bias1,
             gate1,
             state1,
@@ -805,16 +835,15 @@
             *rims0,
         ),
         smem=(0,),
-        scratch=window + back_scratch + [pltpu.VMEM((blocks, 128, 128), BF16)],
+        scratch=window + back_scratch,
     )
     rims1 = swapped(near1, far1)
-    got_one = hop(scores1[1], 3, 1)
     grad_token, grad_out1, grad_bias1 = run(
         middle_weights_kernel,
         [((384, 128), F32), ((128, 128), F32), ((16, 128), F32)],
-        (pair, *scores1, narrow_state, grad_hidden, att1, grad_update1),
-    )
-    *rims1, got_one, grad_token = lax.optimization_barrier((*rims1, got_one, grad_token))
+        (pair, scores1, narrow_state, grad_hidden, att1, grad_update1),
+    )
+    rims1, grad_token = lax.optimization_barrier((rims1, grad_token))
     (
         joined1,
         grad_gain1,
@@ -841,7 +870,7 @@
             ((blocks, 128, 128), BF16),
         ],
         (
-            window_shift,
+            shift_row,
             grad_q1,
             center1,
             *rims1,
@@ -852,7 +881,6 @@
             grad_state2,
             q0,
             kv0,
-            *rims0,
             gate0,
             att0,
             weight_out,
@@ -862,9 +890,9 @@
         scratch=window + back_scratch,
     )
     last_rims = swapped(near0, far0)
-    keep, send = run(
+    keep, send, *score_parts = run(
         backward_weights_kernel,
-        [((4, EXTRA, 128), F32), ((4, EXTRA, 128), F32)],
+        [((4, EXTRA, 128), F32), ((4, EXTRA, 128), F32)] + [((4, 128, 128), BF16)] * 4,
         (
             pair,
             scores0,
@@ -876,11 +904,10 @@
             grad_out1,
             grad_bias1,
             grad_gain1,
+            scores1,
         ),
         scratch=[pltpu.VMEM((8, EXTRA, 128), F32)],
     )
-    got_two, got_three = hop(scores1[2], 3, 2), hop(scores1[3], 3, 3)
-    *last_rims, got_two, got_three = lax.optimization_barrier((*last_rims, got_two, got_three))
     grad_atoms, keep, send = run(
         last_kernel,
         [wide, ((4, SPAN, 128), F32), ((4, SPAN, 128), BF16)],
@@ -899,26 +926,28 @@
         ),
         scratch=[pltpu.VMEM((rows, 512), BF16), pltpu.VMEM((8, 80, 128), F32)],
     )
-    message = ((SPAN + 256, 128), BF16)
-    own, own_scores, *pieces = run(
+    chunk = ((SPAN, 128), BF16)
+    own, *pieces = run(
         core_kernel,
-        [((SPAN, 128), F32), score_piece, message, message, message],
-        (keep, hop(send, 2, 1), scores0),
+        [((SPAN, 128), F32), chunk, chunk, chunk],
+        (keep, hop(send, 2, 1)),
         scratch=[pltpu.VMEM((4, SPAN, 128), F32)],
     )
-    pieces = [hop(v, 3, k + 1) for k, v in enumerate(pieces)]
-    out, kept = run(
+    score_got = [hop(score_parts[k], 3, k) for k in range(1, 4)]
+    message, kept = run(
         far_kernel,
-        [message, ((2, 128, 128), F32)],
-        (own, own_scores, *pieces, scores1[0], got_one, got_two, got_three),
+        [((SPAN + 256, 128), BF16), ((2, 128, 128), F32)],
+        (own, *[hop(v, 3, k + 1) for k, v in enumerate(pieces)], score_parts[0], *score_got),
         scratch=[pltpu.VMEM((2, 2, 128, 128), F32)],
     )
-    got = hop(out, 4, 1)
-    total = (out[0:SPAN].astype(F32) + got[0:SPAN].astype(F32)).astype(BF16)
+    far_got = hop(message, 4, 1)
+    total = (message[0:SPAN].astype(F32) + far_got[0:SPAN].astype(F32)).astype(BF16)
+    total = everyone(total, 0)
+    (pair_sum,) = run(
+        expand_kernel, [((512, 128), BF16)], (channel_weight, kept, far_got), smem=(0,)
+    )
+    total, pair_sum = lax.optimization_barrier((total, pair_sum))
     total = everyone(total, 1)
-    (pair_sum,) = run(expand_kernel, [((512, 128), BF16)], (channel_weight, kept, got), smem=(0,))
-    total, pair_sum = lax.optimization_barrier((total, pair_sum))
-    total = everyone(total, 0)
     (half,) = run(
         quarter_kernel,
         [((4, SPAN, 128), BF16)],

time: 99.4 us -> 92.6 us (0.932)
  starting transfers between devices: 54.8 us -> 46.3 us
  waiting for transfers between devices: 21.2 us -> 27.6 us
  local copies, waits for them, and re-layouts: 5.11 us -> 1.36 us
    ppermute x4 -> x3, waiting for transfers between devices: 0.96 us -> 8.77 us  [swapped(): far = lax.ppermute(far, 'seq', across)]
    ppermute x4 -> x3, starting transfers between devices: 12.7 us -> 6.34 us  [swapped(): far = lax.ppermute(far, 'seq', across)]
    unnamed x30 -> x22, local copies, waits for them, and re-layouts: 5.11 us -> 1.36 us
    ppermute x18, starting transfers between devices: 38.6 us -> 36.4 us  [hop(): return lax.ppermute(value, WORLD, moves(part, step))]
    ppermute x18, waiting for transfers between devices: 20.2 us -> 18.9 us  [hop(): return lax.ppermute(value, WORLD, moves(part, step))]
    ppermute x4 -> x3, starting transfers between devices: 3.52 us -> 3.51 us  [swapped(): return (lax.ppermute(near, 'seq', chip), far)]
  transfers between devices with their start and end apart: 26 -> 24, of which waited for: 12 -> 14; matrix products, arithmetic and copies ran while one was open for 0% -> 0% of each run, Pallas kernels for 10% -> 5%
where the time goes in v3:
time: 92.6 us; the launch traced here: 92.4 us
  starting transfers between devices  46.3 us (50%)
  waiting for transfers between devices  27.6 us (30%)
  Pallas kernels  16.1 us (17%)
  local copies, waits for them, and re-layouts  1.36 us (1%)
    ppermute x18, starting transfers between devices, hop(): return lax.ppermute(value, WORLD, moves(part, step))  36.4 us
    ppermute x18, waiting for transfers between devices, hop(): return lax.ppermute(value, WORLD, moves(part, step))  18.9 us
    pallas_call x14, Pallas kernels, run(): pl.pallas_call(body, out_shape=[jax.ShapeDtypeStruct(s, d) for s, d in ou...  16.1 us
    ppermute x3, waiting for transfers between devices, swapped(): far = lax.ppermute(far, 'seq', across)  8.77 us
    ppermute x3, starting transfers between devices, swapped(): far = lax.ppermute(far, 'seq', across)  6.34 us
    ppermute x3, starting transfers between devices, swapped(): return (lax.ppermute(near, 'seq', chip), far)  3.51 us
  transfers between devices with their start and end apart: 24, of which 14 were waited for; matrix products, arithmetic and copies ran while one was open for 0% of the time, Pallas kernels for 5%

profile of v3, /device:TPU:1, one launch (start us, length us, event | category | flops | bytes accessed | tf_op | source)
XLA Modules:
  0.0 92.4 jit_solution(6294853320795994129)
XLA Ops:
  0.6 2.1 %shard_map.162 = (bf16[1168,128]{1,0:T(8,128)(2,1)}, bf16[1168,128]{1,0:T(8,128)(2,1)}, s32[1,128]{1,0:T(1,128)}) custom-call(s32[8]{0:T(128)} %shift_far.1, bf16[8,512,128]{2,1,0:T(8,128)(2,1)} %bitcast.9, bf16[256,128]{1,0:T(8,128)(2,1)} %bitcast.13, bf16[32,384]{1,0:T(8,128)(2,1)} %bitcast.17, s32[1,32]{1,0:T(1,128)} %bitcast.22), custom_call_target="tpu_custom_call" | custom-call | flops 100000000 | bytes 1000000 | tf_op jit(solution)/shard_map/pallas_call | solution.py:68
  2.8 3.3 %collective-permute-start = (bf16[1168,128]{1,0:T(8,128)(2,1)}, bf16[1168,128]{1,0:T(8,128)(2,1)S(1)}, u32[]{:S(2)}, u32[]{:S(2)}) collective-permute-start(bf16[1168,128]{1,0:T(8,128)(2,1)} %get-tuple-element.76), channel_id=1, source_target_pairs={{0,8},{8,0},{16,24},{24,16},{32,40},{40,32},{48,56},{56,48},{64,72... | collective-permute-start | bytes 897032 | tf_op jit(solution)/shard_map/ppermute | solution.py:47
  6.1 1.9 %collective-permute-start.1 = (bf16[1168,128]{1,0:T(8,128)(2,1)}, bf16[1168,128]{1,0:T(8,128)(2,1)S(1)}, u32[]{:S(2)}, u32[]{:S(2)}) collective-permute-start(bf16[1168,128]{1,0:T(8,128)(2,1)} %get-tuple-element.77), channel_id=1, source_target_pairs={{8,16},{16,8},{24,32},{32,24},{40,48},{48,40},{56,64},{64,56},{72,... | collective-permute-start | bytes 897032 | tf_op jit(solution)/shard_map/ppermute | solution.py:46
  8.1 1.9 %shard_map.164 = (f32[8,128,128]{2,1,0:T(8,128)S(1)}, f32[8,128,128]{2,1,0:T(8,128)S(1)}) custom-call(f32[2,4,16]{2,1,0:T(4,128)S(1)} %bitcast.19, bf16[8,512,128]{2,1,0:T(8,128)(2,1)S(1)} %bitcast.10), custom_call_target="tpu_custom_call" | custom-call | flops 100000000 | bytes 1000000 | tf_op jit(solution)/shard_map/pallas_call | solution.py:68
  10.5 3.9 %collective-permute-done.1.far.far_first = bf16[1168,128]{1,0:T(8,128)(2,1)S(1)} collective-permute-done((bf16[1168,128]{1,0:T(8,128)(2,1)}, bf16[1168,128]{1,0:T(8,128)(2,1)S(1)}, u32[]{:S(2)}, u32[]{:S(2)}) %collective-permute-start.1) | collective-permute-done | bytes 299040 | tf_op jit(solution)/shard_map/ppermute | solution.py:46
  15.1 2.5 %shard_map.165 = (f32[256,128]{1,0:T(8,128)S(1)}, f32[8,128,128]{2,1,0:T(8,128)S(1)}, bf16[256,128]{1,0:T(8,128)(2,1)S(1)}, bf16[384,256]{1,0:T(8,128)(2,1)S(1)}...) custom-call(s32[1,128]{1,0:T(1,128)S(1)} %copy-done.8, ...), custom_call_target="tpu_custom_call" | custom-call | flops 100000000 | bytes 1000000 | tf_op jit(solution)/shard_map/pallas_call | solution.py:68
  18.3 2.4 %shard_map.166 = (bf16[256,128]{1,0:T(8,128)(2,1)S(1)}, bf16[256,128]{1,0:T(8,128)(2,1)S(1)}, bf16[256,128]{1,0:T(8,128)(2,1)S(1)}, bf16[256,384]{1,0:T(8,128)(2...) custom-call(s32[1,128]{1,0:T(1,128)S(1)} %copy-done.8, ...), custom_call_target="tpu_custom_call" | custom-call | flops 100000000 | bytes 1000000 | tf_op jit(solution)/shard_map/pallas_call | solution.py:68
  20.7 2.0 %collective-permute-start.3 = (bf16[64,256]{1,0:T(8,128)(2,1)S(1)}, bf16[64,256]{1,0:T(8,128)(2,1)S(1)}, u32[]{:S(2)}, u32[]{:S(2)}) collective-permute-start(bf16[64,256]{1,0:T(8,128)(2,1)S(1)} %get-tuple-element.88), channel_id=1, source_target_pairs={{8,16},{16,8},{24,32},{32,24},{40,48},{48,40},{56,64},{64,56},{72,... | collective-permute-start | bytes 98312 | tf_op jit(solution)/shard_map/ppermute | solution.py:46
  23.3 2.7 %collective-permute-done.3.far_later = bf16[64,256]{1,0:T(8,128)(2,1)S(1)} collective-permute-done((bf16[64,256]{1,0:T(8,128)(2,1)S(1)}, bf16[64,256]{1,0:T(8,128)(2,1)S(1)}, u32[]{:S(2)}, u32[]{:S(2)}) %collective-permute-start.3) | collective-permute-done | bytes 32800 | tf_op jit(solution)/shard_map/ppermute | solution.py:46
  26.0 1.8 %shard_map.168 = (bf16[256,512]{1,0:T(8,128)(2,1)S(1)}, f32[1,128]{1,0:T(1,128)S(1)}, bf16[256,128]{1,0:T(8,128)(2,1)S(1)}, f32[256,128]{1,0:T(8,128)S(1)}, bf16...) custom-call(s32[1,128]{1,0:T(1,128)S(1)} %copy-done.8, ...), custom_call_target="tpu_custom_call" | custom-call | flops 100000000 | bytes 1000000 | tf_op jit(solution)/shard_map/pallas_call | solution.py:68
  27.9 2.4 %collective-permute-start.5 = (bf16[64,256]{1,0:T(8,128)(2,1)S(1)}, bf16[64,256]{1,0:T(8,128)(2,1)S(1)}, u32[]{:S(2)}, u32[]{:S(2)}) collective-permute-start(bf16[64,256]{1,0:T(8,128)(2,1)S(1)} %get-tuple-element.105), channel_id=1, source_target_pairs={{8,16},{16,8},{24,32},{32,24},{40,48},{48,40},{56,64},{64,56},{72,... | collective-permute-start | bytes 98312 | tf_op jit(solution)/shard_map/ppermute | solution.py:46
  30.9 2.2 %collective-permute-done.5.far = bf16[64,256]{1,0:T(8,128)(2,1)S(1)} collective-permute-done((bf16[64,256]{1,0:T(8,128)(2,1)S(1)}, bf16[64,256]{1,0:T(8,128)(2,1)S(1)}, u32[]{:S(2)}, u32[]{:S(2)}) %collective-permute-start.5) | collective-permute-done | bytes 32800 | tf_op jit(solution)/shard_map/ppermute | solution.py:46
  34.2 2.2 %collective-permute-start.11 = (bf16[4,128,128]{2,1,0:T(8,128)(2,1)S(1)}, bf16[4,128,128]{2,1,0:T(8,128)(2,1)S(1)}, u32[]{:S(2)}, u32[]{:S(2)}) collective-permute-start(bf16[4,128,128]{2,1,0:T(8,128)(2,1)S(1)} %get-tuple-element.128), channel_id=1, source_target_pairs={{0,4},{1,5},{2,6},{3,7},{4,0},{5,1},{6,2},{7,3},{8,12},{9,13},{10,... | collective-permute-start | bytes 393224 | tf_op jit(solution)/shard_map/ppermute | solution.py:38
  38.0 1.5 %collective-permute-start.8 = (bf16[224,128]{1,0:T(8,128)(2,1)S(1)}, bf16[224,128]{1,0:T(8,128)(2,1)S(1)}, u32[]{:S(2)}, u32[]{:S(2)}) collective-permute-start(bf16[224,128]{1,0:T(8,128)(2,1)S(1)} %get-tuple-element.124), channel_id=1, source_target_pairs={{0,4},{1,5},{2,6},{3,7},{4,0},{5,1},{6,2},{7,3},{8,12},{9,13},{10,... | collective-permute-start | bytes 172040 | tf_op jit(solution)/shard_map/ppermute | solution.py:38
  43.7 2.2 %collective-permute-done.7.one = bf16[224,128]{1,0:T(8,128)(2,1)S(1)} collective-permute-done((bf16[224,128]{1,0:T(8,128)(2,1)S(1)}, bf16[224,128]{1,0:T(8,128)(2,1)S(1)}, u32[]{:S(2)}, u32[]{:S(2)}) %collective-permute-start.7) | collective-permute-done | bytes 57376 | tf_op jit(solution)/shard_map/ppermute | solution.py:38
  46.0 5.6 %collective-permute-start.13 = (bf16[480,128]{1,0:T(8,128)(2,1)S(1)}, bf16[480,128]{1,0:T(8,128)(2,1)S(1)}, u32[]{:S(2)}, u32[]{:S(2)}) collective-permute-start(bf16[480,128]{1,0:T(8,128)(2,1)S(1)} %get-tuple-element.130), channel_id=1, source_target_pairs={{0,1},{1,0},{2,3},{3,2},{4,5},{5,4},{6,7},{7,6},{8,9},{9,8},{10,11... | collective-permute-start | bytes 368648 | tf_op jit(solution)/shard_map/ppermute | solution.py:38
  51.6 2.3 %collective-permute-done.13.got = bf16[480,128]{1,0:T(8,128)(2,1)S(1)} collective-permute-done((bf16[480,128]{1,0:T(8,128)(2,1)S(1)}, bf16[480,128]{1,0:T(8,128)(2,1)S(1)}, u32[]{:S(2)}, u32[]{:S(2)}) %collective-permute-start.13) | collective-permute-done | bytes 122912 | tf_op jit(solution)/shard_map/ppermute | solution.py:38
  53.9 10.5 %collective-permute-start.16 = (bf16[224,128]{1,0:T(8,128)(2,1)S(1)}, bf16[224,128]{1,0:T(8,128)(2,1)S(1)}, u32[]{:S(2)}, u32[]{:S(2)}) collective-permute-start(bf16[224,128]{1,0:T(8,128)(2,1)S(1)} %add_convert_fusion.2), channel_id=1, source_target_pairs={{0,192},{1,193},{2,194},{3,195},{4,196},{5,197},{6,198},{7,199},{8... | collective-permute-start | bytes 172040 | tf_op jit(solution)/shard_map/ppermute | solution.py:38
  66.4 2.9 %collective-permute-done.15 = bf16[224,128]{1,0:T(8,128)(2,1)S(1)} collective-permute-done((bf16[224,128]{1,0:T(8,128)(2,1)S(1)}, bf16[224,128]{1,0:T(8,128)(2,1)S(1)}, u32[]{:S(2)}, u32[]{:S(2)}) %collective-permute-start.15) | collective-permute-done | bytes 57376 | tf_op jit(solution)/shard_map/ppermute | solution.py:38
  69.3 3.9 %collective-permute-start.19 = (bf16[224,128]{1,0:T(8,128)(2,1)S(1)}, bf16[224,128]{1,0:T(8,128)(2,1)S(1)}, u32[]{:S(2)}, u32[]{:S(2)}) collective-permute-start(bf16[224,128]{1,0:T(8,128)(2,1)S(1)} %add_convert_fusion.1), channel_id=1, source_target_pairs={{0,48},{1,49},{2,50},{3,51},{4,52},{5,53},{6,54},{7,55},{8,56},{9,... | collective-permute-start | bytes 172040 | tf_op jit(solution)/shard_map/ppermute | solution.py:38
  74.5 3.6 %collective-permute-done.18 = bf16[224,128]{1,0:T(8,128)(2,1)S(1)} collective-permute-done((bf16[224,128]{1,0:T(8,128)(2,1)S(1)}, bf16[224,128]{1,0:T(8,128)(2,1)S(1)}, u32[]{:S(2)}, u32[]{:S(2)}) %collective-permute-start.18) | collective-permute-done | bytes 57376 | tf_op jit(solution)/shard_map/ppermute | solution.py:38
  78.2 2.4 %collective-permute-start.21 = (bf16[224,128]{1,0:T(8,128)(2,1)S(1)}, bf16[224,128]{1,0:T(8,128)(2,1)S(1)}, u32[]{:S(2)}, u32[]{:S(2)}) collective-permute-start(bf16[224,128]{1,0:T(8,128)(2,1)S(1)} %add_convert_fusion.own), channel_id=1, source_target_pairs={{0,4},{1,5},{2,6},{3,7},{4,0},{5,1},{6,2},{7,3},{8,12},{9,13},{10,... | collective-permute-start | bytes 172040 | tf_op jit(solution)/shard_map/ppermute | solution.py:38
  82.9 2.1 %collective-permute-done.20.one = bf16[224,128]{1,0:T(8,128)(2,1)S(1)} collective-permute-done((bf16[224,128]{1,0:T(8,128)(2,1)S(1)}, bf16[224,128]{1,0:T(8,128)(2,1)S(1)}, u32[]{:S(2)}, u32[]{:S(2)}) %collective-permute-start.20) | collective-permute-done | bytes 57376 | tf_op jit(solution)/shard_map/ppermute | solution.py:38
  85.0 5.2 %collective-permute-start.23 = (bf16[4,224,128]{2,1,0:T(8,128)(2,1)S(1)}, bf16[4,224,128]{2,1,0:T(8,128)(2,1)S(1)}, u32[]{:S(2)}, u32[]{:S(2)}) collective-permute-start(bf16[4,224,128]{2,1,0:T(8,128)(2,1)S(1)} %shard_map.174.half), channel_id=1, source_target_pairs={{0,8},{1,9},{2,10},{3,11},{4,12},{5,13},{6,14},{7,15},{8,0},{9,1},... | collective-permute-start | bytes 688136 | tf_op jit(solution)/shard_map/ppermute | solution.py:38
  (63 shorter events, 17.9 us)
Async XLA Ops:
  2.8 7.7 %collective-permute-start = (bf16[1168,128]{1,0:T(8,128)(2,1)}, bf16[1168,128]{1,0:T(8,128)(2,1)S(1)}, u32[]{:S(2)}, u32[]{:S(2)}) collective-permute-start(bf16[1168,128]{1,0:T(8,128)(2,1)} %get-tuple-element.76), channel_id=1, source_target_pairs={{0,8},{8,0},{16,24},{24,16},{32,40},{40,32},{48,56},{56,48},{64,72... | collective-permute-start | bytes 897032 | tf_op jit(solution)/shard_map/ppermute | solution.py:47
  6.1 8.3 %collective-permute-start.1 = (bf16[1168,128]{1,0:T(8,128)(2,1)}, bf16[1168,128]{1,0:T(8,128)(2,1)S(1)}, u32[]{:S(2)}, u32[]{:S(2)}) collective-permute-start(bf16[1168,128]{1,0:T(8,128)(2,1)} %get-tuple-element.77), channel_id=1, source_target_pairs={{8,16},{16,8},{24,32},{32,24},{40,48},{48,40},{56,64},{64,56},{72,... | collective-permute-start | bytes 897032 | tf_op jit(solution)/shard_map/ppermute | solution.py:46
  20.6 2.7 %collective-permute-start.2 = (bf16[64,256]{1,0:T(8,128)(2,1)S(1)}, bf16[64,256]{1,0:T(8,128)(2,1)S(1)}, u32[]{:S(2)}, u32[]{:S(2)}) collective-permute-start(bf16[64,256]{1,0:T(8,128)(2,1)S(1)} %get-tuple-element.87), channel_id=1, source_target_pairs={{0,8},{8,0},{16,24},{24,16},{32,40},{40,32},{48,56},{56,48},{64,72... | collective-permute-start | bytes 98312 | tf_op jit(solution)/shard_map/ppermute | solution.py:47
  20.7 5.2 %collective-permute-start.3 = (bf16[64,256]{1,0:T(8,128)(2,1)S(1)}, bf16[64,256]{1,0:T(8,128)(2,1)S(1)}, u32[]{:S(2)}, u32[]{:S(2)}) collective-permute-start(bf16[64,256]{1,0:T(8,128)(2,1)S(1)} %get-tuple-element.88), channel_id=1, source_target_pairs={{8,16},{16,8},{24,32},{32,24},{40,48},{48,40},{56,64},{64,56},{72,... | collective-permute-start | bytes 98312 | tf_op jit(solution)/shard_map/ppermute | solution.py:46
  27.8 3.1 %collective-permute-start.4 = (bf16[64,256]{1,0:T(8,128)(2,1)S(1)}, bf16[64,256]{1,0:T(8,128)(2,1)S(1)}, u32[]{:S(2)}, u32[]{:S(2)}) collective-permute-start(bf16[64,256]{1,0:T(8,128)(2,1)S(1)} %get-tuple-element.104), channel_id=1, source_target_pairs={{0,8},{8,0},{16,24},{24,16},{32,40},{40,32},{48,56},{56,48},{64,72... | collective-permute-start | bytes 98312 | tf_op jit(solution)/shard_map/ppermute | solution.py:47
  27.9 5.2 %collective-permute-start.5 = (bf16[64,256]{1,0:T(8,128)(2,1)S(1)}, bf16[64,256]{1,0:T(8,128)(2,1)S(1)}, u32[]{:S(2)}, u32[]{:S(2)}) collective-permute-start(bf16[64,256]{1,0:T(8,128)(2,1)S(1)} %get-tuple-element.105), channel_id=1, source_target_pairs={{8,16},{16,8},{24,32},{32,24},{40,48},{48,40},{56,64},{64,56},{72,... | collective-permute-start | bytes 98312 | tf_op jit(solution)/shard_map/ppermute | solution.py:46
  34.2 3.3 %collective-permute-start.6 = (bf16[4,224,128]{2,1,0:T(8,128)(2,1)S(1)}, bf16[4,224,128]{2,1,0:T(8,128)(2,1)S(1)}, u32[]{:S(2)}, u32[]{:S(2)}) collective-permute-start(bf16[4,224,128]{2,1,0:T(8,128)(2,1)S(1)} %get-tuple-element.121), channel_id=1, source_target_pairs={{0,8},{1,9},{2,10},{3,11},{4,12},{5,13},{6,14},{7,15},{8,0},{9,1},... | collective-permute-start | bytes 688136 | tf_op jit(solution)/shard_map/ppermute | solution.py:38
  34.2 6.3 %collective-permute-start.10 = (bf16[4,128,128]{2,1,0:T(8,128)(2,1)S(1)}, bf16[4,128,128]{2,1,0:T(8,128)(2,1)S(1)}, u32[]{:S(2)}, u32[]{:S(2)}) collective-permute-start(bf16[4,128,128]{2,1,0:T(8,128)(2,1)S(1)} %get-tuple-element.127), channel_id=1, source_target_pairs={{0,2},{1,3},{2,4},{3,5},{4,6},{5,7},{6,0},{7,1},{8,10},{9,11},{10,... | collective-permute-start | bytes 393224 | tf_op jit(solution)/shard_map/ppermute | solution.py:38
  34.2 8.1 %collective-permute-start.11 = (bf16[4,128,128]{2,1,0:T(8,128)(2,1)S(1)}, bf16[4,128,128]{2,1,0:T(8,128)(2,1)S(1)}, u32[]{:S(2)}, u32[]{:S(2)}) collective-permute-start(bf16[4,128,128]{2,1,0:T(8,128)(2,1)S(1)} %get-tuple-element.128), channel_id=1, source_target_pairs={{0,4},{1,5},{2,6},{3,7},{4,0},{5,1},{6,2},{7,3},{8,12},{9,13},{10,... | collective-permute-start | bytes 393224 | tf_op jit(solution)/shard_map/ppermute | solution.py:38
  36.4 7.3 %collective-permute-start.12 = (bf16[4,128,128]{2,1,0:T(8,128)(2,1)S(1)}, bf16[4,128,128]{2,1,0:T(8,128)(2,1)S(1)}, u32[]{:S(2)}, u32[]{:S(2)}) collective-permute-start(bf16[4,128,128]{2,1,0:T(8,128)(2,1)S(1)} %get-tuple-element.129), channel_id=1, source_target_pairs={{0,6},{1,7},{2,0},{3,1},{4,2},{5,3},{6,4},{7,5},{8,14},{9,15},{10,... | collective-permute-start | bytes 393224 | tf_op jit(solution)/shard_map/ppermute | solution.py:38
  37.6 8.3 %collective-permute-start.7 = (bf16[224,128]{1,0:T(8,128)(2,1)S(1)}, bf16[224,128]{1,0:T(8,128)(2,1)S(1)}, u32[]{:S(2)}, u32[]{:S(2)}) collective-permute-start(bf16[224,128]{1,0:T(8,128)(2,1)S(1)} %get-tuple-element.123), channel_id=1, source_target_pairs={{0,2},{1,3},{2,4},{3,5},{4,6},{5,7},{6,0},{7,1},{8,10},{9,11},{10,... | collective-permute-start | bytes 172040 | tf_op jit(solution)/shard_map/ppermute | solution.py:38
  38.0 7.8 %collective-permute-start.8 = (bf16[224,128]{1,0:T(8,128)(2,1)S(1)}, bf16[224,128]{1,0:T(8,128)(2,1)S(1)}, u32[]{:S(2)}, u32[]{:S(2)}) collective-permute-start(bf16[224,128]{1,0:T(8,128)(2,1)S(1)} %get-tuple-element.124), channel_id=1, source_target_pairs={{0,4},{1,5},{2,6},{3,7},{4,0},{5,1},{6,2},{7,3},{8,12},{9,13},{10,... | collective-permute-start | bytes 172040 | tf_op jit(solution)/shard_map/ppermute | solution.py:38
  40.5 5.4 %collective-permute-start.9 = (bf16[224,128]{1,0:T(8,128)(2,1)S(1)}, bf16[224,128]{1,0:T(8,128)(2,1)S(1)}, u32[]{:S(2)}, u32[]{:S(2)}) collective-permute-start(bf16[224,128]{1,0:T(8,128)(2,1)S(1)} %get-tuple-element.125), channel_id=1, source_target_pairs={{0,6},{1,7},{2,0},{3,1},{4,2},{5,3},{6,4},{7,5},{8,14},{9,15},{10,... | collective-permute-start | bytes 172040 | tf_op jit(solution)/shard_map/ppermute | solution.py:38
  46.0 7.8 %collective-permute-start.13 = (bf16[480,128]{1,0:T(8,128)(2,1)S(1)}, bf16[480,128]{1,0:T(8,128)(2,1)S(1)}, u32[]{:S(2)}, u32[]{:S(2)}) collective-permute-start(bf16[480,128]{1,0:T(8,128)(2,1)S(1)} %get-tuple-element.130), channel_id=1, source_target_pairs={{0,1},{1,0},{2,3},{3,2},{4,5},{5,4},{6,7},{7,6},{8,9},{9,8},{10,11... | collective-permute-start | bytes 368648 | tf_op jit(solution)/shard_map/ppermute | solution.py:38
  53.9 12.5 %collective-permute-start.16 = (bf16[224,128]{1,0:T(8,128)(2,1)S(1)}, bf16[224,128]{1,0:T(8,128)(2,1)S(1)}, u32[]{:S(2)}, u32[]{:S(2)}) collective-permute-start(bf16[224,128]{1,0:T(8,128)(2,1)S(1)} %add_convert_fusion.2), channel_id=1, source_target_pairs={{0,192},{1,193},{2,194},{3,195},{4,196},{5,197},{6,198},{7,199},{8... | collective-permute-start | bytes 172040 | tf_op jit(solution)/shard_map/ppermute | solution.py:38
  64.4 4.9 %collective-permute-start.15 = (bf16[224,128]{1,0:T(8,128)(2,1)S(1)}, bf16[224,128]{1,0:T(8,128)(2,1)S(1)}, u32[]{:S(2)}, u32[]{:S(2)}) collective-permute-start(bf16[224,128]{1,0:T(8,128)(2,1)S(1)} %add_convert_fusion.2), channel_id=1, source_target_pairs={{0,64},{1,65},{2,66},{3,67},{4,68},{5,69},{6,70},{7,71},{8,72},{9,... | collective-permute-start | bytes 172040 | tf_op jit(solution)/shard_map/ppermute | solution.py:38
  64.4 4.9 %collective-permute-start.14 = (bf16[224,128]{1,0:T(8,128)(2,1)S(1)}, bf16[224,128]{1,0:T(8,128)(2,1)S(1)}, u32[]{:S(2)}, u32[]{:S(2)}) collective-permute-start(bf16[224,128]{1,0:T(8,128)(2,1)S(1)} %add_convert_fusion.2), channel_id=1, source_target_pairs={{0,128},{1,129},{2,130},{3,131},{4,132},{5,133},{6,134},{7,135},{8... | collective-permute-start | bytes 172040 | tf_op jit(solution)/shard_map/ppermute | solution.py:38
  69.3 5.2 %collective-permute-start.19 = (bf16[224,128]{1,0:T(8,128)(2,1)S(1)}, bf16[224,128]{1,0:T(8,128)(2,1)S(1)}, u32[]{:S(2)}, u32[]{:S(2)}) collective-permute-start(bf16[224,128]{1,0:T(8,128)(2,1)S(1)} %add_convert_fusion.1), channel_id=1, source_target_pairs={{0,48},{1,49},{2,50},{3,51},{4,52},{5,53},{6,54},{7,55},{8,56},{9,... | collective-permute-start | bytes 172040 | tf_op jit(solution)/shard_map/ppermute | solution.py:38
  73.3 4.9 %collective-permute-start.18 = (bf16[224,128]{1,0:T(8,128)(2,1)S(1)}, bf16[224,128]{1,0:T(8,128)(2,1)S(1)}, u32[]{:S(2)}, u32[]{:S(2)}) collective-permute-start(bf16[224,128]{1,0:T(8,128)(2,1)S(1)} %add_convert_fusion.1), channel_id=1, source_target_pairs={{0,16},{1,17},{2,18},{3,19},{4,20},{5,21},{6,22},{7,23},{8,24},{9,... | collective-permute-start | bytes 172040 | tf_op jit(solution)/shard_map/ppermute | solution.py:38
  73.3 4.9 %collective-permute-start.17 = (bf16[224,128]{1,0:T(8,128)(2,1)S(1)}, bf16[224,128]{1,0:T(8,128)(2,1)S(1)}, u32[]{:S(2)}, u32[]{:S(2)}) collective-permute-start(bf16[224,128]{1,0:T(8,128)(2,1)S(1)} %add_convert_fusion.1), channel_id=1, source_target_pairs={{0,32},{1,33},{2,34},{3,35},{4,36},{5,37},{6,38},{7,39},{8,40},{9,... | collective-permute-start | bytes 172040 | tf_op jit(solution)/shard_map/ppermute | solution.py:38
  78.2 3.3 %collective-permute-start.22 = (bf16[224,128]{1,0:T(8,128)(2,1)S(1)}, bf16[224,128]{1,0:T(8,128)(2,1)S(1)}, u32[]{:S(2)}, u32[]{:S(2)}) collective-permute-start(bf16[224,128]{1,0:T(8,128)(2,1)S(1)} %add_convert_fusion.own), channel_id=1, source_target_pairs={{0,6},{1,7},{2,0},{3,1},{4,2},{5,3},{6,4},{7,5},{8,14},{9,15},{10,... | collective-permute-start | bytes 172040 | tf_op jit(solution)/shard_map/ppermute | solution.py:38
  78.2 4.6 %collective-permute-start.21 = (bf16[224,128]{1,0:T(8,128)(2,1)S(1)}, bf16[224,128]{1,0:T(8,128)(2,1)S(1)}, u32[]{:S(2)}, u32[]{:S(2)}) collective-permute-start(bf16[224,128]{1,0:T(8,128)(2,1)S(1)} %add_convert_fusion.own), channel_id=1, source_target_pairs={{0,4},{1,5},{2,6},{3,7},{4,0},{5,1},{6,2},{7,3},{8,12},{9,13},{10,... | collective-permute-start | bytes 172040 | tf_op jit(solution)/shard_map/ppermute | solution.py:38
  80.7 4.2 %collective-permute-start.20 = (bf16[224,128]{1,0:T(8,128)(2,1)S(1)}, bf16[224,128]{1,0:T(8,128)(2,1)S(1)}, u32[]{:S(2)}, u32[]{:S(2)}) collective-permute-start(bf16[224,128]{1,0:T(8,128)(2,1)S(1)} %add_convert_fusion.own), channel_id=1, source_target_pairs={{0,2},{1,3},{2,4},{3,5},{4,6},{5,7},{6,0},{7,1},{8,10},{9,11},{10,... | collective-permute-start | bytes 172040 | tf_op jit(solution)/shard_map/ppermute | solution.py:38
  85.0 6.4 %collective-permute-start.23 = (bf16[4,224,128]{2,1,0:T(8,128)(2,1)S(1)}, bf16[4,224,128]{2,1,0:T(8,128)(2,1)S(1)}, u32[]{:S(2)}, u32[]{:S(2)}) collective-permute-start(bf16[4,224,128]{2,1,0:T(8,128)(2,1)S(1)} %shard_map.174.half), channel_id=1, source_target_pairs={{0,8},{1,9},{2,10},{3,11},{4,12},{5,13},{6,14},{7,15},{8,0},{9,1},... | collective-permute-start | bytes 688136 | tf_op jit(solution)/shard_map/ppermute | solution.py:38
  (11 other events, 30.0 us)

commit v4 on v3

--- a/solution.py
+++ b/solution.py
@@ -252,14 +252,20 @@
         place = first + (j * QBLK + shifts[j]) + lane
         inside = jnp.logical_and(place >= 0, place < atom_total)
         weights = jnp.where(inside, jnp.exp(scores[j] * (32.0**-0.5) + bias[j]), 0.0)
-        chances.append(weights * (1.0 / jnp.sum(weights, -1, keepdims=True)))
+        query = first + j * QBLK
+        real = jnp.logical_and(query >= 0, query < atom_total)
+        size = jnp.where(real, jnp.sum(weights, -1, keepdims=True), 1.0)
+        chances.append(weights * (1.0 / size))
     out = [nn(chances[j].astype(BF16), value[j]) for j in range(count)]
     return chances, jnp.concatenate([picked(v, mask) for v in out], 0).astype(BF16)
 
 
-def attention_backward(found, chances, grad_att, grad_q, grad_keys, grad_values, score_grad):
+def attention_backward(
+    found, chances, grad_att, edge, grad_q, grad_keys, grad_values, score_grad
+):
     spans, wide, key, value = found
     count = len(wide)
+    own = range(edge, count - edge)
     mask = head_mask(128)
     out = [stacked(grad_att[j * QBLK : (j + 1) * QBLK, :], mask) for j in range(count)]
     rising = [nt(out[j], value[j]) for j in range(count)]
@@ -268,12 +274,13 @@
     for j in range(count):
         term = chances[j] * rising[j].astype(BF16).astype(F32)
         grad_score = term - chances[j] * jnp.sum(term, -1, keepdims=True)
-        score_grad[j] = grad_score.astype(BF16)
+        if j in own:
+            score_grad[j - edge] = grad_score.astype(BF16)
         scaled.append((grad_score * (32.0**-0.5)).astype(BF16))
-    query_back = [nn(scaled[j], key[j]) for j in range(count)]
+    query_back = [nn(scaled[j], key[j]) for j in own]
     key_back = [tn(scaled[j], wide[j]) for j in range(count)]
-    for j in range(count):
-        grad_q[j * QBLK : (j + 1) * QBLK, :] = picked(query_back[j], mask).astype(BF16)
+    for n, value in enumerate(query_back):
+        grad_q[n * QBLK : (n + 1) * QBLK, 0:128] = picked(value, mask).astype(BF16)
     grad_keys[...] = jnp.zeros_like(grad_keys)
     grad_values[...] = jnp.zeros_like(grad_values)
     for j in range(count):
@@ -306,6 +313,9 @@
     chances,
     att,
     kv_all,
+    q_all,
+    gate_all,
+    shift_all,
     normed,
     q_next,
     kv_next,
@@ -325,13 +335,15 @@
         ref[0 : 2 * HALO, :] = projected[0 : 2 * HALO, at : at + 128].astype(BF16).astype(F32)
         ref[2 * HALO : 2 * HALO + rows, :] = kv[:, at - 128 : at].astype(F32)
         ref[2 * HALO + rows :, :] = projected[2 * HALO :, at : at + 128].astype(BF16).astype(F32)
-    kv_all[:, 0:128] = keys[HALO : 3 * HALO + rows, :].astype(BF16)
-    kv_all[:, 128:256] = values[HALO : 3 * HALO + rows, :].astype(BF16)
+    kv_all[:, 0:128] = keys[...].astype(BF16)
+    kv_all[:, 128:256] = values[...].astype(BF16)
     ends = slice(HALO, 2 * HALO), slice(2 * HALO, 3 * HALO)
     queries = [projected[end, 0:128].astype(BF16) for end in ends]
     queries = jnp.concatenate([queries[0], q[...], queries[1]], 0)
     gates = [sigmoid(projected[end, 384:512]) for end in ends]
     gates = jnp.concatenate([gates[0], gate[...], gates[1]], 0)
+    q_all[...] = queries
+    gate_all[...] = gates
     began = jnp.concatenate([beside[ends[0]], atoms[...].astype(F32), beside[ends[1]]], 0)
     biases, shifts = [], []
     tail = slice(ATOM_ROWS, MESSAGE)
@@ -352,13 +364,18 @@
             biases.append(jnp.concatenate(total, 0))
     biases = biases[:edge] + [bias[j] for j in range(blocks)] + biases[edge:]
     shifts = shifts[:edge] + [shift[0, j] for j in range(blocks)] + shifts[edge:]
+    lanes = lax.broadcasted_iota(jnp.int32, (1, 128), 1)
+    row_of = jnp.zeros((1, 128), jnp.int32)
+    for j, value in enumerate(shifts):
+        row_of = jnp.where(lanes == j, value, row_of)
+    shift_all[...] = row_of
     found = windows(shifts, queries, keys, values, 2 * HALO - HALO)
     kept, attended = attention_forward(shifts, found, biases, first - HALO, atom_total)
-    for j in range(blocks):
-        chances[j] = kept[j + edge]
-    att[...] = attended[HALO : HALO + rows]
+    for j, chance in enumerate(kept):
+        chances[j] = chance
+    att[...] = attended
     done = began + gates * nn(attended, weight_out[0])
-    state[...] = done[HALO : HALO + rows]
+    state[...] = done
     unit, _ = stats(done)
     normed_all = (unit * gain[1:2, :]).astype(BF16)
     normed[...] = normed_all[HALO : HALO + rows]
@@ -370,25 +387,20 @@
     gate_next[...] = sigmoid(projected[HALO : HALO + rows, 384:512])
 
 
-def layer_back(
-    grad_state, gate, att, weight_out, layer, grad_gate, grad_update, grad_att, update=None
-):
-    if update is None:
-        update = nn(att[...], weight_out[layer])
-    gates = gate[...]
-    grad_gate[...] = (grad_state * update * gates * (1.0 - gates)).astype(BF16)
-    change = (grad_state * gates).astype(BF16)
-    grad_update[...] = change
-    grad_att[...] = nt(change, weight_out[layer]).astype(BF16)
-
-
-def send_halo(grad_keys, grad_values, center, near, far):
+def send_halo(grad_keys, grad_values, grad_q, grad_gate, grad_state, center, outgoing, near, far):
     rows = center.shape[0]
-    odd = odd_core()
+    ends = []
+    for own, other in ((slice(0, HALO), 0), (slice(rows - HALO, rows), HALO + rows)):
+        there = slice(other, other + HALO)
+        here = slice(HALO + own.start, HALO + own.stop)
+        parts = [grad_keys[there, :], grad_values[there, :], grad_keys[here, :]]
+        parts += [grad_values[here, :], grad_q[own, :].astype(F32), grad_gate[own, :].astype(F32)]
+        ends.append(jnp.concatenate([*parts, grad_state[own, :]], 1))
+    near[...] = jnp.where(odd_core(), ends[0], ends[1]).astype(BF16)
+    far[...] = jnp.where(odd_core(), ends[1], ends[0]).astype(BF16)
+    outgoing[0:HALO, :] = ends[0][:, 0:256].astype(BF16)
+    outgoing[HALO:, :] = ends[1][:, 0:256].astype(BF16)
     for ref, at in ((grad_keys, 0), (grad_values, 128)):
-        before, after = ref[0:HALO, :], ref[HALO + rows : HALO + rows + HALO, :]
-        near[:, at : at + 128] = jnp.where(odd, before, after).astype(BF16)
-        far[:, at : at + 128] = jnp.where(odd, after, before).astype(BF16)
         center[:, at : at + 128] = ref[HALO : HALO + rows, :]
 
 
@@ -415,17 +427,17 @@
     grad_gate,
     grad_q,
     center,
+    outgoing,
     grad_near,
     grad_far,
     score_grad,
     keys,
     values,
-    grad_att,
     grad_keys,
     grad_values,
 ):
     load_window(kv, keys, values)
-    shifts = [shift[0, j] for j in range(bias.shape[0])]
+    shifts = [shift[0, j + HALO // QBLK] for j in range(bias.shape[0])]
     found = windows(shifts, q, keys, values, HALO)
     first = lax.axis_index("seq") * q.shape[0]
     chances, attended = attention_forward(
@@ -433,7 +445,7 @@
     )
     att[...] = attended
     update = nn(attended, weight_out[1])
-    after = (state[...] + gate[...] * update).astype(BF16)
+    after = (state[HALO : HALO + q.shape[0], :] + gate[...] * update).astype(BF16)
     narrow_state[...] = after
     tokens = grad.shape[0]
     atoms = q.shape[0]
@@ -454,9 +466,23 @@
     grad_hidden[...] = back
     rising = nt(back, weight_token[...]).astype(BF16).astype(F32)
     grad_state[...] = rising
-    layer_back(rising, gate, att, weight_out, 1, grad_gate, grad_update, grad_att, update)
-    attention_backward(found, chances, grad_att, grad_q, grad_keys, grad_values, score_grad)
-    send_halo(grad_keys, grad_values, center, grad_near, grad_far)
+    gates = gate[...]
+    grad_gate[...] = (rising * update * gates * (1.0 - gates)).astype(BF16)
+    change = (rising * gates).astype(BF16)
+    grad_update[...] = change
+    grad_att = nt(change, weight_out[1]).astype(BF16)
+    attention_backward(found, chances, grad_att, 0, grad_q, grad_keys, grad_values, score_grad)
+    send_halo(
+        grad_keys,
+        grad_values,
+        grad_q,
+        grad_gate,
+        grad_state,
+        center,
+        outgoing,
+        grad_near,
+        grad_far,
+    )
 
 
 def pair_weight_grad(pair, scores, out):
@@ -479,32 +505,22 @@
     out[...] = tn(att[...], grad_update[...])
 
 
-def join_projected(grad_q, center, near, far, grad_gate, joined):
-    rows = center.shape[0]
-    joined[:, 0:128] = grad_q[...]
-    joined[:, 384:512] = grad_gate[...]
-    below, above = from_before(near[...], far[...]), from_after(near[...], far[...])
-    joined[0:HALO, 128:384] = (center[0:HALO, :] + below).astype(BF16)
-    joined[HALO : rows - HALO, 128:384] = center[HALO : rows - HALO, :].astype(BF16)
-    joined[rows - HALO : rows, 128:384] = (center[rows - HALO : rows, :] + above).astype(BF16)
-
-
 def norm_back(grad_normed, state, gain):
     unit, scale = stats(state)
-    grad_gain = jnp.sum(grad_normed * unit, 0, keepdims=True)
     back = grad_normed * gain
     back = scale * (
         back - jnp.mean(back, -1, keepdims=True) - unit * jnp.mean(back * unit, -1, keepdims=True)
     )
-    return back, grad_gain
+    return back, grad_normed * unit
 
 
 def backward_kernel(
     shift,
     grad_q_later,
     center_later,
-    near_later,
-    far_later,
+    outgoing,
+    near,
+    far,
     grad_gate_later,
     state,
     gain,
@@ -516,35 +532,59 @@
     att,
     weight_out,
     chances,
+    atoms,
+    joined_later,
     joined,
     grad_gain,
     grad_update,
-    grad_state,
-    grad_gate,
-    grad_q,
-    center,
-    grad_near,
-    grad_far,
     score_grad,
+    grad_atoms,
+    joined_all,
     keys,
     values,
-    grad_att,
     grad_keys,
     grad_values,
 ):
+    rows = center_later.shape[0]
+    edge = HALO // QBLK
+    own = slice(HALO, HALO + rows)
     load_window(kv, keys, values)
+    before, after = from_before(near[...], far[...]), from_after(near[...], far[...])
+    for place, part, other in ((0, before, 0), (HALO + rows, after, HALO)):
+        there = slice(place, place + HALO)
+        joined_all[there, 0:128] = part[:, 512:640].astype(BF16)
+        shares = part[:, 256:512] + outgoing[other : other + HALO, :].astype(F32)
+        joined_all[there, 128:384] = shares.astype(BF16)
+        joined_all[there, 384:512] = part[:, 640:768].astype(BF16)
+    received = jnp.concatenate(
+        [before[:, 0:256], jnp.zeros((rows - 2 * HALO, 256), F32), after[:, 0:256]], 0
+    )
+    joined_all[own, 0:128] = grad_q_later[...]
+    joined_all[own, 128:384] = (center_later[...] + received).astype(BF16)
+    joined_all[own, 384:512] = grad_gate_later[...]
+    joined_later[...] = joined_all[own, :]
+    grad_normed = nt(joined_all[...], weight_in[1]).astype(BF16).astype(F32)
+    back, gained = norm_back(grad_normed, state[...], gain[1:2, :])
+    grad_gain[1:2, :] = jnp.sum(gained[own], 0, keepdims=True)
+    rising = [before[:, 768:896], grad_state_later[...], after[:, 768:896]]
+    rising = jnp.concatenate(rising, 0) + back
+    change = (rising * gate[...]).astype(BF16)
+    grad_update[...] = change[own]
+    grad_att = nt(change, weight_out[0]).astype(BF16)
+    gates = gate[own, :]
+    update = nn(att[own, :], weight_out[0])
+    joined[:, 384:512] = (rising[own] * update * gates * (1.0 - gates)).astype(BF16)
     shifts = [shift[0, j] for j in range(chances.shape[0])]
     found = windows(shifts, q, keys, values, HALO)
-    join_projected(grad_q_later, center_later, near_later, far_later, grad_gate_later, joined)
-    grad_normed = nt(joined[...], weight_in[1]).astype(BF16).astype(F32)
-    back, gained = norm_back(grad_normed, state[...], gain[1:2, :])
-    grad_gain[...] = gained
-    rising = grad_state_later[...] + back
-    grad_state[...] = rising
-    layer_back(rising, gate, att, weight_out, 0, grad_gate, grad_update, grad_att)
     kept = [chances[j] for j in range(chances.shape[0])]
-    attention_backward(found, kept, grad_att, grad_q, grad_keys, grad_values, score_grad)
-    send_halo(grad_keys, grad_values, center, grad_near, grad_far)
+    attention_backward(found, kept, grad_att, edge, joined, grad_keys, grad_values, score_grad)
+    inner = slice(2 * HALO, 2 * HALO + rows)
+    joined[:, 128:256] = grad_keys[inner, :].astype(BF16)
+    joined[:, 256:384] = grad_values[inner, :].astype(BF16)
+    grad_normed = nt(joined[...], weight_in[0]).astype(BF16).astype(F32)
+    back, gained = norm_back(grad_normed, atoms[...].astype(F32), gain[0:1, :])
+    grad_gain[0:1, :] = jnp.sum(gained, 0, keepdims=True)
+    grad_atoms[...] = (rising[own] + back).astype(BF16)
 
 
 EARLY = 144
@@ -555,6 +595,8 @@
 def backward_weights_kernel(
     pair,
     scores,
+    normed_first,
+    joined_first,
     normed,
     joined,
     att,
@@ -562,7 +604,7 @@
     token,
     out_later,
     bias_later,
-    gain_later,
+    grad_gain,
     scores_later,
     keep,
     send,
@@ -585,7 +627,7 @@
     for m in range(4):
         for r in range(0, 128, 16):
             put(512 + m * 128 + r, inner[r : r + 16, m * 128 : (m + 1) * 128])
-    out = tn(att[...], grad_update[...])
+    out = tn(att[HALO : HALO + joined.shape[0], :], grad_update[...])
     for r in range(0, 128, 16):
         put(1024 + r, out[r : r + 16, :])
     for m in range(2, 8):
@@ -594,47 +636,15 @@
         pair, [(j, scores[j]) for j in range(pair.shape[0])], whole.at[0, EARLY:EXTRA]
     )
     whole[1, EARLY:EXTRA, :] = bias_later[...]
-    whole[3, EARLY : EARLY + 1, :] = gain_later[...]
+    whole[2, EARLY : EARLY + 1, :] = grad_gain[0:1, :]
+    whole[3, EARLY : EARLY + 1, :] = grad_gain[1:2, :]
+    inner = tn(normed_first[...], joined_first[...])
+    for m in range(8):
+        half = (m % 2) * 64
+        whole[m, EXTRA:SPAN, :] = inner[half : half + 64, (m // 2) * 128 : (m // 2 + 1) * 128]
     core = lax.rem(lax.axis_index("seq"), 2)
     keep[...] = whole[pl.ds(core * 4, 4)]
-    send[...] = whole[pl.ds((1 - core) * 4, 4)]
-
-
-def last_kernel(
-    grad_q,
-    center,
-    near,
-    far,
-    grad_gate,
-    atoms,
-    gain,
-    weight_in,
-    grad_state,
-    normed,
-    keep_early,
-    send_early,
-    grad_atoms,
-    keep,
-    send,
-    joined,
-    late,
-):
-    join_projected(grad_q, center, near, far, grad_gate, joined)
-    grad_normed = nt(joined[...], weight_in[0]).astype(BF16).astype(F32)
-    product = tn(normed[...], joined[...])
-    back, gained = norm_back(grad_normed, atoms[...].astype(F32), gain[0:1, :])
-    grad_atoms[...] = (grad_state[...] + back).astype(BF16)
-    for m in range(8):
-        late[m, 0:16, :] = jnp.zeros((16, 128), F32)
-        half = (m % 2) * 64
-        late[m, 16:80, :] = product[half : half + 64, (m // 2) * 128 : (m // 2 + 1) * 128]
-    late[2, 0:1, :] = gained
-    core = lax.rem(lax.axis_index("seq"), 2)
-    for ref, early, at in ((keep, keep_early, core), (send, send_early, 1 - core)):
-        piece = late[pl.ds(at * 4, 4)]
-        ref[:, 0:EARLY, :] = early[:, 0:EARLY, :].astype(ref.dtype)
-        ref[:, EARLY:EXTRA, :] = (early[:, EARLY:EXTRA, :] + piece[:, 0:16]).astype(ref.dtype)
-        ref[:, EXTRA:SPAN, :] = piece[:, 16:80].astype(ref.dtype)
+    send[...] = whole[pl.ds((1 - core) * 4, 4)].astype(BF16)
 
 
 def core_kernel(keep, got, own, one, two, three, whole):
@@ -745,7 +755,7 @@
     wide = ((rows, 128), BF16)
     full = ((rows, 128), F32)
     kv_shape = ((rows, 256), BF16)
-    rim = ((HALO, 256), BF16)
+    rim = ((HALO, 896), BF16)
     scores_shape = ((blocks, 128, 128), BF16)
     channel_weight = weight_bias.transpose(0, 2, 1)
 
@@ -769,9 +779,23 @@
     )
     bias0, bias1 = run(bias_kernel, [square, square], (channel_weight, pair), smem=(0,))
     ext_kv = ((ext, 256), BF16)
-    state1, chances0, att0, kv0, normed1, q1, kv1, gate1 = run(
+    more = blocks + 2 * HALO // QBLK
+    broad = ext + 2 * HALO
+    state1, chances0, att0, kv0, q0, gate0, shift_row, normed1, q1, kv1, gate1 = run(
         partial(forward_kernel, atom_total),
-        [full, square, wide, ext_kv, wide, wide, ext_kv, full],
+        [
+            ((ext, 128), F32),
+            ((more, 128, 128), F32),
+            ((ext, 128), BF16),
+            ((broad, 256), BF16),
+            ((ext, 128), BF16),
+            ((ext, 128), F32),
+            ((1, 128), jnp.int32),
+            wide,
+            wide,
+            ext_kv,
+            full,
+        ],
         (
             shift_row,
             channel_weight,
@@ -788,11 +812,6 @@
         smem=(0, 1),
         scratch=[pltpu.VMEM((rows + 4 * HALO, 128), F32)] * 2,
     )
-    back_scratch = [
-        pltpu.VMEM((rows, 128), BF16),
-        pltpu.VMEM((ext, 128), F32),
-        pltpu.VMEM((ext, 128), F32),
-    ]
     (
         att1,
         grad_update1,
@@ -802,6 +821,7 @@
         grad_gate1,
         grad_q1,
         center1,
+        outgoing,
         near1,
         far1,
         scores1,
@@ -816,6 +836,7 @@
             wide,
             wide,
             ((rows, 256), F32),
+            ((2 * HALO, 256), BF16),
             rim,
             rim,
             scores_shape,
@@ -835,7 +856,7 @@
             *rims0,
         ),
         smem=(0,),
-        scratch=window + back_scratch,
+        scratch=window + window,
     )
     rims1 = swapped(near1, far1)
     grad_token, grad_out1, grad_bias1 = run(
@@ -844,35 +865,14 @@
         (pair, scores1, narrow_state, grad_hidden, att1, grad_update1),
     )
     rims1, grad_token = lax.optimization_barrier((rims1, grad_token))
-    (
-        joined1,
-        grad_gain1,
-        grad_update0,
-        grad_state1,
-        grad_gate0,
-        grad_q0,
-        center0,
-        near0,
-        far0,
-        scores0,
-    ) = run(
+    joined1, joined0, gains, grad_update0, scores0, grad_atoms = run(
         backward_kernel,
-        [
-            ((rows, 512), BF16),
-            ((1, 128), F32),
-            wide,
-            full,
-            wide,
-            wide,
-            ((rows, 256), F32),
-            rim,
-            rim,
-            ((blocks, 128, 128), BF16),
-        ],
+        [((rows, 512), BF16), ((rows, 512), BF16), ((2, 128), F32), wide, scores_shape, wide],
         (
             shift_row,
             grad_q1,
             center1,
+            outgoing,
             *rims1,
             grad_gate1,
             state1,
@@ -885,17 +885,19 @@
             att0,
             weight_out,
             chances0,
+            atoms,
         ),
         smem=(0,),
-        scratch=window + back_scratch,
-    )
-    last_rims = swapped(near0, far0)
+        scratch=[pltpu.VMEM((ext, 512), BF16)] + [pltpu.VMEM((broad, 128), F32)] * 4,
+    )
     keep, send, *score_parts = run(
         backward_weights_kernel,
-        [((4, EXTRA, 128), F32), ((4, EXTRA, 128), F32)] + [((4, 128, 128), BF16)] * 4,
+        [((4, SPAN, 128), F32), ((4, SPAN, 128), BF16)] + [((4, 128, 128), BF16)] * 4,
         (
             pair,
             scores0,
+            normed0,
+            joined0,
             normed1,
             joined1,
             att0,
@@ -903,28 +905,10 @@
             grad_token,
             grad_out1,
             grad_bias1,
-            grad_gain1,
+            gains,
             scores1,
         ),
-        scratch=[pltpu.VMEM((8, EXTRA, 128), F32)],
-    )
-    grad_atoms, keep, send = run(
-        last_kernel,
-        [wide, ((4, SPAN, 128), F32), ((4, SPAN, 128), BF16)],
-        (
-            grad_q0,
-            center0,
-            *last_rims,
-            grad_gate0,
-            atoms,
-            norm_gain,
-            weight_in,
-            grad_state1,
-            normed0,
-            keep,
-            send,
-        ),
-        scratch=[pltpu.VMEM((rows, 512), BF16), pltpu.VMEM((8, 80, 128), F32)],
+        scratch=[pltpu.VMEM((8, SPAN, 128), F32)],
     )
     chunk = ((SPAN, 128), BF16)
     own, *pieces = run(

time: 92.6 us -> 87.2 us (0.942)
  starting transfers between devices: 46.3 us -> 41.7 us
  waiting for transfers between devices: 27.6 us -> 26.4 us
    ppermute x3 -> x2, starting transfers between devices: 6.34 us -> 3.93 us  [swapped(): far = lax.ppermute(far, 'seq', across)]
    ppermute x18, starting transfers between devices: 36.4 us -> 34.4 us  [hop(): return lax.ppermute(value, WORLD, moves(part, step))]
    ppermute x3 -> x2, waiting for transfers between devices: 8.77 us -> 7.48 us  [swapped(): far = lax.ppermute(far, 'seq', across)]
    pallas_call x14 -> x13, Pallas kernels: 16.1 us -> 16.5 us  [run(): pl.pallas_call(body, out_shape=[jax.ShapeDtypeStruct(s, d) for s, d in ou...]
    ppermute x3 -> x2, starting transfers between devices: 3.51 us -> 3.42 us  [swapped(): return (lax.ppermute(near, 'seq', chip), far)]
  transfers between devices with their start and end apart: 24 -> 22, of which waited for: 14 -> 14; matrix products, arithmetic and copies ran while one was open for 0% -> 0% of each run, Pallas kernels for 5% -> 5%
where the time goes in v4:
time: 87.2 us; the launch traced here: 87 us
  starting transfers between devices  41.7 us (48%)
  waiting for transfers between devices  26.4 us (30%)
  Pallas kernels  16.5 us (19%)
  local copies, waits for them, and re-layouts  1.36 us (2%)
  between operations  0.89 us (1%)
    ppermute x18, starting transfers between devices, hop(): return lax.ppermute(value, WORLD, moves(part, step))  34.4 us
    ppermute x18, waiting for transfers between devices, hop(): return lax.ppermute(value, WORLD, moves(part, step))  18.9 us
    pallas_call x13, Pallas kernels, run(): pl.pallas_call(body, out_shape=[jax.ShapeDtypeStruct(s, d) for s, d in ou...  16.5 us
    ppermute x2, waiting for transfers between devices, swapped(): far = lax.ppermute(far, 'seq', across)  7.48 us
    ppermute x2, starting transfers between devices, swapped(): far = lax.ppermute(far, 'seq', across)  3.93 us
    ppermute x2, starting transfers between devices, swapped(): return (lax.ppermute(near, 'seq', chip), far)  3.42 us
  transfers between devices with their start and end apart: 22, of which 14 were waited for; matrix products, arithmetic and copies ran while one was open for 0% of the time, Pallas kernels for 5%

profile of v4, /device:TPU:1, one launch (start us, length us, event | category | flops | bytes accessed | tf_op | source)
XLA Modules:
  0.0 87.0 jit_solution(6220761966204482543)
XLA Ops:
  0.6 2.1 %shard_map.162 = (bf16[1168,128]{1,0:T(8,128)(2,1)}, bf16[1168,128]{1,0:T(8,128)(2,1)}, s32[1,128]{1,0:T(1,128)}) custom-call(s32[8]{0:T(128)} %shift_far.1, bf16[8,512,128]{2,1,0:T(8,128)(2,1)} %bitcast.9, bf16[256,128]{1,0:T(8,128)(2,1)} %bitcast.13, bf16[32,384]{1,0:T(8,128)(2,1)} %bitcast.17, s32[1,32]{1,0:T(1,128)} %bitcast.22), custom_call_target="tpu_custom_call" | custom-call | flops 100000000 | bytes 1000000 | tf_op jit(solution)/shard_map/pallas_call | solution.py:68
  2.8 3.3 %collective-permute-start = (bf16[1168,128]{1,0:T(8,128)(2,1)}, bf16[1168,128]{1,0:T(8,128)(2,1)S(1)}, u32[]{:S(2)}, u32[]{:S(2)}) collective-permute-start(bf16[1168,128]{1,0:T(8,128)(2,1)} %get-tuple-element.73), channel_id=1, source_target_pairs={{0,8},{8,0},{16,24},{24,16},{32,40},{40,32},{48,56},{56,48},{64,72... | collective-permute-start | bytes 897032 | tf_op jit(solution)/shard_map/ppermute | solution.py:47
  6.1 1.9 %collective-permute-start.1 = (bf16[1168,128]{1,0:T(8,128)(2,1)}, bf16[1168,128]{1,0:T(8,128)(2,1)S(1)}, u32[]{:S(2)}, u32[]{:S(2)}) collective-permute-start(bf16[1168,128]{1,0:T(8,128)(2,1)} %get-tuple-element.74), channel_id=1, source_target_pairs={{8,16},{16,8},{24,32},{32,24},{40,48},{48,40},{56,64},{64,56},{72,... | collective-permute-start | bytes 897032 | tf_op jit(solution)/shard_map/ppermute | solution.py:46
  8.1 1.9 %shard_map.164 = (f32[8,128,128]{2,1,0:T(8,128)S(1)}, f32[8,128,128]{2,1,0:T(8,128)S(1)}) custom-call(f32[2,4,16]{2,1,0:T(4,128)S(1)} %bitcast.19, bf16[8,512,128]{2,1,0:T(8,128)(2,1)S(1)} %bitcast.10), custom_call_target="tpu_custom_call" | custom-call | flops 100000000 | bytes 1000000 | tf_op jit(solution)/shard_map/pallas_call | solution.py:68
  10.5 3.9 %collective-permute-done.1.far.far_first = bf16[1168,128]{1,0:T(8,128)(2,1)S(1)} collective-permute-done((bf16[1168,128]{1,0:T(8,128)(2,1)}, bf16[1168,128]{1,0:T(8,128)(2,1)S(1)}, u32[]{:S(2)}, u32[]{:S(2)}) %collective-permute-start.1) | collective-permute-done | bytes 299040 | tf_op jit(solution)/shard_map/ppermute | solution.py:46
  15.1 2.5 %shard_map.165 = (f32[384,128]{1,0:T(8,128)S(1)}, f32[12,128,128]{2,1,0:T(8,128)S(1)}, bf16[384,128]{1,0:T(8,128)(2,1)S(1)}, bf16[512,256]{1,0:T(8,128)(2,1)S(1)...) custom-call(s32[1,128]{1,0:T(1,128)S(1)} %copy-done.10, ...), custom_call_target="tpu_custom_call" | custom-call | flops 100000000 | bytes 1000000 | tf_op jit(solution)/shard_map/pallas_call | solution.py:68
  18.3 2.3 %shard_map.166 = (bf16[256,128]{1,0:T(8,128)(2,1)S(1)}, bf16[256,128]{1,0:T(8,128)(2,1)S(1)}, bf16[256,128]{1,0:T(8,128)(2,1)S(1)}, bf16[256,384]{1,0:T(8,128)(2...) custom-call(s32[1,128]{1,0:T(1,128)S(1)} %get-tuple-element.77.shift, ...), custom_call_target="tpu_custom_call" | custom-call | flops 100000000 | bytes 1000000 | tf_op jit(solution)/shard_map/pallas_call | solution.py:68
  20.7 2.0 %collective-permute-start.3 = (bf16[64,896]{1,0:T(8,128)(2,1)S(1)}, bf16[64,896]{1,0:T(8,128)(2,1)S(1)}, u32[]{:S(2)}, u32[]{:S(2)}) collective-permute-start(bf16[64,896]{1,0:T(8,128)(2,1)S(1)} %get-tuple-element.87), channel_id=1, source_target_pairs={{8,16},{16,8},{24,32},{32,24},{40,48},{48,40},{56,64},{64,56},{72,... | collective-permute-start | bytes 344072 | tf_op jit(solution)/shard_map/ppermute | solution.py:46
  23.3 3.6 %collective-permute-done.3.far = bf16[64,896]{1,0:T(8,128)(2,1)S(1)} collective-permute-done((bf16[64,896]{1,0:T(8,128)(2,1)S(1)}, bf16[64,896]{1,0:T(8,128)(2,1)S(1)}, u32[]{:S(2)}, u32[]{:S(2)}) %collective-permute-start.3) | collective-permute-done | bytes 114720 | tf_op jit(solution)/shard_map/ppermute | solution.py:46
  26.8 3.2 %shard_map.168 = (bf16[256,512]{1,0:T(8,128)(2,1)S(1)}, bf16[256,512]{1,0:T(8,128)(2,1)S(1)}, f32[2,128]{1,0:T(2,128)S(1)}, bf16[256,128]{1,0:T(8,128)(2,1)S(1)}...) custom-call(s32[1,128]{1,0:T(1,128)S(1)} %get-tuple-element.77.shift, ...), custom_call_target="tpu_custom_call" | custom-call | flops 100000000 | bytes 1000000 | tf_op jit(solution)/shard_map/pallas_call | solution.py:68
  31.0 2.2 %collective-permute-start.9 = (bf16[4,128,128]{2,1,0:T(8,128)(2,1)S(1)}, bf16[4,128,128]{2,1,0:T(8,128)(2,1)S(1)}, u32[]{:S(2)}, u32[]{:S(2)}) collective-permute-start(bf16[4,128,128]{2,1,0:T(8,128)(2,1)S(1)} %get-tuple-element.122), channel_id=1, source_target_pairs={{0,4},{1,5},{2,6},{3,7},{4,0},{5,1},{6,2},{7,3},{8,12},{9,13},{10,... | collective-permute-start | bytes 393224 | tf_op jit(solution)/shard_map/ppermute | solution.py:38
  34.8 1.5 %collective-permute-start.6 = (bf16[224,128]{1,0:T(8,128)(2,1)S(1)}, bf16[224,128]{1,0:T(8,128)(2,1)S(1)}, u32[]{:S(2)}, u32[]{:S(2)}) collective-permute-start(bf16[224,128]{1,0:T(8,128)(2,1)S(1)} %get-tuple-element.118), channel_id=1, source_target_pairs={{0,4},{1,5},{2,6},{3,7},{4,0},{5,1},{6,2},{7,3},{8,12},{9,13},{10,... | collective-permute-start | bytes 172040 | tf_op jit(solution)/shard_map/ppermute | solution.py:38
  40.4 2.2 %collective-permute-done.5.one = bf16[224,128]{1,0:T(8,128)(2,1)S(1)} collective-permute-done((bf16[224,128]{1,0:T(8,128)(2,1)S(1)}, bf16[224,128]{1,0:T(8,128)(2,1)S(1)}, u32[]{:S(2)}, u32[]{:S(2)}) %collective-permute-start.5) | collective-permute-done | bytes 57376 | tf_op jit(solution)/shard_map/ppermute | solution.py:38
  42.7 5.7 %collective-permute-start.11 = (bf16[480,128]{1,0:T(8,128)(2,1)S(1)}, bf16[480,128]{1,0:T(8,128)(2,1)S(1)}, u32[]{:S(2)}, u32[]{:S(2)}) collective-permute-start(bf16[480,128]{1,0:T(8,128)(2,1)S(1)} %get-tuple-element.124), channel_id=1, source_target_pairs={{0,1},{1,0},{2,3},{3,2},{4,5},{5,4},{6,7},{7,6},{8,9},{9,8},{10,11... | collective-permute-start | bytes 368648 | tf_op jit(solution)/shard_map/ppermute | solution.py:38
  48.4 2.3 %collective-permute-done.11.got = bf16[480,128]{1,0:T(8,128)(2,1)S(1)} collective-permute-done((bf16[480,128]{1,0:T(8,128)(2,1)S(1)}, bf16[480,128]{1,0:T(8,128)(2,1)S(1)}, u32[]{:S(2)}, u32[]{:S(2)}) %collective-permute-start.11) | collective-permute-done | bytes 122912 | tf_op jit(solution)/shard_map/ppermute | solution.py:38
  50.7 8.1 %collective-permute-start.14 = (bf16[224,128]{1,0:T(8,128)(2,1)S(1)}, bf16[224,128]{1,0:T(8,128)(2,1)S(1)}, u32[]{:S(2)}, u32[]{:S(2)}) collective-permute-start(bf16[224,128]{1,0:T(8,128)(2,1)S(1)} %add_convert_fusion.2), channel_id=1, source_target_pairs={{0,192},{1,193},{2,194},{3,195},{4,196},{5,197},{6,198},{7,199},{8... | collective-permute-start | bytes 172040 | tf_op jit(solution)/shard_map/ppermute | solution.py:38
  59.8 1.4 %shard_map.172 = bf16[512,128]{1,0:T(8,128)(2,1)} custom-call(f32[2,4,16]{2,1,0:T(4,128)S(1)} %bitcast.21, f32[2,128,128]{2,1,0:T(8,128)S(1)} %get-tuple-element.125.kept, bf16[480,128]{1,0:T(8,128)(2,1)S(1)} %collective-permute-done.11.got), custom_call_target="tpu_custom_call" | custom-call | flops 100000000 | bytes 1000000 | tf_op jit(solution)/shard_map/pallas_call | solution.py:68
  61.3 2.4 %collective-permute-done.13 = bf16[224,128]{1,0:T(8,128)(2,1)S(1)} collective-permute-done((bf16[224,128]{1,0:T(8,128)(2,1)S(1)}, bf16[224,128]{1,0:T(8,128)(2,1)S(1)}, u32[]{:S(2)}, u32[]{:S(2)}) %collective-permute-start.13) | collective-permute-done | bytes 57376 | tf_op jit(solution)/shard_map/ppermute | solution.py:38
  63.7 4.9 %collective-permute-start.17 = (bf16[224,128]{1,0:T(8,128)(2,1)S(1)}, bf16[224,128]{1,0:T(8,128)(2,1)S(1)}, u32[]{:S(2)}, u32[]{:S(2)}) collective-permute-start(bf16[224,128]{1,0:T(8,128)(2,1)S(1)} %add_convert_fusion.1), channel_id=1, source_target_pairs={{0,48},{1,49},{2,50},{3,51},{4,52},{5,53},{6,54},{7,55},{8,56},{9,... | collective-permute-start | bytes 172040 | tf_op jit(solution)/shard_map/ppermute | solution.py:38
  68.6 1.3 %collective-permute-start.15 = (bf16[224,128]{1,0:T(8,128)(2,1)S(1)}, bf16[224,128]{1,0:T(8,128)(2,1)S(1)}, u32[]{:S(2)}, u32[]{:S(2)}) collective-permute-start(bf16[224,128]{1,0:T(8,128)(2,1)S(1)} %add_convert_fusion.1), channel_id=1, source_target_pairs={{0,32},{1,33},{2,34},{3,35},{4,36},{5,37},{6,38},{7,39},{8,40},{9,... | collective-permute-start | bytes 172040 | tf_op jit(solution)/shard_map/ppermute | solution.py:38
  69.9 3.3 %collective-permute-done.16 = bf16[224,128]{1,0:T(8,128)(2,1)S(1)} collective-permute-done((bf16[224,128]{1,0:T(8,128)(2,1)S(1)}, bf16[224,128]{1,0:T(8,128)(2,1)S(1)}, u32[]{:S(2)}, u32[]{:S(2)}) %collective-permute-start.16) | collective-permute-done | bytes 57376 | tf_op jit(solution)/shard_map/ppermute | solution.py:38
  75.4 1.4 %collective-permute-done.20.three = bf16[224,128]{1,0:T(8,128)(2,1)S(1)} collective-permute-done((bf16[224,128]{1,0:T(8,128)(2,1)S(1)}, bf16[224,128]{1,0:T(8,128)(2,1)S(1)}, u32[]{:S(2)}, u32[]{:S(2)}) %collective-permute-start.20) | collective-permute-done | bytes 57376 | tf_op jit(solution)/shard_map/ppermute | solution.py:38
  76.8 1.9 %collective-permute-done.19.two = bf16[224,128]{1,0:T(8,128)(2,1)S(1)} collective-permute-done((bf16[224,128]{1,0:T(8,128)(2,1)S(1)}, bf16[224,128]{1,0:T(8,128)(2,1)S(1)}, u32[]{:S(2)}, u32[]{:S(2)}) %collective-permute-start.19) | collective-permute-done | bytes 57376 | tf_op jit(solution)/shard_map/ppermute | solution.py:38
  79.3 5.4 %collective-permute-start.21 = (bf16[4,224,128]{2,1,0:T(8,128)(2,1)S(1)}, bf16[4,224,128]{2,1,0:T(8,128)(2,1)S(1)}, u32[]{:S(2)}, u32[]{:S(2)}) collective-permute-start(bf16[4,224,128]{2,1,0:T(8,128)(2,1)S(1)} %shard_map.173.half), channel_id=1, source_target_pairs={{0,8},{1,9},{2,10},{3,11},{4,12},{5,13},{6,14},{7,15},{8,0},{9,1},... | collective-permute-start | bytes 688136 | tf_op jit(solution)/shard_map/ppermute | solution.py:38
  (58 shorter events, 15.3 us)
Async XLA Ops:
  0.6 7.4 %copy-start = (bf16[8,16,32,128]{3,2,1,0:T(8,128)(2,1)S(1)}, bf16[8,16,32,128]{3,2,1,0:T(8,128)(2,1)}, u32[]{:S(2)}) copy-start(bf16[8,16,32,128]{3,2,1,0:T(8,128)(2,1)} %param.12) | copy-start | bytes 3145732
  2.8 5.3 %copy-start.6 = (f32[2,16,4]{1,2,0:T(4,128)S(1)}, f32[2,16,4]{1,2,0:T(4,128)}, u32[]{:S(2)}) copy-start(f32[2,16,4]{1,2,0:T(4,128)} %param.20) | copy-start | bytes 1540
  2.8 7.7 %collective-permute-start = (bf16[1168,128]{1,0:T(8,128)(2,1)}, bf16[1168,128]{1,0:T(8,128)(2,1)S(1)}, u32[]{:S(2)}, u32[]{:S(2)}) collective-permute-start(bf16[1168,128]{1,0:T(8,128)(2,1)} %get-tuple-element.73), channel_id=1, source_target_pairs={{0,8},{8,0},{16,24},{24,16},{32,40},{40,32},{48,56},{56,48},{64,72... | collective-permute-start | bytes 897032 | tf_op jit(solution)/shard_map/ppermute | solution.py:47
  6.1 8.3 %collective-permute-start.1 = (bf16[1168,128]{1,0:T(8,128)(2,1)}, bf16[1168,128]{1,0:T(8,128)(2,1)S(1)}, u32[]{:S(2)}, u32[]{:S(2)}) collective-permute-start(bf16[1168,128]{1,0:T(8,128)(2,1)} %get-tuple-element.74), channel_id=1, source_target_pairs={{8,16},{16,8},{24,32},{32,24},{40,48},{48,40},{56,64},{64,56},{72,... | collective-permute-start | bytes 897032 | tf_op jit(solution)/shard_map/ppermute | solution.py:46
  20.6 2.6 %collective-permute-start.2 = (bf16[64,896]{1,0:T(8,128)(2,1)S(1)}, bf16[64,896]{1,0:T(8,128)(2,1)S(1)}, u32[]{:S(2)}, u32[]{:S(2)}) collective-permute-start(bf16[64,896]{1,0:T(8,128)(2,1)S(1)} %get-tuple-element.86), channel_id=1, source_target_pairs={{0,8},{8,0},{16,24},{24,16},{32,40},{40,32},{48,56},{56,48},{64,72... | collective-permute-start | bytes 344072 | tf_op jit(solution)/shard_map/ppermute | solution.py:47
  20.7 6.1 %collective-permute-start.3 = (bf16[64,896]{1,0:T(8,128)(2,1)S(1)}, bf16[64,896]{1,0:T(8,128)(2,1)S(1)}, u32[]{:S(2)}, u32[]{:S(2)}) collective-permute-start(bf16[64,896]{1,0:T(8,128)(2,1)S(1)} %get-tuple-element.87), channel_id=1, source_target_pairs={{8,16},{16,8},{24,32},{32,24},{40,48},{48,40},{56,64},{64,56},{72,... | collective-permute-start | bytes 344072 | tf_op jit(solution)/shard_map/ppermute | solution.py:46
  30.8 3.4 %collective-permute-start.4 = (bf16[4,224,128]{2,1,0:T(8,128)(2,1)S(1)}, bf16[4,224,128]{2,1,0:T(8,128)(2,1)S(1)}, u32[]{:S(2)}, u32[]{:S(2)}) collective-permute-start(bf16[4,224,128]{2,1,0:T(8,128)(2,1)S(1)} %get-tuple-element.115), channel_id=1, source_target_pairs={{0,8},{1,9},{2,10},{3,11},{4,12},{5,13},{6,14},{7,15},{8,0},{9,1},... | collective-permute-start | bytes 688136 | tf_op jit(solution)/shard_map/ppermute | solution.py:38
  30.9 6.4 %collective-permute-start.8 = (bf16[4,128,128]{2,1,0:T(8,128)(2,1)S(1)}, bf16[4,128,128]{2,1,0:T(8,128)(2,1)S(1)}, u32[]{:S(2)}, u32[]{:S(2)}) collective-permute-start(bf16[4,128,128]{2,1,0:T(8,128)(2,1)S(1)} %get-tuple-element.121), channel_id=1, source_target_pairs={{0,2},{1,3},{2,4},{3,5},{4,6},{5,7},{6,0},{7,1},{8,10},{9,11},{10,... | collective-permute-start | bytes 393224 | tf_op jit(solution)/shard_map/ppermute | solution.py:38
  31.0 8.2 %collective-permute-start.9 = (bf16[4,128,128]{2,1,0:T(8,128)(2,1)S(1)}, bf16[4,128,128]{2,1,0:T(8,128)(2,1)S(1)}, u32[]{:S(2)}, u32[]{:S(2)}) collective-permute-start(bf16[4,128,128]{2,1,0:T(8,128)(2,1)S(1)} %get-tuple-element.122), channel_id=1, source_target_pairs={{0,4},{1,5},{2,6},{3,7},{4,0},{5,1},{6,2},{7,3},{8,12},{9,13},{10,... | collective-permute-start | bytes 393224 | tf_op jit(solution)/shard_map/ppermute | solution.py:38
  33.1 7.3 %collective-permute-start.10 = (bf16[4,128,128]{2,1,0:T(8,128)(2,1)S(1)}, bf16[4,128,128]{2,1,0:T(8,128)(2,1)S(1)}, u32[]{:S(2)}, u32[]{:S(2)}) collective-permute-start(bf16[4,128,128]{2,1,0:T(8,128)(2,1)S(1)} %get-tuple-element.123), channel_id=1, source_target_pairs={{0,6},{1,7},{2,0},{3,1},{4,2},{5,3},{6,4},{7,5},{8,14},{9,15},{10,... | collective-permute-start | bytes 393224 | tf_op jit(solution)/shard_map/ppermute | solution.py:38
  34.3 8.3 %collective-permute-start.5 = (bf16[224,128]{1,0:T(8,128)(2,1)S(1)}, bf16[224,128]{1,0:T(8,128)(2,1)S(1)}, u32[]{:S(2)}, u32[]{:S(2)}) collective-permute-start(bf16[224,128]{1,0:T(8,128)(2,1)S(1)} %get-tuple-element.117), channel_id=1, source_target_pairs={{0,2},{1,3},{2,4},{3,5},{4,6},{5,7},{6,0},{7,1},{8,10},{9,11},{10,... | collective-permute-start | bytes 172040 | tf_op jit(solution)/shard_map/ppermute | solution.py:38
  34.8 7.9 %collective-permute-start.6 = (bf16[224,128]{1,0:T(8,128)(2,1)S(1)}, bf16[224,128]{1,0:T(8,128)(2,1)S(1)}, u32[]{:S(2)}, u32[]{:S(2)}) collective-permute-start(bf16[224,128]{1,0:T(8,128)(2,1)S(1)} %get-tuple-element.118), channel_id=1, source_target_pairs={{0,4},{1,5},{2,6},{3,7},{4,0},{5,1},{6,2},{7,3},{8,12},{9,13},{10,... | collective-permute-start | bytes 172040 | tf_op jit(solution)/shard_map/ppermute | solution.py:38
  37.3 5.3 %collective-permute-start.7 = (bf16[224,128]{1,0:T(8,128)(2,1)S(1)}, bf16[224,128]{1,0:T(8,128)(2,1)S(1)}, u32[]{:S(2)}, u32[]{:S(2)}) collective-permute-start(bf16[224,128]{1,0:T(8,128)(2,1)S(1)} %get-tuple-element.119), channel_id=1, source_target_pairs={{0,6},{1,7},{2,0},{3,1},{4,2},{5,3},{6,4},{7,5},{8,14},{9,15},{10,... | collective-permute-start | bytes 172040 | tf_op jit(solution)/shard_map/ppermute | solution.py:38
  42.7 7.9 %collective-permute-start.11 = (bf16[480,128]{1,0:T(8,128)(2,1)S(1)}, bf16[480,128]{1,0:T(8,128)(2,1)S(1)}, u32[]{:S(2)}, u32[]{:S(2)}) collective-permute-start(bf16[480,128]{1,0:T(8,128)(2,1)S(1)} %get-tuple-element.124), channel_id=1, source_target_pairs={{0,1},{1,0},{2,3},{3,2},{4,5},{5,4},{6,7},{7,6},{8,9},{9,8},{10,11... | collective-permute-start | bytes 368648 | tf_op jit(solution)/shard_map/ppermute | solution.py:38
  50.7 10.6 %collective-permute-start.14 = (bf16[224,128]{1,0:T(8,128)(2,1)S(1)}, bf16[224,128]{1,0:T(8,128)(2,1)S(1)}, u32[]{:S(2)}, u32[]{:S(2)}) collective-permute-start(bf16[224,128]{1,0:T(8,128)(2,1)S(1)} %add_convert_fusion.2), channel_id=1, source_target_pairs={{0,192},{1,193},{2,194},{3,195},{4,196},{5,197},{6,198},{7,199},{8... | collective-permute-start | bytes 172040 | tf_op jit(solution)/shard_map/ppermute | solution.py:38
  58.8 4.9 %collective-permute-start.13 = (bf16[224,128]{1,0:T(8,128)(2,1)S(1)}, bf16[224,128]{1,0:T(8,128)(2,1)S(1)}, u32[]{:S(2)}, u32[]{:S(2)}) collective-permute-start(bf16[224,128]{1,0:T(8,128)(2,1)S(1)} %add_convert_fusion.2), channel_id=1, source_target_pairs={{0,64},{1,65},{2,66},{3,67},{4,68},{5,69},{6,70},{7,71},{8,72},{9,... | collective-permute-start | bytes 172040 | tf_op jit(solution)/shard_map/ppermute | solution.py:38
  58.8 4.9 %collective-permute-start.12 = (bf16[224,128]{1,0:T(8,128)(2,1)S(1)}, bf16[224,128]{1,0:T(8,128)(2,1)S(1)}, u32[]{:S(2)}, u32[]{:S(2)}) collective-permute-start(bf16[224,128]{1,0:T(8,128)(2,1)S(1)} %add_convert_fusion.2), channel_id=1, source_target_pairs={{0,128},{1,129},{2,130},{3,131},{4,132},{5,133},{6,134},{7,135},{8... | collective-permute-start | bytes 172040 | tf_op jit(solution)/shard_map/ppermute | solution.py:38
  63.7 6.2 %collective-permute-start.17 = (bf16[224,128]{1,0:T(8,128)(2,1)S(1)}, bf16[224,128]{1,0:T(8,128)(2,1)S(1)}, u32[]{:S(2)}, u32[]{:S(2)}) collective-permute-start(bf16[224,128]{1,0:T(8,128)(2,1)S(1)} %add_convert_fusion.1), channel_id=1, source_target_pairs={{0,48},{1,49},{2,50},{3,51},{4,52},{5,53},{6,54},{7,55},{8,56},{9,... | collective-permute-start | bytes 172040 | tf_op jit(solution)/shard_map/ppermute | solution.py:38
  68.6 4.6 %collective-permute-start.16 = (bf16[224,128]{1,0:T(8,128)(2,1)S(1)}, bf16[224,128]{1,0:T(8,128)(2,1)S(1)}, u32[]{:S(2)}, u32[]{:S(2)}) collective-permute-start(bf16[224,128]{1,0:T(8,128)(2,1)S(1)} %add_convert_fusion.1), channel_id=1, source_target_pairs={{0,16},{1,17},{2,18},{3,19},{4,20},{5,21},{6,22},{7,23},{8,24},{9,... | collective-permute-start | bytes 172040 | tf_op jit(solution)/shard_map/ppermute | solution.py:38
  68.6 5.1 %collective-permute-start.15 = (bf16[224,128]{1,0:T(8,128)(2,1)S(1)}, bf16[224,128]{1,0:T(8,128)(2,1)S(1)}, u32[]{:S(2)}, u32[]{:S(2)}) collective-permute-start(bf16[224,128]{1,0:T(8,128)(2,1)S(1)} %add_convert_fusion.1), channel_id=1, source_target_pairs={{0,32},{1,33},{2,34},{3,35},{4,36},{5,37},{6,38},{7,39},{8,40},{9,... | collective-permute-start | bytes 172040 | tf_op jit(solution)/shard_map/ppermute | solution.py:38
  73.7 3.1 %collective-permute-start.20 = (bf16[224,128]{1,0:T(8,128)(2,1)S(1)}, bf16[224,128]{1,0:T(8,128)(2,1)S(1)}, u32[]{:S(2)}, u32[]{:S(2)}) collective-permute-start(bf16[224,128]{1,0:T(8,128)(2,1)S(1)} %add_convert_fusion.own), channel_id=1, source_target_pairs={{0,6},{1,7},{2,0},{3,1},{4,2},{5,3},{6,4},{7,5},{8,14},{9,15},{10,... | collective-permute-start | bytes 172040 | tf_op jit(solution)/shard_map/ppermute | solution.py:38
  74.2 4.5 %collective-permute-start.19 = (bf16[224,128]{1,0:T(8,128)(2,1)S(1)}, bf16[224,128]{1,0:T(8,128)(2,1)S(1)}, u32[]{:S(2)}, u32[]{:S(2)}) collective-permute-start(bf16[224,128]{1,0:T(8,128)(2,1)S(1)} %add_convert_fusion.own), channel_id=1, source_target_pairs={{0,4},{1,5},{2,6},{3,7},{4,0},{5,1},{6,2},{7,3},{8,12},{9,13},{10,... | collective-permute-start | bytes 172040 | tf_op jit(solution)/shard_map/ppermute | solution.py:38
  74.6 4.7 %collective-permute-start.18 = (bf16[224,128]{1,0:T(8,128)(2,1)S(1)}, bf16[224,128]{1,0:T(8,128)(2,1)S(1)}, u32[]{:S(2)}, u32[]{:S(2)}) collective-permute-start(bf16[224,128]{1,0:T(8,128)(2,1)S(1)} %add_convert_fusion.own), channel_id=1, source_target_pairs={{0,2},{1,3},{2,4},{3,5},{4,6},{5,7},{6,0},{7,1},{8,10},{9,11},{10,... | collective-permute-start | bytes 172040 | tf_op jit(solution)/shard_map/ppermute | solution.py:38
  79.3 6.5 %collective-permute-start.21 = (bf16[4,224,128]{2,1,0:T(8,128)(2,1)S(1)}, bf16[4,224,128]{2,1,0:T(8,128)(2,1)S(1)}, u32[]{:S(2)}, u32[]{:S(2)}) collective-permute-start(bf16[4,224,128]{2,1,0:T(8,128)(2,1)S(1)} %shard_map.173.half), channel_id=1, source_target_pairs={{0,8},{1,9},{2,10},{3,11},{4,12},{5,13},{6,14},{7,15},{8,0},{9,1},... | collective-permute-start | bytes 688136 | tf_op jit(solution)/shard_map/ppermute | solution.py:38
  (9 other events, 17.3 us)

commit v5 on v4

--- a/solution.py
+++ b/solution.py
@@ -194,7 +194,12 @@
         copy.wait()
 
 
-def first_kernel(atoms, gain, weight, normed, q, kv, gate):
+def first_kernel(
+    atoms, gain, weight, shift, token, counts, normed, q, kv, gate, shift_here, token_here, counts_here
+):
+    shift_here[...] = shift[...]
+    token_here[...] = token[...]
+    counts_here[...] = counts[...]
     unit, _ = stats(atoms[...].astype(F32))
     normed[...] = (unit * gain[0:1, :]).astype(BF16)
     projected = nn(normed[...], weight[0])
@@ -232,60 +237,77 @@
     values[...] = kv[:, 128:256].astype(F32)
 
 
-def windows(shifts, q, keys, values, margin):
+def windows(at, shifts, q, keys, values, margin):
     mask = head_mask(128)
-    spans = [pl.ds(j * QBLK + shift + margin, KWIN) for j, shift in enumerate(shifts)]
-    wide = [stacked(q[j * QBLK : (j + 1) * QBLK, :], mask) for j in range(len(spans))]
+    spans = [pl.ds(j * QBLK + shift + margin, KWIN) for j, shift in zip(at, shifts)]
+    wide = [stacked(block, mask) for block in q]
     key = [keys[span, :].astype(BF16) for span in spans]
     value = [values[span, :].astype(BF16) for span in spans]
     return spans, wide, key, value
 
 
-def attention_forward(shifts, found, bias, first, atom_total):
+def blocks_of(array, at):
+    return [array[j * QBLK : (j + 1) * QBLK, :] for j in at]
+
+
+def attention_forward(at, shifts, found, bias, first, atom_total):
     _, wide, key, value = found
     count = len(wide)
     mask = head_mask(128)
     lane = lax.broadcasted_iota(jnp.int32, (1, KWIN), 1)
-    scores = [nt(wide[j], key[j]) for j in range(count)]
+    scores = [nt(wide[n], key[n]) for n in range(count)]
     chances = []
-    for j in range(count):
-        place = first + (j * QBLK + shifts[j]) + lane
+    for n in range(count):
+        query = first + at[n] * QBLK
+        place = query + shifts[n] + lane
         inside = jnp.logical_and(place >= 0, place < atom_total)
-        weights = jnp.where(inside, jnp.exp(scores[j] * (32.0**-0.5) + bias[j]), 0.0)
-        query = first + j * QBLK
+        weights = jnp.where(inside, jnp.exp(scores[n] * (32.0**-0.5) + bias[n]), 0.0)
         real = jnp.logical_and(query >= 0, query < atom_total)
         size = jnp.where(real, jnp.sum(weights, -1, keepdims=True), 1.0)
         chances.append(weights * (1.0 / size))
-    out = [nn(chances[j].astype(BF16), value[j]) for j in range(count)]
-    return chances, jnp.concatenate([picked(v, mask) for v in out], 0).astype(BF16)
-
-
-def attention_backward(
-    found, chances, grad_att, edge, grad_q, grad_keys, grad_values, score_grad
-):
+    out = [nn(chances[n].astype(BF16), value[n]) for n in range(count)]
+    return chances, [picked(v, mask).astype(BF16) for v in out]
+
+
+def attention_backward(found, chances, grad_att, own, grad_q, grad_keys, grad_values, score_grad):
     spans, wide, key, value = found
     count = len(wide)
-    own = range(edge, count - edge)
     mask = head_mask(128)
-    out = [stacked(grad_att[j * QBLK : (j + 1) * QBLK, :], mask) for j in range(count)]
-    rising = [nt(out[j], value[j]) for j in range(count)]
-    value_back = [tn(chances[j].astype(BF16), out[j]) for j in range(count)]
+    out = [stacked(block, mask) for block in blocks_of(grad_att, range(count))]
+    rising = [nt(out[n], value[n]) for n in range(count)]
+    value_back = [tn(chances[n].astype(BF16), out[n]) for n in range(count)]
     scaled = []
-    for j in range(count):
-        term = chances[j] * rising[j].astype(BF16).astype(F32)
-        grad_score = term - chances[j] * jnp.sum(term, -1, keepdims=True)
-        if j in own:
-            score_grad[j - edge] = grad_score.astype(BF16)
+    for n in range(count):
+        term = chances[n] * rising[n].astype(BF16).astype(F32)
+        grad_score = term - chances[n] * jnp.sum(term, -1, keepdims=True)
+        if own[n] is not None:
+            score_grad[own[n]] = grad_score.astype(BF16)
         scaled.append((grad_score * (32.0**-0.5)).astype(BF16))
-    query_back = [nn(scaled[j], key[j]) for j in own]
-    key_back = [tn(scaled[j], wide[j]) for j in range(count)]
-    for n, value in enumerate(query_back):
-        grad_q[n * QBLK : (n + 1) * QBLK, 0:128] = picked(value, mask).astype(BF16)
-    grad_keys[...] = jnp.zeros_like(grad_keys)
-    grad_values[...] = jnp.zeros_like(grad_values)
-    for j in range(count):
-        grad_keys[spans[j], :] += key_back[j].astype(BF16).astype(F32)
-        grad_values[spans[j], :] += value_back[j].astype(BF16).astype(F32)
+    query_back = [None if own[n] is None else nn(scaled[n], key[n]) for n in range(count)]
+    key_back = [tn(scaled[n], wide[n]) for n in range(count)]
+    for n in range(count):
+        if own[n] is not None:
+            rows = slice(own[n] * QBLK, (own[n] + 1) * QBLK)
+            grad_q[rows, 0:128] = picked(query_back[n], mask).astype(BF16)
+    for n in range(count):
+        grad_keys[spans[n], :] += key_back[n].astype(BF16).astype(F32)
+        grad_values[spans[n], :] += value_back[n].astype(BF16).astype(F32)
+
+
+INNER = (2, 3, 4, 5)
+
+
+def inner_kernel(atom_total, shift, q, kv, bias, chances, att, keys, values):
+    load_window(kv, keys, values)
+    shifts = [shift[0, j] for j in INNER]
+    found = windows(INNER, shifts, blocks_of(q, INNER), keys, values, 0)
+    first = lax.axis_index("seq") * q.shape[0]
+    kept, attended = attention_forward(
+        INNER, shifts, found, [bias[j] for j in INNER], first, atom_total
+    )
+    for n, chance in enumerate(kept):
+        chances[n] = chance
+    att[...] = jnp.concatenate(attended, 0)
 
 
 def share_scores(scores, parts):
@@ -309,6 +331,7 @@
     weight_out,
     gain,
     weight_in,
+    att_inner,
     state,
     chances,
     att,
@@ -369,10 +392,16 @@
     for j, value in enumerate(shifts):
         row_of = jnp.where(lanes == j, value, row_of)
     shift_all[...] = row_of
-    found = windows(shifts, queries, keys, values, 2 * HALO - HALO)
-    kept, attended = attention_forward(shifts, found, biases, first - HALO, atom_total)
-    for j, chance in enumerate(kept):
-        chances[j] = chance
+    outer = [j for j in range(len(shifts)) if j - edge not in INNER]
+    near_shifts = [shifts[j] for j in outer]
+    found = windows(outer, near_shifts, blocks_of(queries, outer), keys, values, HALO)
+    kept, attended = attention_forward(
+        outer, near_shifts, found, [biases[j] for j in outer], first - HALO, atom_total
+    )
+    for n, chance in enumerate(kept):
+        chances[n] = chance
+    half = len(attended) // 2
+    attended = jnp.concatenate([*attended[:half], att_inner[...], *attended[half:]], 0)
     att[...] = attended
     done = began + gates * nn(attended, weight_out[0])
     state[...] = done
@@ -438,11 +467,13 @@
 ):
     load_window(kv, keys, values)
     shifts = [shift[0, j + HALO // QBLK] for j in range(bias.shape[0])]
-    found = windows(shifts, q, keys, values, HALO)
+    at = range(bias.shape[0])
+    found = windows(at, shifts, blocks_of(q, at), keys, values, HALO)
     first = lax.axis_index("seq") * q.shape[0]
     chances, attended = attention_forward(
-        shifts, found, [bias[j] for j in range(bias.shape[0])], first, atom_total
-    )
+        at, shifts, found, [bias[j] for j in at], first, atom_total
+    )
+    attended = jnp.concatenate(attended, 0)
     att[...] = attended
     update = nn(attended, weight_out[1])
     after = (state[HALO : HALO + q.shape[0], :] + gate[...] * update).astype(BF16)
@@ -471,7 +502,9 @@
     change = (rising * gates).astype(BF16)
     grad_update[...] = change
     grad_att = nt(change, weight_out[1]).astype(BF16)
-    attention_backward(found, chances, grad_att, 0, grad_q, grad_keys, grad_values, score_grad)
+    grad_keys[...] = jnp.zeros_like(grad_keys)
+    grad_values[...] = jnp.zeros_like(grad_values)
+    attention_backward(found, chances, grad_att, at, grad_q, grad_keys, grad_values, score_grad)
     send_halo(
         grad_keys,
         grad_values,
@@ -512,6 +545,52 @@
         back - jnp.mean(back, -1, keepdims=True) - unit * jnp.mean(back * unit, -1, keepdims=True)
     )
     return back, grad_normed * unit
+
+
+def inner_back_kernel(
+    shift,
+    grad_q_later,
+    center_later,
+    grad_gate_later,
+    state,
+    gain,
+    weight_in,
+    grad_state_later,
+    q,
+    kv,
+    gate,
+    weight_out,
+    chances,
+    grad_gain,
+    rising_inner,
+    grad_q,
+    score_grad,
+    grad_keys,
+    grad_values,
+    keys,
+    values,
+):
+    rows = center_later.shape[0]
+    edge = HALO // QBLK
+    inner = slice(HALO, rows - HALO)
+    wide = slice(2 * HALO, rows)
+    load_window(kv[2 * HALO : 2 * HALO + rows, :], keys, values)
+    parts = [grad_q_later[inner, :], center_later[inner, :].astype(BF16), grad_gate_later[inner, :]]
+    joined = jnp.concatenate(parts, 1)
+    grad_normed = nt(joined, weight_in[1]).astype(BF16).astype(F32)
+    back, gained = norm_back(grad_normed, state[wide, :], gain[1:2, :])
+    grad_gain[...] = jnp.sum(gained, 0, keepdims=True)
+    rising = grad_state_later[inner, :] + back
+    rising_inner[...] = rising
+    grad_att = nt((rising * gate[wide, :]).astype(BF16), weight_out[0]).astype(BF16)
+    shifts = [shift[0, j + edge] for j in INNER]
+    queries = blocks_of(q, [j + edge for j in INNER])
+    found = windows(INNER, shifts, queries, keys, values, 0)
+    grad_keys[...] = jnp.zeros_like(grad_keys)
+    grad_values[...] = jnp.zeros_like(grad_values)
+    kept = [chances[n] for n in range(len(INNER))]
+    own = range(len(INNER))
+    attention_backward(found, kept, grad_att, own, grad_q, grad_keys, grad_values, score_grad)
 
 
 def backward_kernel(
@@ -533,6 +612,12 @@
     weight_out,
     chances,
     atoms,
+    gain_inner,
+    rising_inner,
+    grad_q_inner,
+    score_inner,
+    keys_inner,
+    values_inner,
     joined_later,
     joined,
     grad_gain,
@@ -563,28 +648,47 @@
     joined_all[own, 128:384] = (center_later[...] + received).astype(BF16)
     joined_all[own, 384:512] = grad_gate_later[...]
     joined_later[...] = joined_all[own, :]
-    grad_normed = nt(joined_all[...], weight_in[1]).astype(BF16).astype(F32)
-    back, gained = norm_back(grad_normed, state[...], gain[1:2, :])
-    grad_gain[1:2, :] = jnp.sum(gained[own], 0, keepdims=True)
-    rising = [before[:, 768:896], grad_state_later[...], after[:, 768:896]]
+    ends = slice(0, 2 * HALO), slice(rows, rows + 2 * HALO)
+
+    def outer_of(array):
+        return jnp.concatenate([array[end, :] for end in ends], 0)
+
+    grad_normed = nt(outer_of(joined_all), weight_in[1]).astype(BF16).astype(F32)
+    back, gained = norm_back(grad_normed, outer_of(state), gain[1:2, :])
+    gained = jnp.sum(gained[HALO : 3 * HALO], 0, keepdims=True)
+    grad_gain[1:2, :] = gained + gain_inner[...]
+    rising = [before[:, 768:896], grad_state_later[0:HALO, :]]
+    rising += [grad_state_later[rows - HALO : rows, :], after[:, 768:896]]
     rising = jnp.concatenate(rising, 0) + back
-    change = (rising * gate[...]).astype(BF16)
-    grad_update[...] = change[own]
-    grad_att = nt(change, weight_out[0]).astype(BF16)
+    grad_att = nt((rising * outer_of(gate)).astype(BF16), weight_out[0]).astype(BF16)
+    rising = jnp.concatenate(
+        [rising[HALO : 2 * HALO], rising_inner[...], rising[2 * HALO : 3 * HALO]], 0
+    )
     gates = gate[own, :]
+    grad_update[...] = (rising * gates).astype(BF16)
     update = nn(att[own, :], weight_out[0])
-    joined[:, 384:512] = (rising[own] * update * gates * (1.0 - gates)).astype(BF16)
-    shifts = [shift[0, j] for j in range(chances.shape[0])]
-    found = windows(shifts, q, keys, values, HALO)
-    kept = [chances[j] for j in range(chances.shape[0])]
-    attention_backward(found, kept, grad_att, edge, joined, grad_keys, grad_values, score_grad)
+    joined[:, 384:512] = (rising * update * gates * (1.0 - gates)).astype(BF16)
+    count = rows // QBLK
+    outer = [j for j in range(count + 2 * edge) if j - edge not in INNER]
+    shifts = [shift[0, j] for j in outer]
+    found = windows(outer, shifts, blocks_of(q, outer), keys, values, HALO)
+    kept = [chances[n] for n in range(len(outer))]
+    mine = [j - edge if 0 <= j - edge < count else None for j in outer]
+    for ref, first in ((grad_keys, keys_inner), (grad_values, values_inner)):
+        ref[0 : 2 * HALO, :] = jnp.zeros((2 * HALO, 128), F32)
+        ref[2 * HALO : 2 * HALO + rows, :] = first[...]
+        ref[2 * HALO + rows :, :] = jnp.zeros((2 * HALO, 128), F32)
+    attention_backward(found, kept, grad_att, mine, joined, grad_keys, grad_values, score_grad)
+    joined[HALO : rows - HALO, 0:128] = grad_q_inner[...]
+    for n, j in enumerate(INNER):
+        score_grad[j] = score_inner[n]
     inner = slice(2 * HALO, 2 * HALO + rows)
     joined[:, 128:256] = grad_keys[inner, :].astype(BF16)
     joined[:, 256:384] = grad_values[inner, :].astype(BF16)
     grad_normed = nt(joined[...], weight_in[0]).astype(BF16).astype(F32)
     back, gained = norm_back(grad_normed, atoms[...].astype(F32), gain[0:1, :])
     grad_gain[0:1, :] = jnp.sum(gained, 0, keepdims=True)
-    grad_atoms[...] = (rising[own] + back).astype(BF16)
+    grad_atoms[...] = (rising + back).astype(BF16)
 
 
 EARLY = 144
@@ -774,12 +878,25 @@
         vmem=FIRST_VMEM,
     )
     rims0 = swapped(*rims0)
-    normed0, q0, kv0, gate0 = run(
-        first_kernel, [wide, wide, kv_shape, full], (atoms, norm_gain, weight_in)
+    normed0, q0, kv0, gate0, shift_row, token_row, counts = run(
+        first_kernel,
+        [wide, wide, kv_shape, full]
+        + [((1, 128), jnp.int32), (token_row.shape, jnp.int32), (counts.shape, jnp.int32)],
+        (atoms, norm_gain, weight_in, shift_row, token_row, counts),
     )
     bias0, bias1 = run(bias_kernel, [square, square], (channel_weight, pair), smem=(0,))
+    inner_square = ((len(INNER), 128, 128), F32)
+    inner_wide = ((len(INNER) * QBLK, 128), BF16)
+    own_window = [pltpu.VMEM((rows, 128), F32)] * 2
+    chances_inner, att_inner = run(
+        partial(inner_kernel, atom_total),
+        [inner_square, inner_wide],
+        (shift_row, q0, kv0, bias0),
+        smem=(0,),
+        scratch=own_window,
+    )
     ext_kv = ((ext, 256), BF16)
-    more = blocks + 2 * HALO // QBLK
+    more = blocks + 2 * HALO // QBLK - len(INNER)
     broad = ext + 2 * HALO
     state1, chances0, att0, kv0, q0, gate0, shift_row, normed1, q1, kv1, gate1 = run(
         partial(forward_kernel, atom_total),
@@ -808,6 +925,7 @@
             weight_out,
             norm_gain,
             weight_in,
+            att_inner,
         ),
         smem=(0, 1),
         scratch=[pltpu.VMEM((rows + 4 * HALO, 128), F32)] * 2,
@@ -864,6 +982,34 @@
         [((384, 128), F32), ((128, 128), F32), ((16, 128), F32)],
         (pair, scores1, narrow_state, grad_hidden, att1, grad_update1),
     )
+    inner_back = run(
+        inner_back_kernel,
+        [
+            ((1, 128), F32),
+            ((len(INNER) * QBLK, 128), F32),
+            inner_wide,
+            ((len(INNER), 128, 128), BF16),
+            full,
+            full,
+        ],
+        (
+            shift_row,
+            grad_q1,
+            center1,
+            grad_gate1,
+            state1,
+            norm_gain,
+            weight_in,
+            grad_state2,
+            q0,
+            kv0,
+            gate0,
+            weight_out,
+            chances_inner,
+        ),
+        smem=(0,),
+        scratch=own_window,
+    )
     rims1, grad_token = lax.optimization_barrier((rims1, grad_token))
     joined1, joined0, gains, grad_update0, scores0, grad_atoms = run(
         backward_kernel,
@@ -886,6 +1032,7 @@
             weight_out,
             chances0,
             atoms,
+            *inner_back,
         ),
         smem=(0,),
         scratch=[pltpu.VMEM((ext, 512), BF16)] + [pltpu.VMEM((broad, 128), F32)] * 4,

time: 87.2 us -> 85.2 us (0.977)
  waiting for transfers between devices: 26.4 us -> 23.3 us
  Pallas kernels: 16.5 us -> 18.3 us
    ppermute x2, waiting for transfers between devices: 7.48 us -> 4.37 us  [swapped(): far = lax.ppermute(far, 'seq', across)]
    pallas_call x13 -> x15, Pallas kernels: 16.5 us -> 18.3 us  [run(): pl.pallas_call(body, out_shape=[jax.ShapeDtypeStruct(s, d) for s, d in ou...]
  transfers between devices with their start and end apart: 22 -> 22, of which waited for: 14 -> 14; matrix products, arithmetic and copies ran while one was open for 0% -> 0% of each run, Pallas kernels for 5% -> 8%
where the time goes in v5:
time: 85.2 us; the launch traced here: 85 us
  starting transfers between devices  41.7 us (49%)
  waiting for transfers between devices  23.3 us (27%)
  Pallas kernels  18.3 us (21%)
  between operations  0.92 us (1%)
    ppermute x18, starting transfers between devices, hop(): return lax.ppermute(value, WORLD, moves(part, step))  34.4 us
    ppermute x18, waiting for transfers between devices, hop(): return lax.ppermute(value, WORLD, moves(part, step))  18.9 us
    pallas_call x15, Pallas kernels, run(): pl.pallas_call(body, out_shape=[jax.ShapeDtypeStruct(s, d) for s, d in ou...  18.3 us
    ppermute x2, waiting for transfers between devices, swapped(): far = lax.ppermute(far, 'seq', across)  4.37 us
    ppermute x2, starting transfers between devices, swapped(): far = lax.ppermute(far, 'seq', across)  3.91 us
    ppermute x2, starting transfers between devices, swapped(): return (lax.ppermute(near, 'seq', chip), far)  3.42 us
  transfers between devices with their start and end apart: 22, of which 14 were waited for; matrix products, arithmetic and copies ran while one was open for 0% of the time, Pallas kernels for 8%

profile of v5, /device:TPU:1, one launch (start us, length us, event | category | flops | bytes accessed | tf_op | source)
XLA Modules:
  0.0 85.0 jit_solution(4514572459716971017)
XLA Ops:
  0.6 2.1 %shard_map.162 = (bf16[1168,128]{1,0:T(8,128)(2,1)}, bf16[1168,128]{1,0:T(8,128)(2,1)}, s32[1,128]{1,0:T(1,128)}) custom-call(s32[8]{0:T(128)} %shift_far.1, bf16[8,512,128]{2,1,0:T(8,128)(2,1)} %bitcast.9, bf16[256,128]{1,0:T(8,128)(2,1)} %bitcast.13, bf16[32,384]{1,0:T(8,128)(2,1)} %bitcast.17, s32[1,32]{1,0:T(1,128)} %bitcast.22), custom_call_target="tpu_custom_call" | custom-call | flops 100000000 | bytes 1000000 | tf_op jit(solution)/shard_map/pallas_call | solution.py:68
  2.8 3.3 %collective-permute-start = (bf16[1168,128]{1,0:T(8,128)(2,1)}, bf16[1168,128]{1,0:T(8,128)(2,1)S(1)}, u32[]{:S(2)}, u32[]{:S(2)}) collective-permute-start(bf16[1168,128]{1,0:T(8,128)(2,1)} %get-tuple-element.85), channel_id=1, source_target_pairs={{0,8},{8,0},{16,24},{24,16},{32,40},{40,32},{48,56},{56,48},{64,72... | collective-permute-start | bytes 897032 | tf_op jit(solution)/shard_map/ppermute | solution.py:47
  6.1 1.9 %collective-permute-start.1 = (bf16[1168,128]{1,0:T(8,128)(2,1)}, bf16[1168,128]{1,0:T(8,128)(2,1)S(1)}, u32[]{:S(2)}, u32[]{:S(2)}) collective-permute-start(bf16[1168,128]{1,0:T(8,128)(2,1)} %get-tuple-element.86), channel_id=1, source_target_pairs={{8,16},{16,8},{24,32},{32,24},{40,48},{48,40},{56,64},{64,56},{72,... | collective-permute-start | bytes 897032 | tf_op jit(solution)/shard_map/ppermute | solution.py:46
  8.1 1.9 %shard_map.164 = (f32[8,128,128]{2,1,0:T(8,128)S(1)}, f32[8,128,128]{2,1,0:T(8,128)S(1)}) custom-call(f32[2,4,16]{2,1,0:T(4,128)S(1)} %bitcast.19, bf16[8,512,128]{2,1,0:T(8,128)(2,1)S(1)} %bitcast.10), custom_call_target="tpu_custom_call" | custom-call | flops 100000000 | bytes 1000000 | tf_op jit(solution)/shard_map/pallas_call | solution.py:68
  12.2 2.2 %collective-permute-done.1.far.far_first = bf16[1168,128]{1,0:T(8,128)(2,1)S(1)} collective-permute-done((bf16[1168,128]{1,0:T(8,128)(2,1)}, bf16[1168,128]{1,0:T(8,128)(2,1)S(1)}, u32[]{:S(2)}, u32[]{:S(2)}) %collective-permute-start.1) | collective-permute-done | bytes 299040 | tf_op jit(solution)/shard_map/ppermute | solution.py:46
  14.4 2.3 %shard_map.166 = (f32[384,128]{1,0:T(8,128)S(1)}, f32[8,128,128]{2,1,0:T(8,128)S(1)}, bf16[384,128]{1,0:T(8,128)(2,1)S(1)}, bf16[512,256]{1,0:T(8,128)(2,1)S(1)}...) custom-call(s32[1,128]{1,0:T(1,128)S(1)} %get-tuple-element.82.shift, ...), custom_call_target="tpu_custom_call" | custom-call | flops 100000000 | bytes 1000000 | tf_op jit(solution)/shard_map/pallas_call | solution.py:68
  16.8 2.4 %shard_map.167 = (bf16[256,128]{1,0:T(8,128)(2,1)S(1)}, bf16[256,128]{1,0:T(8,128)(2,1)S(1)}, bf16[256,128]{1,0:T(8,128)(2,1)S(1)}, bf16[256,384]{1,0:T(8,128)(2...) custom-call(s32[1,128]{1,0:T(1,128)S(1)} %get-tuple-element.90.shift, ...), custom_call_target="tpu_custom_call" | custom-call | flops 100000000 | bytes 1000000 | tf_op jit(solution)/shard_map/pallas_call | solution.py:68
  19.3 2.0 %collective-permute-start.3 = (bf16[64,896]{1,0:T(8,128)(2,1)S(1)}, bf16[64,896]{1,0:T(8,128)(2,1)S(1)}, u32[]{:S(2)}, u32[]{:S(2)}) collective-permute-start(bf16[64,896]{1,0:T(8,128)(2,1)S(1)} %get-tuple-element.102), channel_id=1, source_target_pairs={{8,16},{16,8},{24,32},{32,24},{40,48},{48,40},{56,64},{64,56},{72,... | collective-permute-start | bytes 344072 | tf_op jit(solution)/shard_map/ppermute | solution.py:46
  21.8 1.4 %shard_map.169 = (f32[1,128]{1,0:T(1,128)S(1)}, f32[128,128]{1,0:T(8,128)S(1)}, bf16[128,128]{1,0:T(8,128)(2,1)S(1)}, bf16[4,128,128]{2,1,0:T(8,128)(2,1)S(1)}, ...) custom-call(s32[1,128]{1,0:T(1,128)S(1)} %get-tuple-element.90.shift, ...), custom_call_target="tpu_custom_call" | custom-call | flops 100000000 | bytes 1000000 | tf_op jit(solution)/shard_map/pallas_call | solution.py:68
  23.2 2.1 %collective-permute-done.3.far = bf16[64,896]{1,0:T(8,128)(2,1)S(1)} collective-permute-done((bf16[64,896]{1,0:T(8,128)(2,1)S(1)}, bf16[64,896]{1,0:T(8,128)(2,1)S(1)}, u32[]{:S(2)}, u32[]{:S(2)}) %collective-permute-start.3) | collective-permute-done | bytes 114720 | tf_op jit(solution)/shard_map/ppermute | solution.py:46
  25.4 2.8 %shard_map.170 = (bf16[256,512]{1,0:T(8,128)(2,1)S(1)}, bf16[256,512]{1,0:T(8,128)(2,1)S(1)}, f32[2,128]{1,0:T(2,128)S(1)}, bf16[256,128]{1,0:T(8,128)(2,1)S(1)}...) custom-call(s32[1,128]{1,0:T(1,128)S(1)} %get-tuple-element.90.shift, ...), custom_call_target="tpu_custom_call" | custom-call | flops 100000000 | bytes 1000000 | tf_op jit(solution)/shard_map/pallas_call | solution.py:68
  29.0 2.2 %collective-permute-start.9 = (bf16[4,128,128]{2,1,0:T(8,128)(2,1)S(1)}, bf16[4,128,128]{2,1,0:T(8,128)(2,1)S(1)}, u32[]{:S(2)}, u32[]{:S(2)}) collective-permute-start(bf16[4,128,128]{2,1,0:T(8,128)(2,1)S(1)} %get-tuple-element.144), channel_id=1, source_target_pairs={{0,4},{1,5},{2,6},{3,7},{4,0},{5,1},{6,2},{7,3},{8,12},{9,13},{10,... | collective-permute-start | bytes 393224 | tf_op jit(solution)/shard_map/ppermute | solution.py:38
  32.8 1.5 %collective-permute-start.6 = (bf16[224,128]{1,0:T(8,128)(2,1)S(1)}, bf16[224,128]{1,0:T(8,128)(2,1)S(1)}, u32[]{:S(2)}, u32[]{:S(2)}) collective-permute-start(bf16[224,128]{1,0:T(8,128)(2,1)S(1)} %get-tuple-element.140), channel_id=1, source_target_pairs={{0,4},{1,5},{2,6},{3,7},{4,0},{5,1},{6,2},{7,3},{8,12},{9,13},{10,... | collective-permute-start | bytes 172040 | tf_op jit(solution)/shard_map/ppermute | solution.py:38
  38.5 2.2 %collective-permute-done.5.one = bf16[224,128]{1,0:T(8,128)(2,1)S(1)} collective-permute-done((bf16[224,128]{1,0:T(8,128)(2,1)S(1)}, bf16[224,128]{1,0:T(8,128)(2,1)S(1)}, u32[]{:S(2)}, u32[]{:S(2)}) %collective-permute-start.5) | collective-permute-done | bytes 57376 | tf_op jit(solution)/shard_map/ppermute | solution.py:38
  40.8 5.7 %collective-permute-start.11 = (bf16[480,128]{1,0:T(8,128)(2,1)S(1)}, bf16[480,128]{1,0:T(8,128)(2,1)S(1)}, u32[]{:S(2)}, u32[]{:S(2)}) collective-permute-start(bf16[480,128]{1,0:T(8,128)(2,1)S(1)} %get-tuple-element.146), channel_id=1, source_target_pairs={{0,1},{1,0},{2,3},{3,2},{4,5},{5,4},{6,7},{7,6},{8,9},{9,8},{10,11... | collective-permute-start | bytes 368648 | tf_op jit(solution)/shard_map/ppermute | solution.py:38
  46.4 2.3 %collective-permute-done.11.got = bf16[480,128]{1,0:T(8,128)(2,1)S(1)} collective-permute-done((bf16[480,128]{1,0:T(8,128)(2,1)S(1)}, bf16[480,128]{1,0:T(8,128)(2,1)S(1)}, u32[]{:S(2)}, u32[]{:S(2)}) %collective-permute-start.11) | collective-permute-done | bytes 122912 | tf_op jit(solution)/shard_map/ppermute | solution.py:38
  48.7 8.0 %collective-permute-start.14 = (bf16[224,128]{1,0:T(8,128)(2,1)S(1)}, bf16[224,128]{1,0:T(8,128)(2,1)S(1)}, u32[]{:S(2)}, u32[]{:S(2)}) collective-permute-start(bf16[224,128]{1,0:T(8,128)(2,1)S(1)} %add_convert_fusion.2), channel_id=1, source_target_pairs={{0,192},{1,193},{2,194},{3,195},{4,196},{5,197},{6,198},{7,199},{8... | collective-permute-start | bytes 172040 | tf_op jit(solution)/shard_map/ppermute | solution.py:38
  57.9 1.4 %shard_map.174 = bf16[512,128]{1,0:T(8,128)(2,1)} custom-call(f32[2,4,16]{2,1,0:T(4,128)S(1)} %bitcast.21, f32[2,128,128]{2,1,0:T(8,128)S(1)} %get-tuple-element.147.kept, bf16[480,128]{1,0:T(8,128)(2,1)S(1)} %collective-permute-done.11.got), custom_call_target="tpu_custom_call" | custom-call | flops 100000000 | bytes 1000000 | tf_op jit(solution)/shard_map/pallas_call | solution.py:68
  59.3 2.4 %collective-permute-done.13 = bf16[224,128]{1,0:T(8,128)(2,1)S(1)} collective-permute-done((bf16[224,128]{1,0:T(8,128)(2,1)S(1)}, bf16[224,128]{1,0:T(8,128)(2,1)S(1)}, u32[]{:S(2)}, u32[]{:S(2)}) %collective-permute-start.13) | collective-permute-done | bytes 57376 | tf_op jit(solution)/shard_map/ppermute | solution.py:38
  61.7 4.9 %collective-permute-start.17 = (bf16[224,128]{1,0:T(8,128)(2,1)S(1)}, bf16[224,128]{1,0:T(8,128)(2,1)S(1)}, u32[]{:S(2)}, u32[]{:S(2)}) collective-permute-start(bf16[224,128]{1,0:T(8,128)(2,1)S(1)} %add_convert_fusion.1), channel_id=1, source_target_pairs={{0,48},{1,49},{2,50},{3,51},{4,52},{5,53},{6,54},{7,55},{8,56},{9,... | collective-permute-start | bytes 172040 | tf_op jit(solution)/shard_map/ppermute | solution.py:38
  67.9 3.3 %collective-permute-done.16 = bf16[224,128]{1,0:T(8,128)(2,1)S(1)} collective-permute-done((bf16[224,128]{1,0:T(8,128)(2,1)S(1)}, bf16[224,128]{1,0:T(8,128)(2,1)S(1)}, u32[]{:S(2)}, u32[]{:S(2)}) %collective-permute-start.16) | collective-permute-done | bytes 57376 | tf_op jit(solution)/shard_map/ppermute | solution.py:38
  73.4 1.4 %collective-permute-done.20.three = bf16[224,128]{1,0:T(8,128)(2,1)S(1)} collective-permute-done((bf16[224,128]{1,0:T(8,128)(2,1)S(1)}, bf16[224,128]{1,0:T(8,128)(2,1)S(1)}, u32[]{:S(2)}, u32[]{:S(2)}) %collective-permute-start.20) | collective-permute-done | bytes 57376 | tf_op jit(solution)/shard_map/ppermute | solution.py:38
  74.8 1.9 %collective-permute-done.19.two = bf16[224,128]{1,0:T(8,128)(2,1)S(1)} collective-permute-done((bf16[224,128]{1,0:T(8,128)(2,1)S(1)}, bf16[224,128]{1,0:T(8,128)(2,1)S(1)}, u32[]{:S(2)}, u32[]{:S(2)}) %collective-permute-start.19) | collective-permute-done | bytes 57376 | tf_op jit(solution)/shard_map/ppermute | solution.py:38
  77.4 5.4 %collective-permute-start.21 = (bf16[4,224,128]{2,1,0:T(8,128)(2,1)S(1)}, bf16[4,224,128]{2,1,0:T(8,128)(2,1)S(1)}, u32[]{:S(2)}, u32[]{:S(2)}) collective-permute-start(bf16[4,224,128]{2,1,0:T(8,128)(2,1)S(1)} %shard_map.175.half), channel_id=1, source_target_pairs={{0,8},{1,9},{2,10},{3,11},{4,12},{5,13},{6,14},{7,15},{8,0},{9,1},... | collective-permute-start | bytes 688136 | tf_op jit(solution)/shard_map/ppermute | solution.py:38
  (60 shorter events, 16.9 us)
Async XLA Ops:
  0.6 7.4 %copy-start = (bf16[8,16,32,128]{3,2,1,0:T(8,128)(2,1)S(1)}, bf16[8,16,32,128]{3,2,1,0:T(8,128)(2,1)}, u32[]{:S(2)}) copy-start(bf16[8,16,32,128]{3,2,1,0:T(8,128)(2,1)} %param.12) | copy-start | bytes 3145732
  2.8 5.3 %copy-start.6 = (f32[2,16,4]{1,2,0:T(4,128)S(1)}, f32[2,16,4]{1,2,0:T(4,128)}, u32[]{:S(2)}) copy-start(f32[2,16,4]{1,2,0:T(4,128)} %param.20) | copy-start | bytes 1540
  2.8 9.4 %collective-permute-start = (bf16[1168,128]{1,0:T(8,128)(2,1)}, bf16[1168,128]{1,0:T(8,128)(2,1)S(1)}, u32[]{:S(2)}, u32[]{:S(2)}) collective-permute-start(bf16[1168,128]{1,0:T(8,128)(2,1)} %get-tuple-element.85), channel_id=1, source_target_pairs={{0,8},{8,0},{16,24},{24,16},{32,40},{40,32},{48,56},{56,48},{64,72... | collective-permute-start | bytes 897032 | tf_op jit(solution)/shard_map/ppermute | solution.py:47
  6.1 8.3 %collective-permute-start.1 = (bf16[1168,128]{1,0:T(8,128)(2,1)}, bf16[1168,128]{1,0:T(8,128)(2,1)S(1)}, u32[]{:S(2)}, u32[]{:S(2)}) collective-permute-start(bf16[1168,128]{1,0:T(8,128)(2,1)} %get-tuple-element.86), channel_id=1, source_target_pairs={{8,16},{16,8},{24,32},{32,24},{40,48},{48,40},{56,64},{64,56},{72,... | collective-permute-start | bytes 897032 | tf_op jit(solution)/shard_map/ppermute | solution.py:46
  19.1 4.1 %collective-permute-start.2 = (bf16[64,896]{1,0:T(8,128)(2,1)S(1)}, bf16[64,896]{1,0:T(8,128)(2,1)S(1)}, u32[]{:S(2)}, u32[]{:S(2)}) collective-permute-start(bf16[64,896]{1,0:T(8,128)(2,1)S(1)} %get-tuple-element.101), channel_id=1, source_target_pairs={{0,8},{8,0},{16,24},{24,16},{32,40},{40,32},{48,56},{56,48},{64,72... | collective-permute-start | bytes 344072 | tf_op jit(solution)/shard_map/ppermute | solution.py:47
  19.3 6.1 %collective-permute-start.3 = (bf16[64,896]{1,0:T(8,128)(2,1)S(1)}, bf16[64,896]{1,0:T(8,128)(2,1)S(1)}, u32[]{:S(2)}, u32[]{:S(2)}) collective-permute-start(bf16[64,896]{1,0:T(8,128)(2,1)S(1)} %get-tuple-element.102), channel_id=1, source_target_pairs={{8,16},{16,8},{24,32},{32,24},{40,48},{48,40},{56,64},{64,56},{72,... | collective-permute-start | bytes 344072 | tf_op jit(solution)/shard_map/ppermute | solution.py:46
  28.8 3.4 %collective-permute-start.4 = (bf16[4,224,128]{2,1,0:T(8,128)(2,1)S(1)}, bf16[4,224,128]{2,1,0:T(8,128)(2,1)S(1)}, u32[]{:S(2)}, u32[]{:S(2)}) collective-permute-start(bf16[4,224,128]{2,1,0:T(8,128)(2,1)S(1)} %get-tuple-element.137), channel_id=1, source_target_pairs={{0,8},{1,9},{2,10},{3,11},{4,12},{5,13},{6,14},{7,15},{8,0},{9,1},... | collective-permute-start | bytes 688136 | tf_op jit(solution)/shard_map/ppermute | solution.py:38
  28.9 6.4 %collective-permute-start.8 = (bf16[4,128,128]{2,1,0:T(8,128)(2,1)S(1)}, bf16[4,128,128]{2,1,0:T(8,128)(2,1)S(1)}, u32[]{:S(2)}, u32[]{:S(2)}) collective-permute-start(bf16[4,128,128]{2,1,0:T(8,128)(2,1)S(1)} %get-tuple-element.143), channel_id=1, source_target_pairs={{0,2},{1,3},{2,4},{3,5},{4,6},{5,7},{6,0},{7,1},{8,10},{9,11},{10,... | collective-permute-start | bytes 393224 | tf_op jit(solution)/shard_map/ppermute | solution.py:38
  29.0 8.2 %collective-permute-start.9 = (bf16[4,128,128]{2,1,0:T(8,128)(2,1)S(1)}, bf16[4,128,128]{2,1,0:T(8,128)(2,1)S(1)}, u32[]{:S(2)}, u32[]{:S(2)}) collective-permute-start(bf16[4,128,128]{2,1,0:T(8,128)(2,1)S(1)} %get-tuple-element.144), channel_id=1, source_target_pairs={{0,4},{1,5},{2,6},{3,7},{4,0},{5,1},{6,2},{7,3},{8,12},{9,13},{10,... | collective-permute-start | bytes 393224 | tf_op jit(solution)/shard_map/ppermute | solution.py:38
  31.2 7.3 %collective-permute-start.10 = (bf16[4,128,128]{2,1,0:T(8,128)(2,1)S(1)}, bf16[4,128,128]{2,1,0:T(8,128)(2,1)S(1)}, u32[]{:S(2)}, u32[]{:S(2)}) collective-permute-start(bf16[4,128,128]{2,1,0:T(8,128)(2,1)S(1)} %get-tuple-element.145), channel_id=1, source_target_pairs={{0,6},{1,7},{2,0},{3,1},{4,2},{5,3},{6,4},{7,5},{8,14},{9,15},{10,... | collective-permute-start | bytes 393224 | tf_op jit(solution)/shard_map/ppermute | solution.py:38
  32.3 8.3 %collective-permute-start.5 = (bf16[224,128]{1,0:T(8,128)(2,1)S(1)}, bf16[224,128]{1,0:T(8,128)(2,1)S(1)}, u32[]{:S(2)}, u32[]{:S(2)}) collective-permute-start(bf16[224,128]{1,0:T(8,128)(2,1)S(1)} %get-tuple-element.139), channel_id=1, source_target_pairs={{0,2},{1,3},{2,4},{3,5},{4,6},{5,7},{6,0},{7,1},{8,10},{9,11},{10,... | collective-permute-start | bytes 172040 | tf_op jit(solution)/shard_map/ppermute | solution.py:38
  32.8 7.9 %collective-permute-start.6 = (bf16[224,128]{1,0:T(8,128)(2,1)S(1)}, bf16[224,128]{1,0:T(8,128)(2,1)S(1)}, u32[]{:S(2)}, u32[]{:S(2)}) collective-permute-start(bf16[224,128]{1,0:T(8,128)(2,1)S(1)} %get-tuple-element.140), channel_id=1, source_target_pairs={{0,4},{1,5},{2,6},{3,7},{4,0},{5,1},{6,2},{7,3},{8,12},{9,13},{10,... | collective-permute-start | bytes 172040 | tf_op jit(solution)/shard_map/ppermute | solution.py:38
  35.3 5.3 %collective-permute-start.7 = (bf16[224,128]{1,0:T(8,128)(2,1)S(1)}, bf16[224,128]{1,0:T(8,128)(2,1)S(1)}, u32[]{:S(2)}, u32[]{:S(2)}) collective-permute-start(bf16[224,128]{1,0:T(8,128)(2,1)S(1)} %get-tuple-element.141), channel_id=1, source_target_pairs={{0,6},{1,7},{2,0},{3,1},{4,2},{5,3},{6,4},{7,5},{8,14},{9,15},{10,... | collective-permute-start | bytes 172040 | tf_op jit(solution)/shard_map/ppermute | solution.py:38
  40.8 7.9 %collective-permute-start.11 = (bf16[480,128]{1,0:T(8,128)(2,1)S(1)}, bf16[480,128]{1,0:T(8,128)(2,1)S(1)}, u32[]{:S(2)}, u32[]{:S(2)}) collective-permute-start(bf16[480,128]{1,0:T(8,128)(2,1)S(1)} %get-tuple-element.146), channel_id=1, source_target_pairs={{0,1},{1,0},{2,3},{3,2},{4,5},{5,4},{6,7},{7,6},{8,9},{9,8},{10,11... | collective-permute-start | bytes 368648 | tf_op jit(solution)/shard_map/ppermute | solution.py:38
  48.7 10.6 %collective-permute-start.14 = (bf16[224,128]{1,0:T(8,128)(2,1)S(1)}, bf16[224,128]{1,0:T(8,128)(2,1)S(1)}, u32[]{:S(2)}, u32[]{:S(2)}) collective-permute-start(bf16[224,128]{1,0:T(8,128)(2,1)S(1)} %add_convert_fusion.2), channel_id=1, source_target_pairs={{0,192},{1,193},{2,194},{3,195},{4,196},{5,197},{6,198},{7,199},{8... | collective-permute-start | bytes 172040 | tf_op jit(solution)/shard_map/ppermute | solution.py:38
  56.8 4.9 %collective-permute-start.13 = (bf16[224,128]{1,0:T(8,128)(2,1)S(1)}, bf16[224,128]{1,0:T(8,128)(2,1)S(1)}, u32[]{:S(2)}, u32[]{:S(2)}) collective-permute-start(bf16[224,128]{1,0:T(8,128)(2,1)S(1)} %add_convert_fusion.2), channel_id=1, source_target_pairs={{0,64},{1,65},{2,66},{3,67},{4,68},{5,69},{6,70},{7,71},{8,72},{9,... | collective-permute-start | bytes 172040 | tf_op jit(solution)/shard_map/ppermute | solution.py:38
  56.8 4.9 %collective-permute-start.12 = (bf16[224,128]{1,0:T(8,128)(2,1)S(1)}, bf16[224,128]{1,0:T(8,128)(2,1)S(1)}, u32[]{:S(2)}, u32[]{:S(2)}) collective-permute-start(bf16[224,128]{1,0:T(8,128)(2,1)S(1)} %add_convert_fusion.2), channel_id=1, source_target_pairs={{0,128},{1,129},{2,130},{3,131},{4,132},{5,133},{6,134},{7,135},{8... | collective-permute-start | bytes 172040 | tf_op jit(solution)/shard_map/ppermute | solution.py:38
  61.7 6.2 %collective-permute-start.17 = (bf16[224,128]{1,0:T(8,128)(2,1)S(1)}, bf16[224,128]{1,0:T(8,128)(2,1)S(1)}, u32[]{:S(2)}, u32[]{:S(2)}) collective-permute-start(bf16[224,128]{1,0:T(8,128)(2,1)S(1)} %add_convert_fusion.1), channel_id=1, source_target_pairs={{0,48},{1,49},{2,50},{3,51},{4,52},{5,53},{6,54},{7,55},{8,56},{9,... | collective-permute-start | bytes 172040 | tf_op jit(solution)/shard_map/ppermute | solution.py:38
  66.6 4.6 %collective-permute-start.16 = (bf16[224,128]{1,0:T(8,128)(2,1)S(1)}, bf16[224,128]{1,0:T(8,128)(2,1)S(1)}, u32[]{:S(2)}, u32[]{:S(2)}) collective-permute-start(bf16[224,128]{1,0:T(8,128)(2,1)S(1)} %add_convert_fusion.1), channel_id=1, source_target_pairs={{0,16},{1,17},{2,18},{3,19},{4,20},{5,21},{6,22},{7,23},{8,24},{9,... | collective-permute-start | bytes 172040 | tf_op jit(solution)/shard_map/ppermute | solution.py:38
  66.6 5.1 %collective-permute-start.15 = (bf16[224,128]{1,0:T(8,128)(2,1)S(1)}, bf16[224,128]{1,0:T(8,128)(2,1)S(1)}, u32[]{:S(2)}, u32[]{:S(2)}) collective-permute-start(bf16[224,128]{1,0:T(8,128)(2,1)S(1)} %add_convert_fusion.1), channel_id=1, source_target_pairs={{0,32},{1,33},{2,34},{3,35},{4,36},{5,37},{6,38},{7,39},{8,40},{9,... | collective-permute-start | bytes 172040 | tf_op jit(solution)/shard_map/ppermute | solution.py:38
  71.7 3.1 %collective-permute-start.20 = (bf16[224,128]{1,0:T(8,128)(2,1)S(1)}, bf16[224,128]{1,0:T(8,128)(2,1)S(1)}, u32[]{:S(2)}, u32[]{:S(2)}) collective-permute-start(bf16[224,128]{1,0:T(8,128)(2,1)S(1)} %add_convert_fusion.own), channel_id=1, source_target_pairs={{0,6},{1,7},{2,0},{3,1},{4,2},{5,3},{6,4},{7,5},{8,14},{9,15},{10,... | collective-permute-start | bytes 172040 | tf_op jit(solution)/shard_map/ppermute | solution.py:38
  72.2 4.5 %collective-permute-start.19 = (bf16[224,128]{1,0:T(8,128)(2,1)S(1)}, bf16[224,128]{1,0:T(8,128)(2,1)S(1)}, u32[]{:S(2)}, u32[]{:S(2)}) collective-permute-start(bf16[224,128]{1,0:T(8,128)(2,1)S(1)} %add_convert_fusion.own), channel_id=1, source_target_pairs={{0,4},{1,5},{2,6},{3,7},{4,0},{5,1},{6,2},{7,3},{8,12},{9,13},{10,... | collective-permute-start | bytes 172040 | tf_op jit(solution)/shard_map/ppermute | solution.py:38
  72.6 4.7 %collective-permute-start.18 = (bf16[224,128]{1,0:T(8,128)(2,1)S(1)}, bf16[224,128]{1,0:T(8,128)(2,1)S(1)}, u32[]{:S(2)}, u32[]{:S(2)}) collective-permute-start(bf16[224,128]{1,0:T(8,128)(2,1)S(1)} %add_convert_fusion.own), channel_id=1, source_target_pairs={{0,2},{1,3},{2,4},{3,5},{4,6},{5,7},{6,0},{7,1},{8,10},{9,11},{10,... | collective-permute-start | bytes 172040 | tf_op jit(solution)/shard_map/ppermute | solution.py:38
  77.4 6.5 %collective-permute-start.21 = (bf16[4,224,128]{2,1,0:T(8,128)(2,1)S(1)}, bf16[4,224,128]{2,1,0:T(8,128)(2,1)S(1)}, u32[]{:S(2)}, u32[]{:S(2)}) collective-permute-start(bf16[4,224,128]{2,1,0:T(8,128)(2,1)S(1)} %shard_map.175.half), channel_id=1, source_target_pairs={{0,8},{1,9},{2,10},{3,11},{4,12},{5,13},{6,14},{7,15},{8,0},{9,1},... | collective-permute-start | bytes 688136 | tf_op jit(solution)/shard_map/ppermute | solution.py:38
  (9 other events, 17.3 us)

commit v6 on v5

--- a/solution.py
+++ b/solution.py
@@ -773,17 +773,16 @@
         message[SPAN + n * 128 : SPAN + (n + 1) * 128, :] = away[n]
 
 
-def quarter_kernel(own, one, two, three, half):
+def finish_kernel(own, one, two, three, grad_gain, inner, out, bias, token, whole):
     y = lax.axis_index("samp") // 2
-    half[y] = own[...]
-    for k, ref in enumerate((one, two, three)):
-        half[lax.rem(y + 3 - k, 4)] = ref[...]
-
-
-def finish_kernel(half, got, grad_gain, inner, out, bias, token):
-    def finish(lower, upper):
+    for k, ref in enumerate((own, one, two, three)):
+        at = lax.rem(y + 4 - k, 4)
+        for core in range(2):
+            whole[core * 4 + at] = ref[core]
+
+    def finish():
         def chunk(m):
-            return (lower if m < 4 else upper).at[m % 4]
+            return whole.at[m]
 
         def rows(row):
             return chunk(row // EARLY)[row % EARLY : row % EARLY + 16, :].astype(F32)
@@ -809,15 +808,7 @@
             choose = jnp.where(head == lane, 1.0, 0.0).astype(BF16)
             bias[layer] = nt(choose, chunk(layer)[EARLY:EXTRA, :])
 
-    odd = odd_core()
-
-    @pl.when(jnp.logical_not(odd))
-    def _():
-        finish(half, got)
-
-    @pl.when(odd)
-    def _():
-        finish(got, half)
+    finish()
 
 
 def expand_kernel(weight, kept, got, pair):
@@ -1079,11 +1070,9 @@
     )
     total, pair_sum = lax.optimization_barrier((total, pair_sum))
     total = everyone(total, 1)
-    (half,) = run(
-        quarter_kernel,
-        [((4, SPAN, 128), BF16)],
-        (total, *[hop(total, 3, k) for k in range(1, 4)]),
-    )
+    other = hop(total, 2, 1)
+    odd = odd_core()
+    both = jnp.stack([jnp.where(odd, other, total), jnp.where(odd, total, other)])
     grad_gain, grad_in, grad_out, grad_bias, grad_token = run(
         finish_kernel,
         [
@@ -1093,7 +1082,8 @@
             ((2, 4, 16), F32),
             ((128, 384), F32),
         ],
-        (half, hop(half, 2, 1)),
+        (both, *[hop(both, 3, k) for k in range(1, 4)]),
+        scratch=[pltpu.VMEM((8, SPAN, 128), BF16)],
     )
     return (
         grad_atoms[None],

time: 85.2 us -> 86 us (level)
  starting transfers between devices: 41.7 us -> 43.3 us
    ppermute x18, starting transfers between devices: 34.4 us -> 35.9 us  [hop(): return lax.ppermute(value, WORLD, moves(part, step))]
    pallas_call x15 -> x14, Pallas kernels: 18.3 us -> 18.2 us  [run(): pl.pallas_call(body, out_shape=[jax.ShapeDtypeStruct(s, d) for s, d in ou...]
  transfers between devices with their start and end apart: 22 -> 22, of which waited for: 14 -> 12; matrix products, arithmetic and copies ran while one was open for 0% -> 0% of each run, Pallas kernels for 8% -> 8%
where the time goes in v6:
time: 86 us; the launch traced here: 85.8 us
  starting transfers between devices  43.3 us (50%)
  waiting for transfers between devices  22.6 us (26%)
  Pallas kernels  18.2 us (21%)
  between operations  0.92 us (1%)
    ppermute x18, starting transfers between devices, hop(): return lax.ppermute(value, WORLD, moves(part, step))  35.9 us
    ppermute x18, waiting for transfers between devices, hop(): return lax.ppermute(value, WORLD, moves(part, step))  18.2 us
    pallas_call x14, Pallas kernels, run(): pl.pallas_call(body, out_shape=[jax.ShapeDtypeStruct(s, d) for s, d in ou...  18.2 us
    ppermute x2, waiting for transfers between devices, swapped(): far = lax.ppermute(far, 'seq', across)  4.35 us
    ppermute x2, starting transfers between devices, swapped(): far = lax.ppermute(far, 'seq', across)  3.94 us
    ppermute x2, starting transfers between devices, swapped(): return (lax.ppermute(near, 'seq', chip), far)  3.42 us
  transfers between devices with their start and end apart: 22, of which 12 were waited for; matrix products, arithmetic and copies ran while one was open for 0% of the time, Pallas kernels for 8%

profile of v6, /device:TPU:1, one launch (start us, length us, event | category | flops | bytes accessed | tf_op | source)
XLA Modules:
  0.0 85.8 jit_solution(11824981773246969794)
XLA Ops:
  0.6 2.1 %shard_map.162 = (bf16[1168,128]{1,0:T(8,128)(2,1)}, bf16[1168,128]{1,0:T(8,128)(2,1)}, s32[1,128]{1,0:T(1,128)}) custom-call(s32[8]{0:T(128)} %shift_far.1, bf16[8,512,128]{2,1,0:T(8,128)(2,1)} %bitcast.13, bf16[256,128]{1,0:T(8,128)(2,1)} %bitcast.17, bf16[32,384]{1,0:T(8,128)(2,1)} %bitcast.21, s32[1,32]{1,0:T(1,128)} %bitcast.26), custom_call_target="tpu_custom_call" | custom-call | flops 100000000 | bytes 1000000 | tf_op jit(solution)/shard_map/pallas_call | solution.py:68
  2.8 3.3 %collective-permute-start = (bf16[1168,128]{1,0:T(8,128)(2,1)}, bf16[1168,128]{1,0:T(8,128)(2,1)S(1)}, u32[]{:S(2)}, u32[]{:S(2)}) collective-permute-start(bf16[1168,128]{1,0:T(8,128)(2,1)} %get-tuple-element.85), channel_id=1, source_target_pairs={{0,8},{8,0},{16,24},{24,16},{32,40},{40,32},{48,56},{56,48},{64,72... | collective-permute-start | bytes 897032 | tf_op jit(solution)/shard_map/ppermute | solution.py:47
  6.1 1.9 %collective-permute-start.1 = (bf16[1168,128]{1,0:T(8,128)(2,1)}, bf16[1168,128]{1,0:T(8,128)(2,1)S(1)}, u32[]{:S(2)}, u32[]{:S(2)}) collective-permute-start(bf16[1168,128]{1,0:T(8,128)(2,1)} %get-tuple-element.86), channel_id=1, source_target_pairs={{8,16},{16,8},{24,32},{32,24},{40,48},{48,40},{56,64},{64,56},{72,... | collective-permute-start | bytes 897032 | tf_op jit(solution)/shard_map/ppermute | solution.py:46
  8.1 1.9 %shard_map.164 = (f32[8,128,128]{2,1,0:T(8,128)S(1)}, f32[8,128,128]{2,1,0:T(8,128)S(1)}) custom-call(f32[2,4,16]{2,1,0:T(4,128)S(1)} %bitcast.23, bf16[8,512,128]{2,1,0:T(8,128)(2,1)S(1)} %bitcast.14), custom_call_target="tpu_custom_call" | custom-call | flops 100000000 | bytes 1000000 | tf_op jit(solution)/shard_map/pallas_call | solution.py:68
  12.2 2.2 %collective-permute-done.1.far.far_first = bf16[1168,128]{1,0:T(8,128)(2,1)S(1)} collective-permute-done((bf16[1168,128]{1,0:T(8,128)(2,1)}, bf16[1168,128]{1,0:T(8,128)(2,1)S(1)}, u32[]{:S(2)}, u32[]{:S(2)}) %collective-permute-start.1) | collective-permute-done | bytes 299040 | tf_op jit(solution)/shard_map/ppermute | solution.py:46
  14.4 2.3 %shard_map.166 = (f32[384,128]{1,0:T(8,128)S(1)}, f32[8,128,128]{2,1,0:T(8,128)S(1)}, bf16[384,128]{1,0:T(8,128)(2,1)S(1)}, bf16[512,256]{1,0:T(8,128)(2,1)S(1)}...) custom-call(s32[1,128]{1,0:T(1,128)S(1)} %get-tuple-element.82.shift, ...), custom_call_target="tpu_custom_call" | custom-call | flops 100000000 | bytes 1000000 | tf_op jit(solution)/shard_map/pallas_call | solution.py:68
  16.8 2.4 %shard_map.167 = (bf16[256,128]{1,0:T(8,128)(2,1)S(1)}, bf16[256,128]{1,0:T(8,128)(2,1)S(1)}, bf16[256,128]{1,0:T(8,128)(2,1)S(1)}, bf16[256,384]{1,0:T(8,128)(2...) custom-call(s32[1,128]{1,0:T(1,128)S(1)} %get-tuple-element.90.shift, ...), custom_call_target="tpu_custom_call" | custom-call | flops 100000000 | bytes 1000000 | tf_op jit(solution)/shard_map/pallas_call | solution.py:68
  19.2 2.0 %collective-permute-start.3 = (bf16[64,896]{1,0:T(8,128)(2,1)S(1)}, bf16[64,896]{1,0:T(8,128)(2,1)S(1)}, u32[]{:S(2)}, u32[]{:S(2)}) collective-permute-start(bf16[64,896]{1,0:T(8,128)(2,1)S(1)} %get-tuple-element.102), channel_id=1, source_target_pairs={{8,16},{16,8},{24,32},{32,24},{40,48},{48,40},{56,64},{64,56},{72,... | collective-permute-start | bytes 344072 | tf_op jit(solution)/shard_map/ppermute | solution.py:46
  23.2 2.1 %collective-permute-done.3.far = bf16[64,896]{1,0:T(8,128)(2,1)S(1)} collective-permute-done((bf16[64,896]{1,0:T(8,128)(2,1)S(1)}, bf16[64,896]{1,0:T(8,128)(2,1)S(1)}, u32[]{:S(2)}, u32[]{:S(2)}) %collective-permute-start.3) | collective-permute-done | bytes 114720 | tf_op jit(solution)/shard_map/ppermute | solution.py:46
  25.4 2.8 %shard_map.170 = (bf16[256,512]{1,0:T(8,128)(2,1)S(1)}, bf16[256,512]{1,0:T(8,128)(2,1)S(1)}, f32[2,128]{1,0:T(2,128)S(1)}, bf16[256,128]{1,0:T(8,128)(2,1)S(1)}...) custom-call(s32[1,128]{1,0:T(1,128)S(1)} %get-tuple-element.90.shift, ...), custom_call_target="tpu_custom_call" | custom-call | flops 100000000 | bytes 1000000 | tf_op jit(solution)/shard_map/pallas_call | solution.py:68
  31.7 1.7 %collective-permute-start.5 = (bf16[224,128]{1,0:T(8,128)(2,1)S(1)}, bf16[224,128]{1,0:T(8,128)(2,1)S(1)}, u32[]{:S(2)}, u32[]{:S(2)}) collective-permute-start(bf16[224,128]{1,0:T(8,128)(2,1)S(1)} %get-tuple-element.139), channel_id=1, source_target_pairs={{0,2},{1,3},{2,4},{3,5},{4,6},{5,7},{6,0},{7,1},{8,10},{9,11},{10,... | collective-permute-start | bytes 172040 | tf_op jit(solution)/shard_map/ppermute | solution.py:38
  34.2 1.7 %collective-permute-start.7 = (bf16[224,128]{1,0:T(8,128)(2,1)S(1)}, bf16[224,128]{1,0:T(8,128)(2,1)S(1)}, u32[]{:S(2)}, u32[]{:S(2)}) collective-permute-start(bf16[224,128]{1,0:T(8,128)(2,1)S(1)} %get-tuple-element.141), channel_id=1, source_target_pairs={{0,6},{1,7},{2,0},{3,1},{4,2},{5,3},{6,4},{7,5},{8,14},{9,15},{10,... | collective-permute-start | bytes 172040 | tf_op jit(solution)/shard_map/ppermute | solution.py:38
  35.9 1.7 %collective-permute-done.8.score_one = bf16[4,128,128]{2,1,0:T(8,128)(2,1)S(1)} collective-permute-done((bf16[4,128,128]{2,1,0:T(8,128)(2,1)S(1)}, bf16[4,128,128]{2,1,0:T(8,128)(2,1)S(1)}, u32[]{:S(2)}, u32[]{:S(2)}) %collective-permute-start.8) | collective-permute-done | bytes 131104 | tf_op jit(solution)/shard_map/ppermute | solution.py:38
  37.6 3.5 %collective-permute-done.5.one = bf16[224,128]{1,0:T(8,128)(2,1)S(1)} collective-permute-done((bf16[224,128]{1,0:T(8,128)(2,1)S(1)}, bf16[224,128]{1,0:T(8,128)(2,1)S(1)}, u32[]{:S(2)}, u32[]{:S(2)}) %collective-permute-start.5) | collective-permute-done | bytes 57376 | tf_op jit(solution)/shard_map/ppermute | solution.py:38
  41.1 7.1 %collective-permute-start.11 = (bf16[480,128]{1,0:T(8,128)(2,1)S(1)}, bf16[480,128]{1,0:T(8,128)(2,1)S(1)}, u32[]{:S(2)}, u32[]{:S(2)}) collective-permute-start(bf16[480,128]{1,0:T(8,128)(2,1)S(1)} %get-tuple-element.146), channel_id=1, source_target_pairs={{0,1},{1,0},{2,3},{3,2},{4,5},{5,4},{6,7},{7,6},{8,9},{9,8},{10,11... | collective-permute-start | bytes 368648 | tf_op jit(solution)/shard_map/ppermute | solution.py:38
  48.2 2.3 %collective-permute-done.11.got = bf16[480,128]{1,0:T(8,128)(2,1)S(1)} collective-permute-done((bf16[480,128]{1,0:T(8,128)(2,1)S(1)}, bf16[480,128]{1,0:T(8,128)(2,1)S(1)}, u32[]{:S(2)}, u32[]{:S(2)}) %collective-permute-start.11) | collective-permute-done | bytes 122912 | tf_op jit(solution)/shard_map/ppermute | solution.py:38
  50.5 5.8 %collective-permute-start.12 = (bf16[224,128]{1,0:T(8,128)(2,1)S(1)}, bf16[224,128]{1,0:T(8,128)(2,1)S(1)}, u32[]{:S(2)}, u32[]{:S(2)}) collective-permute-start(bf16[224,128]{1,0:T(8,128)(2,1)S(1)} %add_convert_fusion.2), channel_id=1, source_target_pairs={{0,128},{1,129},{2,130},{3,131},{4,132},{5,133},{6,134},{7,135},{8... | collective-permute-start | bytes 172040 | tf_op jit(solution)/shard_map/ppermute | solution.py:38
  56.3 1.7 %collective-permute-start.13 = (bf16[224,128]{1,0:T(8,128)(2,1)S(1)}, bf16[224,128]{1,0:T(8,128)(2,1)S(1)}, u32[]{:S(2)}, u32[]{:S(2)}) collective-permute-start(bf16[224,128]{1,0:T(8,128)(2,1)S(1)} %add_convert_fusion.2), channel_id=1, source_target_pairs={{0,64},{1,65},{2,66},{3,67},{4,68},{5,69},{6,70},{7,71},{8,72},{9,... | collective-permute-start | bytes 172040 | tf_op jit(solution)/shard_map/ppermute | solution.py:38
  62.3 3.1 %collective-permute-start.15 = (bf16[224,128]{1,0:T(8,128)(2,1)S(1)}, bf16[224,128]{1,0:T(8,128)(2,1)S(1)}, u32[]{:S(2)}, u32[]{:S(2)}) collective-permute-start(bf16[224,128]{1,0:T(8,128)(2,1)S(1)} %add_convert_fusion.1), channel_id=1, source_target_pairs={{0,32},{1,33},{2,34},{3,35},{4,36},{5,37},{6,38},{7,39},{8,40},{9,... | collective-permute-start | bytes 172040 | tf_op jit(solution)/shard_map/ppermute | solution.py:38
  65.4 2.4 %collective-permute-start.16 = (bf16[224,128]{1,0:T(8,128)(2,1)S(1)}, bf16[224,128]{1,0:T(8,128)(2,1)S(1)}, u32[]{:S(2)}, u32[]{:S(2)}) collective-permute-start(bf16[224,128]{1,0:T(8,128)(2,1)S(1)} %add_convert_fusion.1), channel_id=1, source_target_pairs={{0,16},{1,17},{2,18},{3,19},{4,20},{5,21},{6,22},{7,23},{8,24},{9,... | collective-permute-start | bytes 172040 | tf_op jit(solution)/shard_map/ppermute | solution.py:38
  68.0 1.6 %collective-permute-done.16 = bf16[224,128]{1,0:T(8,128)(2,1)S(1)} collective-permute-done((bf16[224,128]{1,0:T(8,128)(2,1)S(1)}, bf16[224,128]{1,0:T(8,128)(2,1)S(1)}, u32[]{:S(2)}, u32[]{:S(2)}) %collective-permute-start.16) | collective-permute-done | bytes 57376 | tf_op jit(solution)/shard_map/ppermute | solution.py:38
  71.1 4.3 %collective-permute-start.18 = (bf16[224,128]{1,0:T(8,128)(2,1)S(1)}, bf16[224,128]{1,0:T(8,128)(2,1)S(1)}, u32[]{:S(2)}, u32[]{:S(2)}) collective-permute-start(bf16[224,128]{1,0:T(8,128)(2,1)S(1)} %add_convert_fusion), channel_id=1, source_target_pairs={{0,8},{1,9},{2,10},{3,11},{4,12},{5,13},{6,14},{7,15},{8,0},{9,1},... | collective-permute-start | bytes 172040 | tf_op jit(solution)/shard_map/ppermute | solution.py:38
  77.5 1.6 %collective-permute-start.21 = (bf16[2,224,128]{2,1,0:T(8,128)(2,1)S(1)}, bf16[2,224,128]{2,1,0:T(8,128)(2,1)S(1)}, u32[]{:S(2)}, u32[]{:S(2)}) collective-permute-start(bf16[2,224,128]{2,1,0:T(8,128)(2,1)S(1)} %pad_maximum_fusion.own), channel_id=1, source_target_pairs={{0,6},{1,7},{2,0},{3,1},{4,2},{5,3},{6,4},{7,5},{8,14},{9,15},{10,... | collective-permute-start | bytes 344072 | tf_op jit(solution)/shard_map/ppermute | solution.py:38
  79.0 5.6 %collective-permute-done.19.one = bf16[2,224,128]{2,1,0:T(8,128)(2,1)S(1)} collective-permute-done((bf16[2,224,128]{2,1,0:T(8,128)(2,1)S(1)}, bf16[2,224,128]{2,1,0:T(8,128)(2,1)S(1)}, u32[]{:S(2)}, u32[]{:S(2)}) %collective-permute-start.19) | collective-permute-done | bytes 114720 | tf_op jit(solution)/shard_map/ppermute | solution.py:38
  (61 shorter events, 17.9 us)
Async XLA Ops:
  0.6 7.4 %copy-start = (bf16[8,16,32,128]{3,2,1,0:T(8,128)(2,1)S(1)}, bf16[8,16,32,128]{3,2,1,0:T(8,128)(2,1)}, u32[]{:S(2)}) copy-start(bf16[8,16,32,128]{3,2,1,0:T(8,128)(2,1)} %param.12) | copy-start | bytes 3145732
  2.8 5.3 %copy-start.6 = (f32[2,16,4]{1,2,0:T(4,128)S(1)}, f32[2,16,4]{1,2,0:T(4,128)}, u32[]{:S(2)}) copy-start(f32[2,16,4]{1,2,0:T(4,128)} %param.20) | copy-start | bytes 1540
  2.8 9.4 %collective-permute-start = (bf16[1168,128]{1,0:T(8,128)(2,1)}, bf16[1168,128]{1,0:T(8,128)(2,1)S(1)}, u32[]{:S(2)}, u32[]{:S(2)}) collective-permute-start(bf16[1168,128]{1,0:T(8,128)(2,1)} %get-tuple-element.85), channel_id=1, source_target_pairs={{0,8},{8,0},{16,24},{24,16},{32,40},{40,32},{48,56},{56,48},{64,72... | collective-permute-start | bytes 897032 | tf_op jit(solution)/shard_map/ppermute | solution.py:47
  6.1 8.3 %collective-permute-start.1 = (bf16[1168,128]{1,0:T(8,128)(2,1)}, bf16[1168,128]{1,0:T(8,128)(2,1)S(1)}, u32[]{:S(2)}, u32[]{:S(2)}) collective-permute-start(bf16[1168,128]{1,0:T(8,128)(2,1)} %get-tuple-element.86), channel_id=1, source_target_pairs={{8,16},{16,8},{24,32},{32,24},{40,48},{48,40},{56,64},{64,56},{72,... | collective-permute-start | bytes 897032 | tf_op jit(solution)/shard_map/ppermute | solution.py:46
  19.1 4.1 %collective-permute-start.2 = (bf16[64,896]{1,0:T(8,128)(2,1)S(1)}, bf16[64,896]{1,0:T(8,128)(2,1)S(1)}, u32[]{:S(2)}, u32[]{:S(2)}) collective-permute-start(bf16[64,896]{1,0:T(8,128)(2,1)S(1)} %get-tuple-element.101), channel_id=1, source_target_pairs={{0,8},{8,0},{16,24},{24,16},{32,40},{40,32},{48,56},{56,48},{64,72... | collective-permute-start | bytes 344072 | tf_op jit(solution)/shard_map/ppermute | solution.py:47
  19.2 6.1 %collective-permute-start.3 = (bf16[64,896]{1,0:T(8,128)(2,1)S(1)}, bf16[64,896]{1,0:T(8,128)(2,1)S(1)}, u32[]{:S(2)}, u32[]{:S(2)}) collective-permute-start(bf16[64,896]{1,0:T(8,128)(2,1)S(1)} %get-tuple-element.102), channel_id=1, source_target_pairs={{8,16},{16,8},{24,32},{32,24},{40,48},{48,40},{56,64},{64,56},{72,... | collective-permute-start | bytes 344072 | tf_op jit(solution)/shard_map/ppermute | solution.py:46
  28.8 2.8 %collective-permute-start.4 = (bf16[4,224,128]{2,1,0:T(8,128)(2,1)S(1)}, bf16[4,224,128]{2,1,0:T(8,128)(2,1)S(1)}, u32[]{:S(2)}, u32[]{:S(2)}) collective-permute-start(bf16[4,224,128]{2,1,0:T(8,128)(2,1)S(1)} %get-tuple-element.137), channel_id=1, source_target_pairs={{0,8},{1,9},{2,10},{3,11},{4,12},{5,13},{6,14},{7,15},{8,0},{9,1},... | collective-permute-start | bytes 688136 | tf_op jit(solution)/shard_map/ppermute | solution.py:38
  28.9 5.3 %collective-permute-start.10 = (bf16[4,128,128]{2,1,0:T(8,128)(2,1)S(1)}, bf16[4,128,128]{2,1,0:T(8,128)(2,1)S(1)}, u32[]{:S(2)}, u32[]{:S(2)}) collective-permute-start(bf16[4,128,128]{2,1,0:T(8,128)(2,1)S(1)} %get-tuple-element.145), channel_id=1, source_target_pairs={{0,6},{1,7},{2,0},{3,1},{4,2},{5,3},{6,4},{7,5},{8,14},{9,15},{10,... | collective-permute-start | bytes 393224 | tf_op jit(solution)/shard_map/ppermute | solution.py:38
  30.0 7.6 %collective-permute-start.8 = (bf16[4,128,128]{2,1,0:T(8,128)(2,1)S(1)}, bf16[4,128,128]{2,1,0:T(8,128)(2,1)S(1)}, u32[]{:S(2)}, u32[]{:S(2)}) collective-permute-start(bf16[4,128,128]{2,1,0:T(8,128)(2,1)S(1)} %get-tuple-element.143), channel_id=1, source_target_pairs={{0,2},{1,3},{2,4},{3,5},{4,6},{5,7},{6,0},{7,1},{8,10},{9,11},{10,... | collective-permute-start | bytes 393224 | tf_op jit(solution)/shard_map/ppermute | solution.py:38
  30.5 7.1 %collective-permute-start.9 = (bf16[4,128,128]{2,1,0:T(8,128)(2,1)S(1)}, bf16[4,128,128]{2,1,0:T(8,128)(2,1)S(1)}, u32[]{:S(2)}, u32[]{:S(2)}) collective-permute-start(bf16[4,128,128]{2,1,0:T(8,128)(2,1)S(1)} %get-tuple-element.144), channel_id=1, source_target_pairs={{0,4},{1,5},{2,6},{3,7},{4,0},{5,1},{6,2},{7,3},{8,12},{9,13},{10,... | collective-permute-start | bytes 393224 | tf_op jit(solution)/shard_map/ppermute | solution.py:38
  31.7 9.3 %collective-permute-start.5 = (bf16[224,128]{1,0:T(8,128)(2,1)S(1)}, bf16[224,128]{1,0:T(8,128)(2,1)S(1)}, u32[]{:S(2)}, u32[]{:S(2)}) collective-permute-start(bf16[224,128]{1,0:T(8,128)(2,1)S(1)} %get-tuple-element.139), channel_id=1, source_target_pairs={{0,2},{1,3},{2,4},{3,5},{4,6},{5,7},{6,0},{7,1},{8,10},{9,11},{10,... | collective-permute-start | bytes 172040 | tf_op jit(solution)/shard_map/ppermute | solution.py:38
  33.4 7.6 %collective-permute-start.6 = (bf16[224,128]{1,0:T(8,128)(2,1)S(1)}, bf16[224,128]{1,0:T(8,128)(2,1)S(1)}, u32[]{:S(2)}, u32[]{:S(2)}) collective-permute-start(bf16[224,128]{1,0:T(8,128)(2,1)S(1)} %get-tuple-element.140), channel_id=1, source_target_pairs={{0,4},{1,5},{2,6},{3,7},{4,0},{5,1},{6,2},{7,3},{8,12},{9,13},{10,... | collective-permute-start | bytes 172040 | tf_op jit(solution)/shard_map/ppermute | solution.py:38
  34.2 6.8 %collective-permute-start.7 = (bf16[224,128]{1,0:T(8,128)(2,1)S(1)}, bf16[224,128]{1,0:T(8,128)(2,1)S(1)}, u32[]{:S(2)}, u32[]{:S(2)}) collective-permute-start(bf16[224,128]{1,0:T(8,128)(2,1)S(1)} %get-tuple-element.141), channel_id=1, source_target_pairs={{0,6},{1,7},{2,0},{3,1},{4,2},{5,3},{6,4},{7,5},{8,14},{9,15},{10,... | collective-permute-start | bytes 172040 | tf_op jit(solution)/shard_map/ppermute | solution.py:38
  41.1 9.3 %collective-permute-start.11 = (bf16[480,128]{1,0:T(8,128)(2,1)S(1)}, bf16[480,128]{1,0:T(8,128)(2,1)S(1)}, u32[]{:S(2)}, u32[]{:S(2)}) collective-permute-start(bf16[480,128]{1,0:T(8,128)(2,1)S(1)} %get-tuple-element.146), channel_id=1, source_target_pairs={{0,1},{1,0},{2,3},{3,2},{4,5},{5,4},{6,7},{7,6},{8,9},{9,8},{10,11... | collective-permute-start | bytes 368648 | tf_op jit(solution)/shard_map/ppermute | solution.py:38
  50.5 11.3 %collective-permute-start.12 = (bf16[224,128]{1,0:T(8,128)(2,1)S(1)}, bf16[224,128]{1,0:T(8,128)(2,1)S(1)}, u32[]{:S(2)}, u32[]{:S(2)}) collective-permute-start(bf16[224,128]{1,0:T(8,128)(2,1)S(1)} %add_convert_fusion.2), channel_id=1, source_target_pairs={{0,128},{1,129},{2,130},{3,131},{4,132},{5,133},{6,134},{7,135},{8... | collective-permute-start | bytes 172040 | tf_op jit(solution)/shard_map/ppermute | solution.py:38
  56.3 5.5 %collective-permute-start.13 = (bf16[224,128]{1,0:T(8,128)(2,1)S(1)}, bf16[224,128]{1,0:T(8,128)(2,1)S(1)}, u32[]{:S(2)}, u32[]{:S(2)}) collective-permute-start(bf16[224,128]{1,0:T(8,128)(2,1)S(1)} %add_convert_fusion.2), channel_id=1, source_target_pairs={{0,64},{1,65},{2,66},{3,67},{4,68},{5,69},{6,70},{7,71},{8,72},{9,... | collective-permute-start | bytes 172040 | tf_op jit(solution)/shard_map/ppermute | solution.py:38
  58.1 4.2 %collective-permute-start.14 = (bf16[224,128]{1,0:T(8,128)(2,1)S(1)}, bf16[224,128]{1,0:T(8,128)(2,1)S(1)}, u32[]{:S(2)}, u32[]{:S(2)}) collective-permute-start(bf16[224,128]{1,0:T(8,128)(2,1)S(1)} %add_convert_fusion.2), channel_id=1, source_target_pairs={{0,192},{1,193},{2,194},{3,195},{4,196},{5,197},{6,198},{7,199},{8... | collective-permute-start | bytes 172040 | tf_op jit(solution)/shard_map/ppermute | solution.py:38
  62.3 5.8 %collective-permute-start.15 = (bf16[224,128]{1,0:T(8,128)(2,1)S(1)}, bf16[224,128]{1,0:T(8,128)(2,1)S(1)}, u32[]{:S(2)}, u32[]{:S(2)}) collective-permute-start(bf16[224,128]{1,0:T(8,128)(2,1)S(1)} %add_convert_fusion.1), channel_id=1, source_target_pairs={{0,32},{1,33},{2,34},{3,35},{4,36},{5,37},{6,38},{7,39},{8,40},{9,... | collective-permute-start | bytes 172040 | tf_op jit(solution)/shard_map/ppermute | solution.py:38
  65.4 4.2 %collective-permute-start.16 = (bf16[224,128]{1,0:T(8,128)(2,1)S(1)}, bf16[224,128]{1,0:T(8,128)(2,1)S(1)}, u32[]{:S(2)}, u32[]{:S(2)}) collective-permute-start(bf16[224,128]{1,0:T(8,128)(2,1)S(1)} %add_convert_fusion.1), channel_id=1, source_target_pairs={{0,16},{1,17},{2,18},{3,19},{4,20},{5,21},{6,22},{7,23},{8,24},{9,... | collective-permute-start | bytes 172040 | tf_op jit(solution)/shard_map/ppermute | solution.py:38
  67.7 3.3 %collective-permute-start.17 = (bf16[224,128]{1,0:T(8,128)(2,1)S(1)}, bf16[224,128]{1,0:T(8,128)(2,1)S(1)}, u32[]{:S(2)}, u32[]{:S(2)}) collective-permute-start(bf16[224,128]{1,0:T(8,128)(2,1)S(1)} %add_convert_fusion.1), channel_id=1, source_target_pairs={{0,48},{1,49},{2,50},{3,51},{4,52},{5,53},{6,54},{7,55},{8,56},{9,... | collective-permute-start | bytes 172040 | tf_op jit(solution)/shard_map/ppermute | solution.py:38
  71.1 5.2 %collective-permute-start.18 = (bf16[224,128]{1,0:T(8,128)(2,1)S(1)}, bf16[224,128]{1,0:T(8,128)(2,1)S(1)}, u32[]{:S(2)}, u32[]{:S(2)}) collective-permute-start(bf16[224,128]{1,0:T(8,128)(2,1)S(1)} %add_convert_fusion), channel_id=1, source_target_pairs={{0,8},{1,9},{2,10},{3,11},{4,12},{5,13},{6,14},{7,15},{8,0},{9,1},... | collective-permute-start | bytes 172040 | tf_op jit(solution)/shard_map/ppermute | solution.py:38
  76.3 8.3 %collective-permute-start.19 = (bf16[2,224,128]{2,1,0:T(8,128)(2,1)S(1)}, bf16[2,224,128]{2,1,0:T(8,128)(2,1)S(1)}, u32[]{:S(2)}, u32[]{:S(2)}) collective-permute-start(bf16[2,224,128]{2,1,0:T(8,128)(2,1)S(1)} %pad_maximum_fusion.own), channel_id=1, source_target_pairs={{0,2},{1,3},{2,4},{3,5},{4,6},{5,7},{6,0},{7,1},{8,10},{9,11},{10,... | collective-permute-start | bytes 344072 | tf_op jit(solution)/shard_map/ppermute | solution.py:38
  76.4 8.2 %collective-permute-start.20 = (bf16[2,224,128]{2,1,0:T(8,128)(2,1)S(1)}, bf16[2,224,128]{2,1,0:T(8,128)(2,1)S(1)}, u32[]{:S(2)}, u32[]{:S(2)}) collective-permute-start(bf16[2,224,128]{2,1,0:T(8,128)(2,1)S(1)} %pad_maximum_fusion.own), channel_id=1, source_target_pairs={{0,4},{1,5},{2,6},{3,7},{4,0},{5,1},{6,2},{7,3},{8,12},{9,13},{10,... | collective-permute-start | bytes 344072 | tf_op jit(solution)/shard_map/ppermute | solution.py:38
  77.5 7.3 %collective-permute-start.21 = (bf16[2,224,128]{2,1,0:T(8,128)(2,1)S(1)}, bf16[2,224,128]{2,1,0:T(8,128)(2,1)S(1)}, u32[]{:S(2)}, u32[]{:S(2)}) collective-permute-start(bf16[2,224,128]{2,1,0:T(8,128)(2,1)S(1)} %pad_maximum_fusion.own), channel_id=1, source_target_pairs={{0,6},{1,7},{2,0},{3,1},{4,2},{5,3},{6,4},{7,5},{8,14},{9,15},{10,... | collective-permute-start | bytes 344072 | tf_op jit(solution)/shard_map/ppermute | solution.py:38
  (9 other events, 17.3 us)
